TPU v7x, 768 devices: a whole 4x8x12 slice. The times are simulated.
768 devices in a mesh: gx: 96 (over z, x, core), gy: 8 (over y).
Axes of the slice: x: 4, y: 8, z: 12, core: 2. Of those that a mesh axis runs over, the one named last changes fastest.
Arguments:
- pressure_rhs: float32 [2, 384, 64, 128], P(None, 'gx', 'gy'), may hold values from -6 to 6
- conductivity: float32 [2, 384, 64, 128], P(None, 'gx', 'gy'), may hold values from 0.05 to 0.6
- block_counts: int32 [96, 8, 8], P('gx'), may hold values from 0 to 2, as said below
- donor_base: int32 [96, 8, 8, 256], P('gx', 'gy'), may hold values from 0 to 5333
- donor_frac: float32 [3, 96, 8, 8, 256], P(None, 'gx', 'gy'), may hold values from 0 to 1
- receptor_cells: int32 [96, 8, 8, 256], P('gx', 'gy'), may hold values from 0 to 8191
Outputs:
- pressure: float32 [2, 384, 64, 128], P(None, 'gx', 'gy')
- residual: float32 [2, 384, 64, 128], P(None, 'gx', 'gy')
Inputs may be any that keep to these rules, and one draw needn't show every extreme that they name: `block_counts`: in every draw some receiver gets 2 blocks from every device of its gy group, and some sender sends 2 blocks to some receiver. `donor_base`: each value selects a box of 2 x 2 x 2 cells inside the sender's own block. `receptor_cells`: local flat indices in the receiver's block; a cell may be named by several rows.
All inputs are finite; a program needn't handle non-finite values.
Results may differ from a plain program's by a relative error of at most 0.0003.
Values sent between devices are 32-bit elements; how exact they have to be, the bound alone decides.
No kernel may reach another device: no remote copies, remote signals or barrier semaphores. Data moves between devices by JAX's collectives and lax.ppermute only.
A program may use at most 32 MiB of HBM per device.

v0:
```python
import jax
import jax.numpy as jnp
from jax import lax
from jax.sharding import PartitionSpec as P

BLOCK = 128
CSWEEP = 4


damping = 0.8
penalty_weight = 2.0
coarse_scale = 0.0625
stencil_offsets = [
    (shift_x, shift_y, shift_z)
    for shift_x in (-1, 0, 1)
    for shift_y in (-1, 0, 1)
    for shift_z in (-1, 0, 1)
    if (shift_x, shift_y, shift_z) != (0, 0, 0)
]
stencil_weight_sum = 44.0 / 3.0


def extended(value, sides, width):
    for axis, dim in sides:
        size, length = (lax.axis_size(axis), value.shape[dim])
        up = [(i, (i + 1) % size) for i in range(size - 1)]
        down = [(j, i) for i, j in up]
        last = lax.slice_in_dim(value, length - width, length, axis=dim)
        leading = lax.slice_in_dim(value, 0, width, axis=dim)
        before = lax.ppermute(last, axis, up)
        after = lax.ppermute(leading, axis, down)
        value = jnp.concatenate([before, value, after], axis=dim)
    return value


def depth_shift(field, shift_z):
    if shift_z == 0:
        return field
    zero_plane = jnp.zeros(field.shape[:-1] + (1,), field.dtype)
    if shift_z > 0:
        return jnp.concatenate([field[..., 1:], zero_plane], axis=-1)
    return jnp.concatenate([zero_plane, field[..., :-1]], axis=-1)


def stencil_apply(field_pad, cond_pad):
    size_x = field_pad.shape[-3] - 2
    size_y = field_pad.shape[-2] - 2
    center_field = field_pad[..., 1:-1, 1:-1, :]
    center_cond = cond_pad[..., 1:-1, 1:-1, :]
    field_shifts = {shift_z: depth_shift(field_pad, shift_z) for shift_z in (-1, 0, 1)}
    cond_shifts = {shift_z: depth_shift(cond_pad, shift_z) for shift_z in (-1, 0, 1)}
    result = jnp.zeros_like(center_field)
    for shift_x, shift_y, shift_z in stencil_offsets:
        weight = 0.5 / (shift_x * shift_x + shift_y * shift_y + shift_z * shift_z)
        near_field = field_shifts[shift_z][
            ..., 1 + shift_x : 1 + shift_x + size_x, 1 + shift_y : 1 + shift_y + size_y, :
        ]
        near_cond = cond_shifts[shift_z][
            ..., 1 + shift_x : 1 + shift_x + size_x, 1 + shift_y : 1 + shift_y + size_y, :
        ]
        result = result + weight * (center_cond + near_cond) * (center_field - near_field)
    return result


def interpolate(flat_field, base_rows, frac_rows, size_x, size_y, size_z):
    box_total = (size_x - 1) * (size_y - 1) * (size_z - 1)
    grid_id = base_rows // box_total
    remain = base_rows % box_total
    pos_x = remain // ((size_y - 1) * (size_z - 1))
    pos_y = remain // (size_z - 1) % (size_y - 1)
    pos_z = remain % (size_z - 1)
    corner = (
        grid_id * (size_x * size_y * size_z) + pos_x * (size_y * size_z) + pos_y * size_z + pos_z
    )
    frac_x, frac_y, frac_z = (frac_rows[0], frac_rows[1], frac_rows[2])
    shifted_copies = []
    corner_weights = []
    for step_x in (0, 1):
        for step_y in (0, 1):
            for step_z in (0, 1):
                offset = step_x * (size_y * size_z) + step_y * size_z + step_z
                if offset == 0:
                    shifted_copies.append(flat_field)
                else:
                    shifted_copies.append(
                        jnp.concatenate([flat_field[offset:], jnp.zeros((offset,), jnp.float32)])
                    )
                weight_x = frac_x if step_x else 1.0 - frac_x
                weight_y = frac_y if step_y else 1.0 - frac_y
                weight_z = frac_z if step_z else 1.0 - frac_z
                corner_weights.append(weight_x * weight_y * weight_z)
    corner_table = jnp.stack(shifted_copies)
    picked = jnp.take(corner_table, corner, axis=1)
    return jnp.sum(jnp.stack(corner_weights) * picked, axis=0)


def block_mean(field):
    grid_count, size_x, size_y, size_z = field.shape
    return field.reshape(grid_count, size_x // 4, 4, size_y // 4, 4, size_z // 4, 4).mean(
        axis=(2, 4, 6)
    )


def prolong(coarse):
    grid_count, coarse_x, coarse_y, coarse_z = coarse.shape
    wide = jnp.broadcast_to(
        coarse[:, :, None, :, None, :, None], (grid_count, coarse_x, 4, coarse_y, 4, coarse_z, 4)
    )
    return wide.reshape(grid_count, coarse_x * 4, coarse_y * 4, coarse_z * 4)


def local(pressure_rhs, conductivity, block_counts, donor_base, donor_frac, receptor_cells):
    grid_count, size_x, size_y, size_z = pressure_rhs.shape
    cell_total = grid_count * size_x * size_y * size_z
    own_index = lax.axis_index("gy")
    row_length = receptor_cells.shape[-1]
    slot_index = lax.broadcasted_iota(jnp.int32, (row_length,), 0) // BLOCK
    incoming = lax.dynamic_index_in_dim(block_counts[0], own_index, axis=1, keepdims=False)
    validity = (slot_index[None, :] < incoming[:, None]).astype(jnp.float32)
    targets = receptor_cells[0, 0].reshape(-1)
    valid_flat = validity.reshape(-1)
    receptor_count = jax.ops.segment_sum(valid_flat, targets, num_segments=cell_total).reshape(
        pressure_rhs.shape
    )
    smoothed = (
        damping
        * pressure_rhs
        / (stencil_weight_sum * conductivity + penalty_weight * receptor_count)
    )
    flat_field = smoothed.reshape(-1)
    donor_values = interpolate(
        flat_field, donor_base[0, 0], donor_frac[:, 0, 0], size_x, size_y, size_z
    )
    arrived = lax.all_to_all(donor_values, "gy", split_axis=0, concat_axis=0, tiled=True)
    padded = extended(jnp.stack([smoothed, conductivity]), (("gx", 2), ("gy", 3)), 1)
    applied = stencil_apply(padded[0], padded[1])
    arrived_sum = jax.ops.segment_sum(
        valid_flat * arrived.reshape(-1), targets, num_segments=cell_total
    ).reshape(pressure_rhs.shape)
    coupling = receptor_count * smoothed - arrived_sum
    residual = pressure_rhs - applied - penalty_weight * coupling
    coarse_rhs = block_mean(residual)
    coarse_cond = block_mean(conductivity)
    coarse_diag = stencil_weight_sum * coarse_cond * coarse_scale
    update = damping * coarse_rhs / coarse_diag
    first_pad = extended(jnp.stack([update, coarse_cond]), (("gx", 2), ("gy", 3)), 1)
    field_pad = first_pad[0]
    cond_pad = first_pad[1]
    for sweep_index in range(CSWEEP - 1):
        if sweep_index > 0:
            field_pad = extended(update, (("gx", 1), ("gy", 2)), 1)
        update = (
            update
            + damping
            * (coarse_rhs - stencil_apply(field_pad, cond_pad) * coarse_scale)
            / coarse_diag
        )
    pressure = smoothed + prolong(update)
    return (pressure, residual)


def solution(mesh):
    return jax.shard_map(
        local,
        mesh=mesh,
        in_specs=(
            P(None, "gx", "gy", None),
            P(None, "gx", "gy", None),
            P("gx", None, None),
            P("gx", "gy", None, None),
            P(None, "gx", "gy", None, None),
            P("gx", "gy", None, None),
        ),
        out_specs=(P(None, "gx", "gy", None), P(None, "gx", "gy", None)),
        check_vma=False,
    )
```

profile of v0, /device:TPU:552, one launch (start us, length us, event | category | flops | bytes accessed | tf_op | source)
XLA Modules:
  0.0 131.4 jit_solution(9914158355198658650)
XLA Ops:
  1.7 11.3 %scatter_custom_fusion = f32[8192]{0:T(1024)S(1)} fusion(s32[2048]{0:T(1024)S(1)} %bitcast.218, f32[2048]{0:T(1024)S(1)} %convert_element_type.4, f32[]{:T(128)} %constant.109.clone.1), kind=kCustom, calls=%fused_computation.193 | custom fusion | flops 2048 | bytes 32772 | tf_op jit(solution)/shard_map/scatter-add | solution.py:122
  14.5 5.3 %collective-permute-start.1 = (f32[2,2,1,8,128]{4,3,2,1,0:T(8,128)S(1)}, f32[2,2,1,8,128]{4,3,2,1,0:T(8,128)S(1)}, u32[]{:S(2)}, u32[]{:S(2)}) collective-permute-start(f32[2,2,1,8,128]{4,3,2,1,0:T(8,128)S(1)} %get-tuple-element.13), channel_id=1, source_target_pairs={{8,0},{16,8},{24,16},{32,24},{40,32},{48,40},{56,48},{64,56},{72,6... | collective-permute-start | bytes 49160 | tf_op jit(solution)/shard_map/ppermute | solution.py:31
  30.0 2.6 %copy.18 = f32[8,8192]{0,1:T(8,128)} copy(f32[8,8192]{1,0:T(8,128)S(1)} %stack.60) | data formatting | bytes 524288 | tf_op jit(solution)/shard_map/stack | solution.py:92
  32.6 7.6 %gather_fusion = f32[2048,8]{1,0:T(8,128)S(1)} fusion(f32[8,8192]{0,1:T(8,128)} %copy.18, s32[2048]{0:T(1024)S(1)} %broadcast_clamp_fusion), kind=kCustom, calls=%fused_computation | custom fusion | bytes 139264 | tf_op jit(solution)/shard_map/jit(_take)/gather | solution.py:93
  41.2 7.1 %all-to-all-start = ((f32[8,1,256]{2,1,0:T(1,128)}), f32[8,1,256]{2,1,0:T(1,128)S(1)}, u32[]{:S(2)}, u32[]{:S(2)}) async-start(f32[8,1,256]{2,1,0:T(1,128)} %all_to_all.6), calls=%async_computation | async-start | bytes 16384 | tf_op jit(solution)/shard_map/all_to_all | solution.py:134
  48.7 3.4 %collective-permute-start.3 = (f32[2,2,6,1,128]{4,3,2,1,0:T(1,128)S(1)}, f32[2,2,6,1,128]{4,3,2,1,0:T(1,128)S(1)}, u32[]{:S(2)}, u32[]{:S(2)}) collective-permute-start(f32[2,2,6,1,128]{4,3,2,1,0:T(1,128)S(1)} %get-tuple-element.11), channel_id=1, source_target_pairs={{1,0},{2,1},{3,2},{4,3},{5,4},{6,5},{7,6},{9,8},{10,9},{11,10},{12... | collective-permute-start | bytes 36872 | tf_op jit(solution)/shard_map/ppermute | solution.py:31
  52.1 2.5 %collective-permute-start.2 = (f32[2,2,6,1,128]{4,3,2,1,0:T(1,128)S(1)}, f32[2,2,6,1,128]{4,3,2,1,0:T(1,128)S(1)}, u32[]{:S(2)}, u32[]{:S(2)}) collective-permute-start(f32[2,2,6,1,128]{4,3,2,1,0:T(1,128)S(1)} %get-tuple-element.10), channel_id=1, source_target_pairs={{0,1},{1,2},{2,3},{3,4},{4,5},{5,6},{6,7},{8,9},{9,10},{10,11},{11... | collective-permute-start | bytes 36872 | tf_op jit(solution)/shard_map/ppermute | solution.py:30
  54.6 11.3 %scatter_custom_fusion.1 = f32[8192]{0:T(1024)S(1)} fusion(s32[2048]{0:T(1024)S(1)} %bitcast.219, f32[2048]{0:T(1024)S(1)} %broadcast_select_fusion, f32[]{:T(128)} %constant.109.clone.1), kind=kCustom, calls=%fused_computation.191 | custom fusion | flops 2048 | bytes 32772 | tf_op jit(solution)/shard_map/scatter-add | solution.py:137
  67.4 5.8 %collective-permute-start.5 = (f32[2,2,1,2,32]{4,3,1,2,0:T(2,128)S(1)}, f32[2,2,1,2,32]{4,3,1,2,0:T(2,128)S(1)}, u32[]{:S(2)}, u32[]{:S(2)}) collective-permute-start(f32[2,2,1,2,32]{4,3,1,2,0:T(2,128)S(1)} %pad_maximum_fusion.14), channel_id=1, source_target_pairs={{8,0},{16,8},{24,16},{32,24},{40,32},{48,40},{56,48},{64,56},{72,6... | collective-permute-start | bytes 3080 | tf_op jit(solution)/shard_map/ppermute | solution.py:31
  73.2 1.9 %collective-permute-start.4 = (f32[2,2,1,2,32]{4,3,1,2,0:T(2,128)S(1)}, f32[2,2,1,2,32]{4,3,1,2,0:T(2,128)S(1)}, u32[]{:S(2)}, u32[]{:S(2)}) collective-permute-start(f32[2,2,1,2,32]{4,3,1,2,0:T(2,128)S(1)} %pad_maximum_fusion.14), channel_id=1, source_target_pairs={{0,8},{8,16},{16,24},{24,32},{32,40},{40,48},{48,56},{56,64},{64,7... | collective-permute-start | bytes 3080 | tf_op jit(solution)/shard_map/ppermute | solution.py:30
  75.1 6.3 %collective-permute-done.4 = f32[2,2,1,2,32]{4,3,1,2,0:T(2,128)S(1)} collective-permute-done((f32[2,2,1,2,32]{4,3,1,2,0:T(2,128)S(1)}, f32[2,2,1,2,32]{4,3,1,2,0:T(2,128)S(1)}, u32[]{:S(2)}, u32[]{:S(2)}) %collective-permute-start.4) | collective-permute-done | bytes 1056 | tf_op jit(solution)/shard_map/ppermute | solution.py:30
  81.5 3.4 %collective-permute-start.7 = (f32[2,2,3,1,32]{4,3,1,2,0:T(1,128)S(1)}, f32[2,2,3,1,32]{4,3,1,2,0:T(1,128)S(1)}, u32[]{:S(2)}, u32[]{:S(2)}) collective-permute-start(f32[2,2,3,1,32]{4,3,1,2,0:T(1,128)S(1)} %get-tuple-element.27), channel_id=1, source_target_pairs={{1,0},{2,1},{3,2},{4,3},{5,4},{6,5},{7,6},{9,8},{10,9},{11,10},{12... | collective-permute-start | bytes 4616 | tf_op jit(solution)/shard_map/ppermute | solution.py:31
  84.9 2.5 %collective-permute-start.6 = (f32[2,2,3,1,32]{4,3,1,2,0:T(1,128)S(1)}, f32[2,2,3,1,32]{4,3,1,2,0:T(1,128)S(1)}, u32[]{:S(2)}, u32[]{:S(2)}) collective-permute-start(f32[2,2,3,1,32]{4,3,1,2,0:T(1,128)S(1)} %get-tuple-element.26), channel_id=1, source_target_pairs={{0,1},{1,2},{2,3},{3,4},{4,5},{5,6},{6,7},{8,9},{9,10},{10,11},{11... | collective-permute-start | bytes 4616 | tf_op jit(solution)/shard_map/ppermute | solution.py:30
  87.3 3.0 %collective-permute-done.6 = f32[2,2,3,1,32]{4,3,1,2,0:T(1,128)S(1)} collective-permute-done((f32[2,2,3,1,32]{4,3,1,2,0:T(1,128)S(1)}, f32[2,2,3,1,32]{4,3,1,2,0:T(1,128)S(1)}, u32[]{:S(2)}, u32[]{:S(2)}) %collective-permute-start.6) | collective-permute-done | bytes 1568 | tf_op jit(solution)/shard_map/ppermute | solution.py:30
  92.6 2.4 %collective-permute-start.8 = (f32[2,1,2,32]{3,2,0,1:T(2,128)S(1)}, f32[2,1,2,32]{3,2,0,1:T(2,128)S(1)}, u32[]{:S(2)}, u32[]{:S(2)}) collective-permute-start(f32[2,1,2,32]{3,2,0,1:T(2,128)S(1)} %fusion.242), channel_id=1, source_target_pairs={{0,8},{8,16},{16,24},{24,32},{32,40},{40,48},{48,56},{56,64},{64,7... | collective-permute-start | bytes 1544 | tf_op jit(solution)/shard_map/ppermute | solution.py:30
  95.0 5.8 %collective-permute-done.8 = f32[2,1,2,32]{3,2,0,1:T(2,128)S(1)} collective-permute-done((f32[2,1,2,32]{3,2,0,1:T(2,128)S(1)}, f32[2,1,2,32]{3,2,0,1:T(2,128)S(1)}, u32[]{:S(2)}, u32[]{:S(2)}) %collective-permute-start.8) | collective-permute-done | bytes 544 | tf_op jit(solution)/shard_map/ppermute | solution.py:30
  100.9 4.9 %collective-permute-start.11 = (f32[2,3,1,32]{3,2,0,1:T(1,128)S(1)}, f32[2,3,1,32]{3,2,0,1:T(1,128)S(1)}, u32[]{:S(2)}, u32[]{:S(2)}) collective-permute-start(f32[2,3,1,32]{3,2,0,1:T(1,128)S(1)} %get-tuple-element.31), channel_id=1, source_target_pairs={{1,0},{2,1},{3,2},{4,3},{5,4},{6,5},{7,6},{9,8},{10,9},{11,10},{12... | collective-permute-start | bytes 2312 | tf_op jit(solution)/shard_map/ppermute | solution.py:31
  105.8 1.9 %collective-permute-start.10 = (f32[2,3,1,32]{3,2,0,1:T(1,128)S(1)}, f32[2,3,1,32]{3,2,0,1:T(1,128)S(1)}, u32[]{:S(2)}, u32[]{:S(2)}) collective-permute-start(f32[2,3,1,32]{3,2,0,1:T(1,128)S(1)} %get-tuple-element.30), channel_id=1, source_target_pairs={{0,1},{1,2},{2,3},{3,4},{4,5},{5,6},{6,7},{8,9},{9,10},{10,11},{11... | collective-permute-start | bytes 2312 | tf_op jit(solution)/shard_map/ppermute | solution.py:30
  107.7 3.6 %collective-permute-done.10 = f32[2,3,1,32]{3,2,0,1:T(1,128)S(1)} collective-permute-done((f32[2,3,1,32]{3,2,0,1:T(1,128)S(1)}, f32[2,3,1,32]{3,2,0,1:T(1,128)S(1)}, u32[]{:S(2)}, u32[]{:S(2)}) %collective-permute-start.10) | collective-permute-done | bytes 800 | tf_op jit(solution)/shard_map/ppermute | solution.py:30
  113.4 2.4 %collective-permute-start.12 = (f32[2,1,2,32]{3,2,0,1:T(2,128)S(1)}, f32[2,1,2,32]{3,2,0,1:T(2,128)S(1)}, u32[]{:S(2)}, u32[]{:S(2)}) collective-permute-start(f32[2,1,2,32]{3,2,0,1:T(2,128)S(1)} %fusion.334), channel_id=1, source_target_pairs={{0,8},{8,16},{16,24},{24,32},{32,40},{40,48},{48,56},{56,64},{64,7... | collective-permute-start | bytes 1544 | tf_op jit(solution)/shard_map/ppermute | solution.py:30
  115.8 5.8 %collective-permute-done.12 = f32[2,1,2,32]{3,2,0,1:T(2,128)S(1)} collective-permute-done((f32[2,1,2,32]{3,2,0,1:T(2,128)S(1)}, f32[2,1,2,32]{3,2,0,1:T(2,128)S(1)}, u32[]{:S(2)}, u32[]{:S(2)}) %collective-permute-start.12) | collective-permute-done | bytes 544 | tf_op jit(solution)/shard_map/ppermute | solution.py:30
  121.6 3.1 %collective-permute-start.15 = (f32[2,3,1,32]{3,2,0,1:T(1,128)S(1)}, f32[2,3,1,32]{3,2,0,1:T(1,128)S(1)}, u32[]{:S(2)}, u32[]{:S(2)}) collective-permute-start(f32[2,3,1,32]{3,2,0,1:T(1,128)S(1)} %get-tuple-element.29), channel_id=1, source_target_pairs={{1,0},{2,1},{3,2},{4,3},{5,4},{6,5},{7,6},{9,8},{10,9},{11,10},{12... | collective-permute-start | bytes 2312 | tf_op jit(solution)/shard_map/ppermute | solution.py:31
  124.8 2.7 %collective-permute-start.14 = (f32[2,3,1,32]{3,2,0,1:T(1,128)S(1)}, f32[2,3,1,32]{3,2,0,1:T(1,128)S(1)}, u32[]{:S(2)}, u32[]{:S(2)}) collective-permute-start(f32[2,3,1,32]{3,2,0,1:T(1,128)S(1)} %get-tuple-element.28), channel_id=1, source_target_pairs={{0,1},{1,2},{2,3},{3,4},{4,5},{5,6},{6,7},{8,9},{9,10},{10,11},{11... | collective-permute-start | bytes 2312 | tf_op jit(solution)/shard_map/ppermute | solution.py:30
  127.5 2.8 %collective-permute-done.14 = f32[2,3,1,32]{3,2,0,1:T(1,128)S(1)} collective-permute-done((f32[2,3,1,32]{3,2,0,1:T(1,128)S(1)}, f32[2,3,1,32]{3,2,0,1:T(1,128)S(1)}, u32[]{:S(2)}, u32[]{:S(2)}) %collective-permute-start.14) | collective-permute-done | bytes 800 | tf_op jit(solution)/shard_map/ppermute | solution.py:30
  (90 shorter events, 20.9 us)
Async XLA Ops:
  0.6 0.7 copy-start
  14.5 34.2 %collective-permute-start.1 = (f32[2,2,1,8,128]{4,3,2,1,0:T(8,128)S(1)}, f32[2,2,1,8,128]{4,3,2,1,0:T(8,128)S(1)}, u32[]{:S(2)}, u32[]{:S(2)}) collective-permute-start(f32[2,2,1,8,128]{4,3,2,1,0:T(8,128)S(1)} %get-tuple-element.13), channel_id=1, source_target_pairs={{8,0},{16,8},{24,16},{32,24},{40,32},{48,40},{56,48},{64,56},{72,6... | collective-permute-start | bytes 49160 | tf_op jit(solution)/shard_map/ppermute | solution.py:31
  19.8 28.9 %collective-permute-start = (f32[2,2,1,8,128]{4,3,2,1,0:T(8,128)S(1)}, f32[2,2,1,8,128]{4,3,2,1,0:T(8,128)S(1)}, u32[]{:S(2)}, u32[]{:S(2)}) collective-permute-start(f32[2,2,1,8,128]{4,3,2,1,0:T(8,128)S(1)} %get-tuple-element.12), channel_id=1, source_target_pairs={{0,8},{8,16},{16,24},{24,32},{32,40},{40,48},{48,56},{56,64},{64,7... | collective-permute-start | bytes 49160 | tf_op jit(solution)/shard_map/ppermute | solution.py:30
  21.9 26.8 %copy-start.1 = (f32[2,4,8,128]{3,2,1,0:T(8,128)S(1)}, f32[2,4,8,128]{3,2,1,0:T(8,128)}, u32[]{:S(2)}) copy-start(f32[2,4,8,128]{3,2,1,0:T(8,128)} %param.7) | copy-start | bytes 98308
  29.9 36.1 %copy-start.2 = (f32[2,4,8,128]{3,2,1,0:T(8,128)S(1)}, f32[2,4,8,128]{3,2,1,0:T(8,128)}, u32[]{:S(2)}) copy-start(f32[2,4,8,128]{3,2,1,0:T(8,128)} %param.6) | copy-start | bytes 98308
  41.2 13.4 %all-to-all-start = ((f32[8,1,256]{2,1,0:T(1,128)}), f32[8,1,256]{2,1,0:T(1,128)S(1)}, u32[]{:S(2)}, u32[]{:S(2)}) async-start(f32[8,1,256]{2,1,0:T(1,128)} %all_to_all.6), calls=%async_computation | async-start | bytes 16384 | tf_op jit(solution)/shard_map/all_to_all | solution.py:134
  48.7 17.2 %collective-permute-start.3 = (f32[2,2,6,1,128]{4,3,2,1,0:T(1,128)S(1)}, f32[2,2,6,1,128]{4,3,2,1,0:T(1,128)S(1)}, u32[]{:S(2)}, u32[]{:S(2)}) collective-permute-start(f32[2,2,6,1,128]{4,3,2,1,0:T(1,128)S(1)} %get-tuple-element.11), channel_id=1, source_target_pairs={{1,0},{2,1},{3,2},{4,3},{5,4},{6,5},{7,6},{9,8},{10,9},{11,10},{12... | collective-permute-start | bytes 36872 | tf_op jit(solution)/shard_map/ppermute | solution.py:31
  52.1 13.8 %collective-permute-start.2 = (f32[2,2,6,1,128]{4,3,2,1,0:T(1,128)S(1)}, f32[2,2,6,1,128]{4,3,2,1,0:T(1,128)S(1)}, u32[]{:S(2)}, u32[]{:S(2)}) collective-permute-start(f32[2,2,6,1,128]{4,3,2,1,0:T(1,128)S(1)} %get-tuple-element.10), channel_id=1, source_target_pairs={{0,1},{1,2},{2,3},{3,4},{4,5},{5,6},{6,7},{8,9},{9,10},{10,11},{11... | collective-permute-start | bytes 36872 | tf_op jit(solution)/shard_map/ppermute | solution.py:30
  67.4 7.8 %collective-permute-start.5 = (f32[2,2,1,2,32]{4,3,1,2,0:T(2,128)S(1)}, f32[2,2,1,2,32]{4,3,1,2,0:T(2,128)S(1)}, u32[]{:S(2)}, u32[]{:S(2)}) collective-permute-start(f32[2,2,1,2,32]{4,3,1,2,0:T(2,128)S(1)} %pad_maximum_fusion.14), channel_id=1, source_target_pairs={{8,0},{16,8},{24,16},{32,24},{40,32},{48,40},{56,48},{64,56},{72,6... | collective-permute-start | bytes 3080 | tf_op jit(solution)/shard_map/ppermute | solution.py:31
  73.2 8.2 %collective-permute-start.4 = (f32[2,2,1,2,32]{4,3,1,2,0:T(2,128)S(1)}, f32[2,2,1,2,32]{4,3,1,2,0:T(2,128)S(1)}, u32[]{:S(2)}, u32[]{:S(2)}) collective-permute-start(f32[2,2,1,2,32]{4,3,1,2,0:T(2,128)S(1)} %pad_maximum_fusion.14), channel_id=1, source_target_pairs={{0,8},{8,16},{16,24},{24,32},{32,40},{40,48},{48,56},{56,64},{64,7... | collective-permute-start | bytes 3080 | tf_op jit(solution)/shard_map/ppermute | solution.py:30
  81.5 5.9 %collective-permute-start.7 = (f32[2,2,3,1,32]{4,3,1,2,0:T(1,128)S(1)}, f32[2,2,3,1,32]{4,3,1,2,0:T(1,128)S(1)}, u32[]{:S(2)}, u32[]{:S(2)}) collective-permute-start(f32[2,2,3,1,32]{4,3,1,2,0:T(1,128)S(1)} %get-tuple-element.27), channel_id=1, source_target_pairs={{1,0},{2,1},{3,2},{4,3},{5,4},{6,5},{7,6},{9,8},{10,9},{11,10},{12... | collective-permute-start | bytes 4616 | tf_op jit(solution)/shard_map/ppermute | solution.py:31
  84.9 5.5 %collective-permute-start.6 = (f32[2,2,3,1,32]{4,3,1,2,0:T(1,128)S(1)}, f32[2,2,3,1,32]{4,3,1,2,0:T(1,128)S(1)}, u32[]{:S(2)}, u32[]{:S(2)}) collective-permute-start(f32[2,2,3,1,32]{4,3,1,2,0:T(1,128)S(1)} %get-tuple-element.26), channel_id=1, source_target_pairs={{0,1},{1,2},{2,3},{3,4},{4,5},{5,6},{6,7},{8,9},{9,10},{10,11},{11... | collective-permute-start | bytes 4616 | tf_op jit(solution)/shard_map/ppermute | solution.py:30
  90.7 4.3 %collective-permute-start.9 = (f32[2,1,2,32]{3,2,0,1:T(2,128)S(1)}, f32[2,1,2,32]{3,2,0,1:T(2,128)S(1)}, u32[]{:S(2)}, u32[]{:S(2)}) collective-permute-start(f32[2,1,2,32]{3,2,0,1:T(2,128)S(1)} %fusion.242), channel_id=1, source_target_pairs={{8,0},{16,8},{24,16},{32,24},{40,32},{48,40},{56,48},{64,56},{72,6... | collective-permute-start | bytes 1544 | tf_op jit(solution)/shard_map/ppermute | solution.py:31
  92.6 8.2 %collective-permute-start.8 = (f32[2,1,2,32]{3,2,0,1:T(2,128)S(1)}, f32[2,1,2,32]{3,2,0,1:T(2,128)S(1)}, u32[]{:S(2)}, u32[]{:S(2)}) collective-permute-start(f32[2,1,2,32]{3,2,0,1:T(2,128)S(1)} %fusion.242), channel_id=1, source_target_pairs={{0,8},{8,16},{16,24},{24,32},{32,40},{40,48},{48,56},{56,64},{64,7... | collective-permute-start | bytes 1544 | tf_op jit(solution)/shard_map/ppermute | solution.py:30
  100.9 6.8 %collective-permute-start.11 = (f32[2,3,1,32]{3,2,0,1:T(1,128)S(1)}, f32[2,3,1,32]{3,2,0,1:T(1,128)S(1)}, u32[]{:S(2)}, u32[]{:S(2)}) collective-permute-start(f32[2,3,1,32]{3,2,0,1:T(1,128)S(1)} %get-tuple-element.31), channel_id=1, source_target_pairs={{1,0},{2,1},{3,2},{4,3},{5,4},{6,5},{7,6},{9,8},{10,9},{11,10},{12... | collective-permute-start | bytes 2312 | tf_op jit(solution)/shard_map/ppermute | solution.py:31
  105.8 5.5 %collective-permute-start.10 = (f32[2,3,1,32]{3,2,0,1:T(1,128)S(1)}, f32[2,3,1,32]{3,2,0,1:T(1,128)S(1)}, u32[]{:S(2)}, u32[]{:S(2)}) collective-permute-start(f32[2,3,1,32]{3,2,0,1:T(1,128)S(1)} %get-tuple-element.30), channel_id=1, source_target_pairs={{0,1},{1,2},{2,3},{3,4},{4,5},{5,6},{6,7},{8,9},{9,10},{10,11},{11... | collective-permute-start | bytes 2312 | tf_op jit(solution)/shard_map/ppermute | solution.py:30
  111.5 4.3 %collective-permute-start.13 = (f32[2,1,2,32]{3,2,0,1:T(2,128)S(1)}, f32[2,1,2,32]{3,2,0,1:T(2,128)S(1)}, u32[]{:S(2)}, u32[]{:S(2)}) collective-permute-start(f32[2,1,2,32]{3,2,0,1:T(2,128)S(1)} %fusion.334), channel_id=1, source_target_pairs={{8,0},{16,8},{24,16},{32,24},{40,32},{48,40},{56,48},{64,56},{72,6... | collective-permute-start | bytes 1544 | tf_op jit(solution)/shard_map/ppermute | solution.py:31
  113.4 8.2 %collective-permute-start.12 = (f32[2,1,2,32]{3,2,0,1:T(2,128)S(1)}, f32[2,1,2,32]{3,2,0,1:T(2,128)S(1)}, u32[]{:S(2)}, u32[]{:S(2)}) collective-permute-start(f32[2,1,2,32]{3,2,0,1:T(2,128)S(1)} %fusion.334), channel_id=1, source_target_pairs={{0,8},{8,16},{16,24},{24,32},{32,40},{40,48},{48,56},{56,64},{64,7... | collective-permute-start | bytes 1544 | tf_op jit(solution)/shard_map/ppermute | solution.py:30
  121.6 5.9 %collective-permute-start.15 = (f32[2,3,1,32]{3,2,0,1:T(1,128)S(1)}, f32[2,3,1,32]{3,2,0,1:T(1,128)S(1)}, u32[]{:S(2)}, u32[]{:S(2)}) collective-permute-start(f32[2,3,1,32]{3,2,0,1:T(1,128)S(1)} %get-tuple-element.29), channel_id=1, source_target_pairs={{1,0},{2,1},{3,2},{4,3},{5,4},{6,5},{7,6},{9,8},{10,9},{11,10},{12... | collective-permute-start | bytes 2312 | tf_op jit(solution)/shard_map/ppermute | solution.py:31
  124.8 5.5 %collective-permute-start.14 = (f32[2,3,1,32]{3,2,0,1:T(1,128)S(1)}, f32[2,3,1,32]{3,2,0,1:T(1,128)S(1)}, u32[]{:S(2)}, u32[]{:S(2)}) collective-permute-start(f32[2,3,1,32]{3,2,0,1:T(1,128)S(1)} %get-tuple-element.28), channel_id=1, source_target_pairs={{0,1},{1,2},{2,3},{3,4},{4,5},{5,6},{6,7},{8,9},{9,10},{10,11},{11... | collective-permute-start | bytes 2312 | tf_op jit(solution)/shard_map/ppermute | solution.py:30
where the time goes:
time: 133 us; the launch traced here: 131 us
  starting transfers between devices  55.1 us (41%)
  other arithmetic  33.9 us (25%)
  waiting for transfers between devices  27.3 us (21%)
  local copies, waits for them, and re-layouts  14 us (11%)
    ppermute x8, starting transfers between devices, extended(): after = lax.ppermute(leading, axis, down)  29.7 us
    ppermute x8, waiting for transfers between devices, extended(): before = lax.ppermute(last, axis, up)  27.3 us
    ppermute x8, starting transfers between devices, extended(): before = lax.ppermute(last, axis, up)  18.2 us
    scatter-add x1, other arithmetic, local(): jax.ops.segment_sum(valid_flat, targets, num_segments=cell_total)  11.3 us
    scatter-add x1, other arithmetic, local(): jax.ops.segment_sum(valid_flat * arrived.reshape(-1), targets, num_segmen...  11.3 us
    gather x2, local copies, waits for them, and re-layouts, interpolate(): picked = jnp.take(corner_table, corner, axis=1)  7.94 us
    all_to_all x1, starting transfers between devices, local(): lax.all_to_all(donor_values, 'gy', split_axis=0, concat_axis=0, tiled=True)  7.09 us
    unnamed x8, other arithmetic  5.89 us
  transfers between devices with their start and end apart: 17, of which 6 were waited for; matrix products, arithmetic and copies ran while one was open for 23% of the time, Pallas kernels for 0%

commit v1 on v0

v1 whole, which is shorter than its diff:
```python
import functools

import jax
import jax.numpy as jnp
from jax import lax
from jax.experimental import pallas as pl
from jax.experimental.pallas import tpu as pltpu
from jax.sharding import PartitionSpec as P

BLOCK = 128
ROW = 8
F32 = jnp.float32
BF16 = jnp.bfloat16
damping = 0.8
penalty_weight = 2.0
coarse_scale = 0.0625
stencil_weight_sum = 44.0 / 3.0
half_weight_sum = 22.0 / 3.0
MEMORY = 32 * 1024 * 1024


def iota(shape, axis):
    return lax.broadcasted_iota(jnp.int32, shape, axis)


def parts(value, count):
    cuts = []
    for index in range(count):
        cut = value.astype(BF16)
        cuts.append(cut)
        if index + 1 < count:
            value = value - cut.astype(F32)
    return cuts


def one_hots(cells, valid):
    rows = cells.shape[1]
    high = jnp.where(valid, cells >> 7, -1)
    low = cells & 127
    return iota((64, rows), 0) == high, (iota((128, rows), 0) == low).astype(F32).astype(BF16)


def contract_rows(left, right):
    return lax.dot_general(left, right, (((1,), (1,)), ((), ())), preferred_element_type=F32)


def smooth_kernel(ids, counts, cells, rhs, cond, smoothed, count, near, far):
    own, core = ids[0], ids[1]
    lane = iota((1, 256), 1)
    total = jnp.zeros((64, 128), F32)
    for b in range(8):
        valid = lane < counts[b, own] * BLOCK
        high, low = one_hots(cells[b : b + 1, :], valid)
        total = total + contract_rows(high.astype(F32).astype(BF16), low)
    total = total.reshape(8, 8, 128)
    count[...] = total
    value = damping * rhs[...] / (stencil_weight_sum * cond[...] + penalty_weight * total)
    smoothed[...] = value
    first = core == 0
    for grid in range(2):
        low_x, high_x = grid * 4, grid * 4 + 3
        near[grid] = jnp.where(first, value[high_x], value[low_x])
        far[grid] = jnp.where(first, value[low_x], value[high_x])
        near[2 + grid] = jnp.where(first, cond[high_x], cond[low_x])
        far[2 + grid] = jnp.where(first, cond[low_x], cond[high_x])


def donor_kernel(base, frac, smoothed, donors):
    field = smoothed[...].reshape(64, 128)
    high = field.astype(BF16).astype(F32)
    stacked = jnp.concatenate([high, field - high, high], axis=0)
    columns = stacked.T.astype(BF16)
    q = base[...]
    grid = (q >= 2667).astype(jnp.int32)
    q = q - grid * 2667
    x = (q >= 889).astype(jnp.int32) + (q >= 1778).astype(jnp.int32)
    q = q - x * 889
    y = jnp.zeros_like(q)
    for step in range(1, 7):
        y = y + (q >= step * 127).astype(jnp.int32)
    z = q - y * 127
    plane = grid * 4 + x
    eight = iota((8, 256), 0)
    wide = iota((128, 256), 0)
    for d in range(8):
        row = slice(d, d + 1)
        frac_x, frac_y, frac_z = frac[0, row, :], frac[1, row, :], frac[2, row, :]
        at_x, at_y, at_z = plane[row], y[row], z[row]
        weight_x = jnp.where(eight == at_x, 1.0 - frac_x, jnp.where(eight == at_x + 1, frac_x, 0.0))
        weight_y = jnp.where(eight == at_y, 1.0 - frac_y, jnp.where(eight == at_y + 1, frac_y, 0.0))
        weight_z = jnp.where(wide == at_z, 1.0 - frac_z, jnp.where(wide == at_z + 1, frac_z, 0.0))
        weight = jnp.concatenate([weight_x[p : p + 1] * weight_y for p in range(8)], axis=0)
        upper, lower = parts(weight, 2)
        mixed = jnp.dot(
            columns, jnp.concatenate([upper, upper, lower], axis=0), preferred_element_type=F32
        )
        donors[row, :] = jnp.sum(mixed * weight_z, axis=0, keepdims=True)


def sides(core, near, far, index):
    first = core == 0
    return (
        jnp.where(first, far[index], near[index]),
        jnp.where(first, near[index], far[index]),
    )


def pack_kernel(ids, donors, smoothed, cond, near, far, sent):
    own, core = ids[0], ids[1]
    first = core == 0
    faces = []
    for y in (0, 7):
        near_rows = near[pl.ds(y, 4, stride=8), :]
        far_rows = far[pl.ds(y, 4, stride=8), :]
        faces.append(
            (
                smoothed[pl.ds(y, 8, stride=8), :],
                cond[pl.ds(y, 8, stride=8), :],
                jnp.where(first, far_rows, near_rows),
                jnp.where(first, near_rows, far_rows),
            )
        )
    for d in range(8):
        above = d > own
        bottom, top = faces
        sent[d, 0:8, :] = jnp.where(above, top[0], bottom[0])
        sent[d, 8:16, :] = jnp.where(above, top[1], bottom[1])
        sent[d, 16:20, :] = jnp.where(above, top[2], bottom[2])
        sent[d, 20:24, :] = jnp.where(above, top[3], bottom[3])
        sent[d, 24:25, :] = donors[d : d + 1, 0:128]
        sent[d, 25:26, :] = donors[d : d + 1, 128:256]


def neighbour_sums(fields, shift_y, shift_z):
    inner, outer = [], []
    for field in fields:
        beside_z = shift_z(field)
        beside_y = shift_y(field)
        both = shift_z(beside_y)
        inner.append(0.5 * (beside_z + beside_y) + 0.25 * both)
        outer.append(0.5 * field + 0.25 * (beside_z + beside_y) + (1.0 / 6.0) * both)
    return [inner[i] + outer[i - 1] + outer[i + 1] for i in range(1, len(fields) - 1)]


def residual_kernel(
    ids, counts, cells, arrived, smoothed, count, rhs, cond, near, far, residual, coarse
):
    own, core = ids[0], ids[1]
    lane = iota((1, 256), 1)
    total = jnp.zeros((192, 128), F32)
    for b in range(8):
        valid = lane < counts[b, own] * BLOCK
        high, low = one_hots(cells[b : b + 1, :], valid)
        values = jnp.concatenate([arrived[b, 24:25, :], arrived[b, 25:26, :]], axis=1)
        left = jnp.concatenate(
            [jnp.where(high, cut.astype(F32), 0.0).astype(BF16) for cut in parts(values, 3)], axis=0
        )
        total = total + contract_rows(left, low)
    total = (total[0:64] + total[64:128] + total[128:192]).reshape(8, 8, 128)

    below = jnp.maximum(own - 1, 0)
    above = jnp.minimum(own + 1, 7)
    has_below = own > 0
    has_above = own < 7
    lanes = iota((8, 128), 1)
    rows = iota((8, 128), 0)
    keep_up = lanes < 127
    keep_down = lanes > 0

    def shift_z(value):
        return jnp.where(keep_down, pltpu.roll(value, 1, 1), 0.0) + jnp.where(
            keep_up, pltpu.roll(value, 127, 1), 0.0
        )

    def shift_y(value, lower, upper):
        down = jnp.where(rows > 0, pltpu.roll(value, 1, 0), lower)
        up = jnp.where(rows < 7, pltpu.roll(value, 7, 0), upper)
        return down + up

    def halo(device, present, row):
        return jnp.where(present, arrived[device, row : row + 1, :], 0.0)

    pooled = []
    for grid in range(2):
        fields = []
        for f, ref in ((0, smoothed), (1, cond)):
            left, right = sides(core, near, far, 2 * f + grid)
            planes = [left] + [ref[grid * 4 + x] for x in range(4)] + [right]
            at = [16 + 2 * f + grid] + [8 * f + grid * 4 + x for x in range(4)] + [20 + 2 * f + grid]
            lower = [halo(below, has_below, row) for row in at]
            upper = [halo(above, has_above, row) for row in at]
            fields.append((planes, lower, upper))
        fields.append(tuple([v * c for v, c in zip(*pair)] for pair in zip(*fields)))
        sums = []
        for planes, lower, upper in fields:
            inner, outer = [], []
            for plane, low_row, high_row in zip(planes, lower, upper):
                beside_z = shift_z(plane)
                beside_y = shift_y(plane, low_row, high_row)
                both = shift_z(beside_y)
                edge = beside_z + beside_y
                inner.append(0.5 * edge + 0.25 * both)
                outer.append(0.5 * plane + 0.25 * edge + (1.0 / 6.0) * both)
            sums.append([inner[i] + outer[i - 1] + outer[i + 1] for i in range(1, 5)])
        summed = jnp.zeros((8, 128), F32)
        for x in range(4):
            plane = grid * 4 + x
            v, c = smoothed[plane], cond[plane]
            applied = v * (half_weight_sum * c + sums[1][x]) - c * sums[0][x] - sums[2][x]
            value = (
                rhs[plane] - applied - penalty_weight * (count[plane] * v - total[plane])
            )
            residual[plane] = value
            summed = summed + value
        pooled.append(summed)
    for grid in range(2):
        pooled.append(cond[grid * 4] + cond[grid * 4 + 1] + cond[grid * 4 + 2] + cond[grid * 4 + 3])
    pool = (iota((128, 128), 0) // 4 == iota((128, 128), 1) % 32).astype(F32)
    means = jnp.dot(
        jnp.concatenate(pooled, axis=0),
        pool,
        preferred_element_type=F32,
        precision=lax.Precision.HIGHEST,
    ) * (1.0 / 64.0)
    own_part = iota((16, 128), 0) // 4 == iota((16, 128), 1) // 32
    both = [
        jnp.sum(jnp.where(own_part, means[f * 16 : f * 16 + 16], 0.0), axis=0, keepdims=True)
        for f in range(2)
    ]
    coarse[...] = jnp.broadcast_to(jnp.concatenate(both, axis=0)[None], (64, 2, 128))


def coarse_kernel(ids, gathered, extra, smoothed, pressure):
    own, place = ids[0], ids[2]
    lanes = iota((8, 128), 1)
    rows = iota((8, 128), 0)
    low_z = lanes % 32 > 0
    high_z = lanes % 32 < 31
    first_y = lanes % 64 < 32

    def shift_z(value):
        return jnp.where(low_z, pltpu.roll(value, 1, 1), 0.0) + jnp.where(
            high_z, pltpu.roll(value, 127, 1), 0.0
        )

    def shift_y(value):
        ahead = pltpu.roll(value, 96, 1)
        behind = pltpu.roll(value, 32, 1)
        within = jnp.where(first_y, ahead, behind)
        from_below = jnp.where(rows > 0, pltpu.roll(ahead, 1, 0), 0.0)
        from_above = jnp.where(rows < 7, pltpu.roll(behind, 7, 0), 0.0)
        return within + jnp.where(first_y, from_below, from_above)

    rhs, cond = [], []
    for slot in range(7):
        at = place + slot - 3
        inside = jnp.logical_and(at >= 0, at < ROW)
        here = pl.multiple_of(jnp.clip(at, 0, ROW - 1) * 16, 16)
        there = pl.multiple_of((at & 3) * 16, 16)
        for f, out in ((0, rhs), (1, cond)):
            out.append(
                jnp.where(
                    inside,
                    gathered[pl.ds(here + f, 8, stride=2), :],
                    extra[pl.ds(there + f, 8, stride=2), :],
                )
            )
    scale = [
        jnp.where(c > 0.0, damping / (stencil_weight_sum * coarse_scale * jnp.where(c > 0.0, c, 1.0)), 0.0)
        for c in cond
    ]
    value = [r * s for r, s in zip(rhs, scale)]
    own_sum = [
        half_weight_sum * c + s for c, s in zip(cond[1:-1], neighbour_sums(cond, shift_y, shift_z))
    ]
    for sweep in range(3):
        around = neighbour_sums(value, shift_y, shift_z)
        around_both = neighbour_sums(
            [v * c for v, c in zip(value, cond)], shift_y, shift_z
        )
        value, cond, rhs, scale = value[1:-1], cond[1:-1], rhs[1:-1], scale[1:-1]
        value = [
            v + s * (r - coarse_scale * (v * o - c * a - b))
            for v, s, r, o, c, a, b in zip(value, scale, rhs, own_sum, cond, around, around_both)
        ]
        own_sum = own_sum[1:-1]
    mine = jnp.sum(jnp.where(rows == own, value[0], 0.0), axis=0, keepdims=True)
    spread = jnp.where(iota((16, 128), 0) // 4 == iota((16, 128), 1) // 32, mine, 0.0)
    expand = (iota((128, 128), 0) % 32 == iota((128, 128), 1) // 4).astype(F32)
    fine = jnp.dot(spread, expand, preferred_element_type=F32, precision=lax.Precision.HIGHEST)
    for grid in range(2):
        for x in range(4):
            pressure[grid * 4 + x] = smoothed[grid * 4 + x] + fine[grid * 8 : grid * 8 + 8]


def call(kernel, name, outs, operands, scalars, flops=1000000):
    memory = [pltpu.SMEM] * scalars + [pltpu.VMEM] * (len(operands) - scalars)
    shapes = [jax.ShapeDtypeStruct(shape, F32) for shape in outs]
    return pl.pallas_call(
        kernel,
        out_shape=shapes,
        in_specs=[pl.BlockSpec(memory_space=space) for space in memory],
        out_specs=[pl.BlockSpec(memory_space=pltpu.VMEM)] * len(outs),
        compiler_params=pltpu.CompilerParams(vmem_limit_bytes=MEMORY),
        cost_estimate=pl.CostEstimate(flops=flops, bytes_accessed=200000, transcendentals=0),
        name=name,
    )(*operands)


def local(pressure_rhs, conductivity, block_counts, donor_base, donor_frac, receptor_cells):
    shape = pressure_rhs.shape
    along = lax.axis_index("gx")
    own = lax.axis_index("gy")
    size = lax.axis_size("gx")
    ids = jnp.stack([own, along % 2, along % ROW]).astype(jnp.int32)
    rhs = pressure_rhs.reshape(8, 8, 128)
    cond = conductivity.reshape(8, 8, 128)
    counts = block_counts[0]
    cells = receptor_cells[0, 0]
    block = (8, 8, 128)
    smoothed, count, near, far = call(
        smooth_kernel, "smooth", [block, block, (4, 8, 128), (4, 8, 128)],
        (ids, counts, cells, rhs, cond), 2,
    )
    beyond = [(i, i + 1) for i in range(1, size - 1, 2)]
    far_in = lax.ppermute(far, "gx", beyond + [(j, i) for i, j in beyond])
    near_in = lax.ppermute(near, "gx", [(i, i ^ 1) for i in range(size)])
    (donors,) = call(
        donor_kernel, "donor", [(8, 256)], (donor_base[0, 0], donor_frac[:, 0, 0], smoothed), 0
    )
    (sent,) = call(
        pack_kernel, "pack", [(8, 32, 128)],
        (
            ids, donors, smoothed.reshape(64, 128), cond.reshape(64, 128),
            near_in.reshape(32, 128), far_in.reshape(32, 128),
        ), 1,
    )
    arrived = lax.all_to_all(sent, "gy", split_axis=0, concat_axis=0, tiled=True)
    residual, coarse = call(
        residual_kernel, "residual", [block, (64, 2, 128)],
        (ids, counts, cells, arrived, smoothed, count, rhs, cond, near_in, far_in), 2,
    )
    groups = [
        [(start + i) * 8 + j for i in range(ROW) for j in range(8)]
        for start in range(0, size, ROW)
    ]
    gathered = lax.all_to_all(
        coarse, ("gx", "gy"), split_axis=0, concat_axis=0, tiled=True, axis_index_groups=groups
    )
    lower_half = along % ROW < ROW // 2
    passed = jnp.where(lower_half, gathered[32:], gathered[:32])
    step = [(i, i + ROW) if i % ROW < ROW // 2 else (i, i - ROW) for i in range(size)]
    extra = lax.ppermute(passed, "gx", [(i, j) for i, j in step if 0 <= j < size])
    (pressure,) = call(
        coarse_kernel, "coarse", [block],
        (ids, gathered.reshape(128, 128), extra.reshape(64, 128), smoothed), 1,
    )
    return pressure.reshape(shape), residual.reshape(shape)


def solution(mesh):
    return jax.shard_map(
        local,
        mesh=mesh,
        in_specs=(
            P(None, "gx", "gy", None),
            P(None, "gx", "gy", None),
            P("gx", None, None),
            P("gx", "gy", None, None),
            P(None, "gx", "gy", None, None),
            P("gx", "gy", None, None),
        ),
        out_specs=(P(None, "gx", "gy", None), P(None, "gx", "gy", None)),
        check_vma=False,
    )
```

time: 133 us -> 55.8 us (0.42)
  the two profiles are of different devices: /device:TPU:552 before, /device:TPU:192 now
where the time goes in v1:
time: 55.8 us; the launch traced here: 55.4 us
  starting transfers between devices  17 us (30%)
  blocking collectives  16 us (29%)
  waiting for transfers between devices  14.3 us (26%)
  Pallas kernels  5.78 us (10%)
  local copies, waits for them, and re-layouts  1.46 us (3%)
  between operations  0.77 us (1%)
    all_to_all x1, blocking collectives, local(): lax.all_to_all(sent, 'gy', split_axis=0, concat_axis=0, tiled=True)  16 us
    all_to_all x1, waiting for transfers between devices, local(): lax.all_to_all(coarse, ('gx', 'gy'), split_axis=0, concat_axis=0, tiled=T...  9.9 us
    ppermute x1, starting transfers between devices, local(): lax.ppermute(passed, 'gx', [(i, j) for i, j in step if 0 <= j < size])  6.33 us
    pallas_call x5, Pallas kernels, call(): pl.pallas_call(kernel, out_shape=shapes, in_specs=[pl.BlockSpec(memory_sp...  5.78 us
    all_to_all x1, starting transfers between devices, local(): lax.all_to_all(coarse, ('gx', 'gy'), split_axis=0, concat_axis=0, tiled=T...  4.93 us
    ppermute x1, starting transfers between devices, local(): far_in = lax.ppermute(far, 'gx', beyond + [(j, i) for i, j in beyond])  3.86 us
    ppermute x1, waiting for transfers between devices, local(): far_in = lax.ppermute(far, 'gx', beyond + [(j, i) for i, j in beyond])  2.8 us
    ppermute x1, starting transfers between devices, local(): near_in = lax.ppermute(near, 'gx', [(i, i ^ 1) for i in range(size)])  1.92 us
  transfers between devices with their start and end apart: 4, of which 3 were waited for; matrix products, arithmetic and copies ran while one was open for 0% of the time, Pallas kernels for 1%

profile of v1, /device:TPU:192, one launch (start us, length us, event | category | flops | bytes accessed | tf_op | source)
XLA Modules:
  0.0 55.4 jit_solution(10025918840778748432)
XLA Ops:
  0.6 0.0 copy-start
  0.7 0.0 copy-start.2
  0.7 0.1 pad_add_fusion.ids
  0.8 0.6 %copy-done = f32[2,4,8,128]{3,2,1,0:T(8,128)S(1)} copy-done((f32[2,4,8,128]{3,2,1,0:T(8,128)S(1)}, f32[2,4,8,128]{3,2,1,0:T(8,128)}, u32[]{:S(2)}) %copy-start) | copy-done | bytes 32792
  1.4 0.0 copy-done.2
  1.4 0.1 copy-done.4
  1.4 0.8 %copy-done.1 = f32[2,4,8,128]{3,2,1,0:T(8,128)S(1)} copy-done((f32[2,4,8,128]{3,2,1,0:T(8,128)S(1)}, f32[2,4,8,128]{3,2,1,0:T(8,128)}, u32[]{:S(2)}) %copy-start.1) | copy-done | bytes 32792
  2.2 0.9 %smooth.1 = (f32[8,8,128]{2,1,0:T(8,128)S(1)}, f32[8,8,128]{2,1,0:T(8,128)S(1)}, f32[4,8,128]{2,1,0:T(8,128)S(1)}, f32[4,8,128]{2,1,0:T(8,128)S(1)}) custom-call(s32[3]{0:T(128)S(1)} %pad_add_fusion.ids, s32[8,8]{1,0:T(8,128)S(1)} %bitcast.30, s32[8,256]{1,0:T(8,128)S(1)} %bitcast.27, f32[8,8,128]{2,1,0:T(8,128)S(1)} %bitcast.22, f32[8,8,128]{2,1,0:T(8,128)S(1)} %bitcast.19), custom_call_target="tpu_custom_call" | custom-call | flops 1000000 | bytes 200000 | tf_op jit(solution)/shard_map/smooth/pallas_call | solution.py:299
  3.1 0.0 copy-start.5
  3.1 1.9 %collective-permute-start = (f32[4,8,128]{2,1,0:T(8,128)S(1)}, f32[4,8,128]{2,1,0:T(8,128)S(1)}, u32[]{:S(2)}, u32[]{:S(2)}) collective-permute-start(f32[4,8,128]{2,1,0:T(8,128)S(1)} %get-tuple-element.9), channel_id=1, source_target_pairs={{0,8},{8,0},{16,24},{24,16},{32,40},{40,32},{48,56},{56,48},{64,72... | collective-permute-start | bytes 49160 | tf_op jit(solution)/shard_map/ppermute | solution.py:327
  5.1 3.9 %collective-permute-start.1 = (f32[4,8,128]{2,1,0:T(8,128)S(1)}, f32[4,8,128]{2,1,0:T(8,128)S(1)}, u32[]{:S(2)}, u32[]{:S(2)}) collective-permute-start(f32[4,8,128]{2,1,0:T(8,128)S(1)} %get-tuple-element.10), channel_id=1, source_target_pairs={{8,16},{24,32},{40,48},{56,64},{72,80},{88,96},{104,112},{120,128}... | collective-permute-start | bytes 49160 | tf_op jit(solution)/shard_map/ppermute | solution.py:326
  8.9 0.0 copy-done.3
  8.9 0.0 copy-done.5
  8.9 0.5 donor.1.donors
  9.4 0.0 collective-permute-done.near
  9.4 2.8 %collective-permute-done.1.far = f32[4,8,128]{2,1,0:T(8,128)S(1)} collective-permute-done((f32[4,8,128]{2,1,0:T(8,128)S(1)}, f32[4,8,128]{2,1,0:T(8,128)S(1)}, u32[]{:S(2)}, u32[]{:S(2)}) %collective-permute-start.1) | collective-permute-done | bytes 16416 | tf_op jit(solution)/shard_map/ppermute | solution.py:326
  12.2 0.6 %pack.1 = f32[8,32,128]{2,1,0:T(8,128)S(1)} custom-call(s32[3]{0:T(128)S(1)} %pad_add_fusion.ids, f32[8,256]{1,0:T(8,128)S(1)} %donor.1.donors, f32[64,128]{1,0:T(8,128)S(1)} %bitcast.18, f32[64,128]{1,0:T(8,128)S(1)} %bitcast.20, f32[32,128]{1,0:T(8,128)S(1)} %bitcast.24, f32[32,128]{1,0:T(8,128)S(1)} %bitcast.25), custom_call_target="tpu_custom_call" | custom-call | flops 1000000 | bytes 200000 | tf_op jit(solution)/shard_map/pack/pallas_call | solution.py:299
  12.8 16.0 %all_to_all.10.arrived = f32[8,32,128]{2,1,0:T(8,128)S(1)} all-to-all(f32[8,32,128]{2,1,0:T(8,128)S(1)} %pack.1), channel_id=1, replica_groups=mesh['gx'=96,'gy'=8] {'gy'}, dimensions={0} | all-to-all | bytes 262144 | tf_op jit(solution)/shard_map/all_to_all | solution.py:338
  28.8 2.0 %residual.1 = (f32[8,8,128]{2,1,0:T(8,128)}, f32[64,2,128]{2,1,0:T(2,128)}) custom-call(s32[3]{0:T(128)S(1)} %pad_add_fusion.ids, s32[8,8]{1,0:T(8,128)S(1)} %bitcast.31, s32[8,256]{1,0:T(8,128)S(1)} %bitcast.28, f32[8,32,128]{2,1,0:T(8,128)S(1)} %all_to_all.10.arrived, f32[8,8,128]{2,1,0:T(8,128)S(1)} %get-tuple-element.8.smoothed, ...), custom_call_target="tpu_custom_call" | custom-call | flops 1000000 | bytes 200000 | tf_op jit(solution)/shard_map/residual/pallas_call | solution.py:299
  30.8 4.9 %all-to-all-start.1 = ((f32[64,2,128]{2,1,0:T(2,128)}), f32[64,2,128]{2,1,0:T(2,128)S(1)}, u32[]{:S(2)}, u32[]{:S(2)}) async-start(f32[64,2,128]{2,1,0:T(2,128)} %get-tuple-element.12), calls=%async_computation.1 | async-start | bytes 131072 | tf_op jit(solution)/shard_map/all_to_all | solution.py:347
  35.7 9.9 %all-to-all-done.1 = f32[64,2,128]{2,1,0:T(2,128)S(1)} async-done(((f32[64,2,128]{2,1,0:T(2,128)}), f32[64,2,128]{2,1,0:T(2,128)S(1)}, u32[]{:S(2)}, u32[]{:S(2)}) %all-to-all-start.1) | async-done | bytes 65568 | tf_op jit(solution)/shard_map/all_to_all | solution.py:347
  45.6 6.3 %collective-permute-start.2 = (f32[32,2,128]{2,1,0:T(2,128)S(1)}, f32[32,2,128]{2,1,0:T(2,128)S(1)}, u32[]{:S(2)}, u32[]{:S(2)}) collective-permute-start(f32[32,2,128]{2,1,0:T(2,128)S(1)} %slice_select_fusion), channel_id=1, source_target_pairs={{0,64},{8,72},{16,80},{24,88},{64,128},{72,136},{80,144},{88,152},... | collective-permute-start | bytes 98312 | tf_op jit(solution)/shard_map/ppermute | solution.py:353
  52.0 1.6 %collective-permute-done.2 = f32[32,2,128]{2,1,0:T(2,128)S(1)} collective-permute-done((f32[32,2,128]{2,1,0:T(2,128)S(1)}, f32[32,2,128]{2,1,0:T(2,128)S(1)}, u32[]{:S(2)}, u32[]{:S(2)}) %collective-permute-start.2) | collective-permute-done | bytes 32800 | tf_op jit(solution)/shard_map/ppermute | solution.py:353
  53.5 1.9 %coarse.1 = f32[8,8,128]{2,1,0:T(8,128)} custom-call(s32[3]{0:T(128)S(1)} %pad_add_fusion.ids, f32[128,128]{1,0:T(8,128)S(1)} %bitcast.17, f32[64,128]{1,0:T(8,128)S(1)} %bitcast.26, f32[8,8,128]{2,1,0:T(8,128)S(1)} %get-tuple-element.8.smoothed), custom_call_target="tpu_custom_call" | custom-call | flops 1000000 | bytes 200000 | tf_op jit(solution)/shard_map/coarse/pallas_call | solution.py:299
  (4 shorter events, 0.0 us)
Async XLA Ops:
  0.6 0.8 %copy-start = (f32[2,4,8,128]{3,2,1,0:T(8,128)S(1)}, f32[2,4,8,128]{3,2,1,0:T(8,128)}, u32[]{:S(2)}) copy-start(f32[2,4,8,128]{3,2,1,0:T(8,128)} %param.7) | copy-start | bytes 98308
  0.7 0.7 %copy-start.2 = (s32[1,1,8,256]{3,2,1,0:T(8,128)S(1)}, s32[1,1,8,256]{3,2,1,0:T(8,128)}, u32[]{:S(2)}) copy-start(s32[1,1,8,256]{3,2,1,0:T(8,128)} %param.11) | copy-start | bytes 24580
  0.8 0.7 %copy-start.4 = (s32[1,8,8]{2,1,0:T(8,128)S(1)}, s32[1,8,8]{2,1,0:T(8,128)}, u32[]{:S(2)}) copy-start(s32[1,8,8]{2,1,0:T(8,128)} %param.8) | copy-start | bytes 772
  1.4 0.8 %copy-start.1 = (f32[2,4,8,128]{3,2,1,0:T(8,128)S(1)}, f32[2,4,8,128]{3,2,1,0:T(8,128)}, u32[]{:S(2)}) copy-start(f32[2,4,8,128]{3,2,1,0:T(8,128)} %param.6) | copy-start | bytes 98308
  2.2 6.7 %copy-start.3 = (f32[3,1,1,8,256]{4,3,2,1,0:T(8,128)S(1)}, f32[3,1,1,8,256]{4,3,2,1,0:T(8,128)}, u32[]{:S(2)}) copy-start(f32[3,1,1,8,256]{4,3,2,1,0:T(8,128)} %param.10) | copy-start | bytes 73732
  3.1 5.8 %copy-start.5 = (s32[1,1,8,256]{3,2,1,0:T(8,128)S(1)}, s32[1,1,8,256]{3,2,1,0:T(8,128)}, u32[]{:S(2)}) copy-start(s32[1,1,8,256]{3,2,1,0:T(8,128)} %param.9) | copy-start | bytes 24580
  3.1 6.3 %collective-permute-start = (f32[4,8,128]{2,1,0:T(8,128)S(1)}, f32[4,8,128]{2,1,0:T(8,128)S(1)}, u32[]{:S(2)}, u32[]{:S(2)}) collective-permute-start(f32[4,8,128]{2,1,0:T(8,128)S(1)} %get-tuple-element.9), channel_id=1, source_target_pairs={{0,8},{8,0},{16,24},{24,16},{32,40},{40,32},{48,56},{56,48},{64,72... | collective-permute-start | bytes 49160 | tf_op jit(solution)/shard_map/ppermute | solution.py:327
  5.1 7.2 %collective-permute-start.1 = (f32[4,8,128]{2,1,0:T(8,128)S(1)}, f32[4,8,128]{2,1,0:T(8,128)S(1)}, u32[]{:S(2)}, u32[]{:S(2)}) collective-permute-start(f32[4,8,128]{2,1,0:T(8,128)S(1)} %get-tuple-element.10), channel_id=1, source_target_pairs={{8,16},{24,32},{40,48},{56,64},{72,80},{88,96},{104,112},{120,128}... | collective-permute-start | bytes 49160 | tf_op jit(solution)/shard_map/ppermute | solution.py:326
  30.8 14.8 %all-to-all-start.1 = ((f32[64,2,128]{2,1,0:T(2,128)}), f32[64,2,128]{2,1,0:T(2,128)S(1)}, u32[]{:S(2)}, u32[]{:S(2)}) async-start(f32[64,2,128]{2,1,0:T(2,128)} %get-tuple-element.12), calls=%async_computation.1 | async-start | bytes 131072 | tf_op jit(solution)/shard_map/all_to_all | solution.py:347
  45.6 7.9 %collective-permute-start.2 = (f32[32,2,128]{2,1,0:T(2,128)S(1)}, f32[32,2,128]{2,1,0:T(2,128)S(1)}, u32[]{:S(2)}, u32[]{:S(2)}) collective-permute-start(f32[32,2,128]{2,1,0:T(2,128)S(1)} %slice_select_fusion), channel_id=1, source_target_pairs={{0,64},{8,72},{16,80},{24,88},{64,128},{72,136},{80,144},{88,152},... | collective-permute-start | bytes 98312 | tf_op jit(solution)/shard_map/ppermute | solution.py:353

commit v2 on v1

v2 whole, which is shorter than its diff:
```python
import functools

import jax
import jax.numpy as jnp
from jax import lax
from jax.experimental import pallas as pl
from jax.experimental.pallas import tpu as pltpu
from jax.sharding import PartitionSpec as P

BLOCK = 128
ROW = 8
F32 = jnp.float32
BF16 = jnp.bfloat16
damping = 0.8
penalty_weight = 2.0
coarse_scale = 0.0625
stencil_weight_sum = 44.0 / 3.0
half_weight_sum = 22.0 / 3.0
MEMORY = 32 * 1024 * 1024


def iota(shape, axis):
    return lax.broadcasted_iota(jnp.int32, shape, axis)


def place():
    along = lax.axis_index("gx")
    return lax.axis_index("gy"), lax.rem(along, 2) == 0, lax.rem(along, ROW)


def parts(value, count):
    cuts = []
    for index in range(count):
        cut = value.astype(BF16)
        cuts.append(cut)
        if index + 1 < count:
            value = value - cut.astype(F32)
    return cuts


def one_hots(cells):
    rows = cells.shape[1]
    low = iota((128, rows), 0) == (cells & 127)
    return iota((64, rows), 0) == (cells >> 7), low.astype(F32).astype(BF16)


def contract_rows(left, right):
    return lax.dot_general(left, right, (((1,), (1,)), ((), ())), preferred_element_type=F32)


def front_kernel(
    counts_in, cells_in, cond_in, rhs_in, base_in, frac_in, smoothed, count, near, far, sent,
    marked, counts, cells, cond, rhs, base, frac, donors, sems,
):
    own, first, _ = place()
    pairs = (
        (counts_in, counts), (cells_in, cells), (cond_in, cond), (rhs_in, rhs), (base_in, base),
        (frac_in, frac),
    )
    copies = [
        pltpu.make_async_copy(source, target, sems.at[i]) for i, (source, target) in enumerate(pairs)
    ]
    for copy in copies:
        copy.start()
    copies[0].wait()
    copies[1].wait()
    lane = iota((1, 256), 1)
    total = jnp.zeros((64, 128), F32)
    for b in range(8):
        row = jnp.where(lane < counts[b, own] * BLOCK, cells[b : b + 1, :], -BLOCK)
        marked[b : b + 1, :] = row
        high, low = one_hots(row)
        total = total + contract_rows(high.astype(F32).astype(BF16), low)
    count[...] = total
    copies[2].wait()
    copies[3].wait()
    field = damping * rhs[...] / (stencil_weight_sum * cond[...] + penalty_weight * total)
    smoothed[...] = field
    for f, ref in ((0, smoothed), (16, cond)):
        for grid in range(2):
            low_x = ref[grid * 32 : grid * 32 + 8, :]
            high_x = ref[grid * 32 + 24 : grid * 32 + 32, :]
            at = slice(f + grid * 8, f + grid * 8 + 8)
            near[at, :] = jnp.where(first, high_x, low_x)
            far[at, :] = jnp.where(first, low_x, high_x)

    faces = [
        [ref[pl.ds(y, 8, stride=8), :] for ref in (smoothed, cond)] for y in (0, 7)
    ]
    for d in range(8):
        for f in range(2):
            sent[d, f * 8 : f * 8 + 8, :] = jnp.where(d > own, faces[1][f], faces[0][f])

    copies[4].wait()
    copies[5].wait()
    high = field.astype(BF16).astype(F32)
    stacked = jnp.concatenate([high, field - high, high], axis=0)
    columns = stacked.T.astype(BF16)
    q = base[...]
    grid = (q >= 2667).astype(jnp.int32)
    q = q - grid * 2667
    x = (q >= 889).astype(jnp.int32) + (q >= 1778).astype(jnp.int32)
    q = q - x * 889
    y = jnp.zeros_like(q)
    for step in range(1, 7):
        y = y + (q >= step * 127).astype(jnp.int32)
    z = q - y * 127
    plane = grid * 4 + x
    eight = iota((8, 256), 0)
    wide = iota((128, 256), 0)
    for d in range(8):
        row = slice(d, d + 1)
        frac_x, frac_y, frac_z = frac[0, row, :], frac[1, row, :], frac[2, row, :]
        at_x, at_y, at_z = plane[row], y[row], z[row]
        weight_x = jnp.where(eight == at_x, 1.0 - frac_x, jnp.where(eight == at_x + 1, frac_x, 0.0))
        weight_y = jnp.where(eight == at_y, 1.0 - frac_y, jnp.where(eight == at_y + 1, frac_y, 0.0))
        weight_z = jnp.where(wide == at_z, 1.0 - frac_z, jnp.where(wide == at_z + 1, frac_z, 0.0))
        weight = jnp.concatenate([weight_x[p : p + 1] * weight_y for p in range(8)], axis=0)
        upper, lower = parts(weight, 2)
        mixed = jnp.dot(
            columns, jnp.concatenate([upper, upper, lower], axis=0), preferred_element_type=F32
        )
        donors[row, :] = jnp.sum(mixed * weight_z, axis=0, keepdims=True)
    for d in range(8):
        sent[d, 16:17, :] = donors[d : d + 1, 0:128]
        sent[d, 17:18, :] = donors[d : d + 1, 128:256]


def neighbour_sums(fields, shift_y, shift_z):
    inner, outer = [], []
    for field in fields:
        beside_z = shift_z(field)
        beside_y = shift_y(field)
        both = shift_z(beside_y)
        inner.append(0.5 * (beside_z + beside_y) + 0.25 * both)
        outer.append(0.5 * field + 0.25 * (beside_z + beside_y) + (1.0 / 6.0) * both)
    return [inner[i] + outer[i - 1] + outer[i + 1] for i in range(1, len(fields) - 1)]


def residual_kernel(
    cells, arrived, smoothed, count, rhs, cond, far, near, partial, coarse, up, down
):
    own, first, _ = place()
    total = jnp.zeros((192, 128), F32)
    for b in range(8):
        high, low = one_hots(cells[b : b + 1, :])
        values = jnp.concatenate([arrived[b, 16:17, :], arrived[b, 17:18, :]], axis=1)
        left = jnp.concatenate(
            [jnp.where(high, cut.astype(F32), 0.0).astype(BF16) for cut in parts(values, 3)], axis=0
        )
        total = total + contract_rows(left, low)
    total = total[0:64] + total[64:128] + total[128:192]

    below = jnp.where(own > 0, arrived[jnp.maximum(own - 1, 0), 0:16, :], 0.0)
    above = jnp.where(own < 7, arrived[jnp.minimum(own + 1, 7), 0:16, :], 0.0)
    lanes = iota((8, 128), 1)
    rows = iota((8, 128), 0)
    keep_up = lanes < 127
    keep_down = lanes > 0

    def shift_z(value):
        return jnp.where(keep_down, pltpu.roll(value, 1, 1), 0.0) + jnp.where(
            keep_up, pltpu.roll(value, 127, 1), 0.0
        )

    def shift_y(value, lower, upper):
        down = jnp.where(rows > 0, pltpu.roll(value, 1, 0), lower)
        up = jnp.where(rows < 7, pltpu.roll(value, 7, 0), upper)
        return down + up

    pooled = []
    for grid in range(2):
        fields = []
        for f, ref in ((0, smoothed), (1, cond)):
            at = slice((2 * f + grid) * 8, (2 * f + grid) * 8 + 8)
            near_plane, far_plane = near[at, :], far[at, :]
            left = jnp.where(first, far_plane, near_plane)
            right = jnp.where(first, near_plane, far_plane)
            start = grid * 32
            planes = [left] + [ref[start + x * 8 : start + x * 8 + 8, :] for x in range(4)] + [right]
            at = 8 * f + grid * 4
            lower = [0.0] + [below[at + x : at + x + 1, :] for x in range(4)] + [0.0]
            upper = [0.0] + [above[at + x : at + x + 1, :] for x in range(4)] + [0.0]
            fields.append((planes, lower, upper))
        fields.append(tuple([v * c for v, c in zip(*pair)] for pair in zip(*fields)))
        sums = []
        for planes, lower, upper in fields:
            inner, outer = [], []
            for plane, low_row, high_row in zip(planes, lower, upper):
                beside_z = shift_z(plane)
                beside_y = shift_y(plane, low_row, high_row)
                both = shift_z(beside_y)
                edge = beside_z + beside_y
                inner.append(0.5 * edge + 0.25 * both)
                outer.append(0.5 * plane + 0.25 * edge + (1.0 / 6.0) * both)
            sums.append([inner[i] + outer[i - 1] + outer[i + 1] for i in range(1, 5)])
        summed = jnp.zeros((8, 128), F32)
        for x in range(4):
            at = slice(grid * 32 + x * 8, grid * 32 + x * 8 + 8)
            v, c = smoothed[at, :], cond[at, :]
            applied = v * (half_weight_sum * c + sums[1][x]) - c * sums[0][x] - sums[2][x]
            value = rhs[at, :] - applied - penalty_weight * (count[at, :] * v - total[at])
            partial[at, :] = value
            summed = summed + value
        pooled.append(summed)
    for grid in range(2):
        start = grid * 32
        pooled.append(sum(cond[start + x * 8 : start + x * 8 + 8, :] for x in range(4)))

    here = []
    there = []
    for f in range(2):
        here.append(
            jnp.concatenate(
                [
                    face[8 * f + 4 * grid + x : 8 * f + 4 * grid + x + 1, :]
                    for face in (below, above)
                    for x in (0, 3)
                    for grid in range(2)
                ],
                axis=0,
            )
        )
        corner = []
        for y in (0, 7):
            near_rows = near[pl.ds(16 * f + y, 2, stride=8), :]
            far_rows = far[pl.ds(16 * f + y, 2, stride=8), :]
            corner.append(jnp.where(first, far_rows, near_rows))
            corner.append(jnp.where(first, near_rows, far_rows))
        there.append(jnp.concatenate(corner, axis=0))

    def corner_sum(value):
        return 0.25 * value + (1.0 / 6.0) * shift_z(value)

    fix = (
        here[1] * corner_sum(there[0])
        + corner_sum(there[0] * there[1])
        - here[0] * corner_sum(there[1])
    )
    down[...] = fix[0:4]
    up[...] = fix[4:8]
    pooled.append(fix)
    pool = (iota((128, 128), 0) // 4 == iota((128, 128), 1) % 32).astype(F32)
    means = jnp.dot(
        jnp.concatenate(pooled, axis=0),
        pool,
        preferred_element_type=F32,
        precision=lax.Precision.HIGHEST,
    ) * (1.0 / 64.0)
    own_part = iota((16, 128), 0) // 4 == iota((16, 128), 1) // 32
    lines = [
        jnp.sum(jnp.where(own_part, means[f * 16 : f * 16 + 16], 0.0), axis=0, keepdims=True)
        for f in range(2)
    ]
    fix_part = (rows % 2) * 2 + 1 - rows // 4 == lanes // 32
    lines.append(jnp.sum(jnp.where(fix_part, means[32:40], 0.0), axis=0, keepdims=True))
    lines.append(jnp.zeros((1, 128), F32))
    coarse[...] = jnp.broadcast_to(jnp.concatenate(lines, axis=0)[None], (64, 4, 128))


def fix_kernel(partial, up, down, residual):
    rows = iota((8, 128), 0)
    for grid in range(2):
        for x in range(4):
            at = slice(grid * 32 + x * 8, grid * 32 + x * 8 + 8)
            value = partial[at, :]
            if x in (0, 3):
                row = (x // 3) * 2 + grid
                value = value + jnp.where(
                    rows == 0,
                    up[row : row + 1, :],
                    jnp.where(rows == 7, down[row : row + 1, :], 0.0),
                )
            residual[at, :] = value


def coarse_kernel(gathered, extra, smoothed, pressure):
    own, _, column = place()
    lanes = iota((8, 128), 1)
    rows = iota((8, 128), 0)
    low_z = lanes % 32 > 0
    high_z = lanes % 32 < 31
    first_y = lanes % 64 < 32

    def shift_z(value):
        return jnp.where(low_z, pltpu.roll(value, 1, 1), 0.0) + jnp.where(
            high_z, pltpu.roll(value, 127, 1), 0.0
        )

    def shift_y(value):
        ahead = pltpu.roll(value, 96, 1)
        behind = pltpu.roll(value, 32, 1)
        within = jnp.where(first_y, ahead, behind)
        from_below = jnp.where(rows > 0, pltpu.roll(ahead, 1, 0), 0.0)
        from_above = jnp.where(rows < 7, pltpu.roll(behind, 7, 0), 0.0)
        return within + jnp.where(first_y, from_below, from_above)

    rhs, cond = [], []
    for slot in range(7):
        at = column + slot - 3
        inside = jnp.logical_and(at >= 0, at < ROW)
        here = pl.multiple_of(jnp.clip(at, 0, ROW - 1) * 32, 32)
        there = pl.multiple_of((at & 3) * 32, 32)
        lines = [
            jnp.where(
                inside,
                gathered[pl.ds(here + f, 8, stride=4), :],
                extra[pl.ds(there + f, 8, stride=4), :],
            )
            for f in range(3)
        ]
        from_below = jnp.where(rows > 0, pltpu.roll(lines[2], 1, 0), 0.0)
        from_above = jnp.where(rows < 7, pltpu.roll(lines[2], 7, 0), 0.0)
        rhs.append(lines[0] + jnp.where(first_y, from_below, from_above))
        cond.append(lines[1])
    scale = [
        jnp.where(c > 0.0, damping / (stencil_weight_sum * coarse_scale * jnp.where(c > 0.0, c, 1.0)), 0.0)
        for c in cond
    ]
    value = [r * s for r, s in zip(rhs, scale)]
    own_sum = [
        half_weight_sum * c + s for c, s in zip(cond[1:-1], neighbour_sums(cond, shift_y, shift_z))
    ]
    for sweep in range(3):
        around = neighbour_sums(value, shift_y, shift_z)
        around_both = neighbour_sums(
            [v * c for v, c in zip(value, cond)], shift_y, shift_z
        )
        value, cond, rhs, scale = value[1:-1], cond[1:-1], rhs[1:-1], scale[1:-1]
        value = [
            v + s * (r - coarse_scale * (v * o - c * a - b))
            for v, s, r, o, c, a, b in zip(value, scale, rhs, own_sum, cond, around, around_both)
        ]
        own_sum = own_sum[1:-1]
    mine = jnp.sum(jnp.where(rows == own, value[0], 0.0), axis=0, keepdims=True)
    spread = jnp.where(iota((16, 128), 0) // 4 == iota((16, 128), 1) // 32, mine, 0.0)
    expand = (iota((128, 128), 0) % 32 == iota((128, 128), 1) // 4).astype(F32)
    fine = jnp.dot(spread, expand, preferred_element_type=F32, precision=lax.Precision.HIGHEST)
    for grid in range(2):
        for x in range(4):
            at = slice(grid * 32 + x * 8, grid * 32 + x * 8 + 8)
            pressure[at, :] = smoothed[at, :] + fine[grid * 8 : grid * 8 + 8]


def call(kernel, name, outs, operands, spaces, scratch=()):
    return pl.pallas_call(
        kernel,
        out_shape=[
            jax.ShapeDtypeStruct(*(out if isinstance(out[0], tuple) else (out, F32))) for out in outs
        ],
        in_specs=[pl.BlockSpec(memory_space=space) for space in spaces],
        out_specs=[pl.BlockSpec(memory_space=pltpu.VMEM)] * len(outs),
        scratch_shapes=scratch,
        compiler_params=pltpu.CompilerParams(vmem_limit_bytes=MEMORY),
        cost_estimate=pl.CostEstimate(flops=1000000, bytes_accessed=200000, transcendentals=0),
        name=name,
    )(*operands)


def local(pressure_rhs, conductivity, block_counts, donor_base, donor_frac, receptor_cells):
    shape = pressure_rhs.shape
    along = lax.axis_index("gx")
    size = lax.axis_size("gx")
    rhs = pressure_rhs.reshape(64, 128)
    cond = conductivity.reshape(64, 128)
    counts = block_counts[0]
    cells = receptor_cells[0, 0]
    base = donor_base[0, 0]
    frac = donor_frac[:, 0, 0]
    vector, far_memory = pltpu.VMEM, pltpu.HBM
    whole = (64, 128)
    smoothed, count, near, far, sent, marked = call(
        front_kernel, "front",
        [whole, whole, (32, 128), (32, 128), (8, 24, 128), ((8, 256), jnp.int32)],
        tuple(
            pltpu.with_memory_space_constraint(value, far_memory)
            for value in (counts, cells, cond, rhs, base, frac)
        ),
        [far_memory] * 6,
        [
            pltpu.SMEM((8, 8), jnp.int32),
            pltpu.VMEM((8, 256), jnp.int32),
            pltpu.VMEM(whole, F32),
            pltpu.VMEM(whole, F32),
            pltpu.VMEM((8, 256), jnp.int32),
            pltpu.VMEM((3, 8, 256), F32),
            pltpu.VMEM((8, 256), F32),
            pltpu.SemaphoreType.DMA((6,)),
        ],
    )
    arrived = lax.all_to_all(sent, "gy", split_axis=0, concat_axis=0, tiled=True)
    beyond = [(i, i + 1) for i in range(1, size - 1, 2)]
    far_in = lax.ppermute(far, "gx", beyond + [(j, i) for i, j in beyond])
    near_in = lax.ppermute(near, "gx", [(i, i ^ 1) for i in range(size)])
    partial, coarse, up, down = call(
        residual_kernel, "residual", [whole, (64, 4, 128), (4, 128), (4, 128)],
        (marked, arrived, smoothed, count, rhs, cond, far_in, near_in),
        [vector] * 8,
    )
    groups = [
        [(start + i) * 8 + j for i in range(ROW) for j in range(8)]
        for start in range(0, size, ROW)
    ]
    gathered = lax.all_to_all(
        coarse, ("gx", "gy"), split_axis=0, concat_axis=0, tiled=True, axis_index_groups=groups
    )
    ahead = [(i, i + 1) for i in range(lax.axis_size("gy") - 1)]
    from_below = lax.ppermute(up, "gy", ahead)
    from_above = lax.ppermute(down, "gy", [(j, i) for i, j in ahead])
    gathered, from_below, from_above = lax.optimization_barrier(
        (gathered, from_below, from_above)
    )
    passed = jnp.where(along % ROW < ROW // 2, gathered[32:], gathered[:32])
    step = [(i, i + ROW) if i % ROW < ROW // 2 else (i, i - ROW) for i in range(size)]
    extra = lax.ppermute(passed, "gx", [(i, j) for i, j in step if 0 <= j < size])
    (residual,) = call(
        fix_kernel, "fix", [whole], (partial, from_below, from_above), [vector] * 3
    )
    (pressure,) = call(
        coarse_kernel, "coarse", [whole],
        (gathered.reshape(256, 128), extra.reshape(128, 128), smoothed), [vector] * 3,
    )
    return pressure.reshape(shape), residual.reshape(shape)


def solution(mesh):
    return jax.shard_map(
        local,
        mesh=mesh,
        in_specs=(
            P(None, "gx", "gy", None),
            P(None, "gx", "gy", None),
            P("gx", None, None),
            P("gx", "gy", None, None),
            P(None, "gx", "gy", None, None),
            P("gx", "gy", None, None),
        ),
        out_specs=(P(None, "gx", "gy", None), P(None, "gx", "gy", None)),
        check_vma=False,
    )
```

time: 55.8 us -> 50.6 us (0.907)
  the two profiles are of different devices: /device:TPU:192 before, /device:TPU:222 now
where the time goes in v2:
time: 50.6 us; the launch traced here: 50.1 us
  starting transfers between devices  33.3 us (66%)
  waiting for transfers between devices  10.4 us (21%)
  Pallas kernels  5.68 us (11%)
  between operations  0.75 us (1%)
    all_to_all x1, starting transfers between devices, local(): lax.all_to_all(coarse, ('gx', 'gy'), split_axis=0, concat_axis=0, tiled=T...  10.1 us
    all_to_all x1, starting transfers between devices, local(): lax.all_to_all(sent, 'gy', split_axis=0, concat_axis=0, tiled=True)  7.33 us
    pallas_call x4, Pallas kernels, call(): pl.pallas_call(kernel, out_shape=[jax.ShapeDtypeStruct(*(out if isinstanc...  5.68 us
    ppermute x1, starting transfers between devices, local(): near_in = lax.ppermute(near, 'gx', [(i, i ^ 1) for i in range(size)])  5.51 us
    ppermute x1, waiting for transfers between devices, local(): lax.ppermute(passed, 'gx', [(i, j) for i, j in step if 0 <= j < size])  4.82 us
    ppermute x1, waiting for transfers between devices, local(): from_above = lax.ppermute(down, 'gy', [(j, i) for i, j in ahead])  4.73 us
    ppermute x1, starting transfers between devices, local(): from_below = lax.ppermute(up, 'gy', ahead)  4.59 us
    ppermute x1, starting transfers between devices, local(): lax.ppermute(passed, 'gx', [(i, j) for i, j in step if 0 <= j < size])  1.92 us
  transfers between devices with their start and end apart: 7, of which 3 were waited for; matrix products, arithmetic and copies ran while one was open for 0% of the time, Pallas kernels for 1%

profile of v2, /device:TPU:222, one launch (start us, length us, event | category | flops | bytes accessed | tf_op | source)
XLA Modules:
  0.0 50.1 jit_solution(9726040310700289659)
XLA Ops:
  0.6 2.4 %front.1 = (f32[64,128]{1,0:T(8,128)S(1)}, f32[64,128]{1,0:T(8,128)S(1)}, f32[32,128]{1,0:T(8,128)S(1)}, f32[32,128]{1,0:T(8,128)S(1)}, f32[8,24,128]{2,1,0:T(8,128)}, /*index=5*/s32[8,256]{1,0:T(8,128)S(1)}) custom-call(s32[8,8]{1,0:T(8,128)} %bitcast.21, s32[8,256]{1,0:T(8,128)} %bitcast.19, f32[64,128]{1,0:T(8,128)} %bitcast.11, f32[64,128]{1,0:T(8,128)} %bitcast.13, ...), custom_call_target="tpu_custom_call" | custom-call | flops 1000000 | bytes 200000 | tf_op jit(solution)/shard_map/front/pallas_call | solution.py:346
  3.0 0.0 copy-start
  3.1 0.0 copy-start.1
  3.1 7.3 %all-to-all-start = ((f32[8,24,128]{2,1,0:T(8,128)}), f32[8,24,128]{2,1,0:T(8,128)S(1)}, u32[]{:S(2)}, u32[]{:S(2)}) async-start(f32[8,24,128]{2,1,0:T(8,128)} %get-tuple-element.16), calls=%async_computation | async-start | bytes 196608 | tf_op jit(solution)/shard_map/all_to_all | solution.py:391
  10.4 1.9 %collective-permute-start = (f32[32,128]{1,0:T(8,128)S(1)}, f32[32,128]{1,0:T(8,128)S(1)}, u32[]{:S(2)}, u32[]{:S(2)}) collective-permute-start(f32[32,128]{1,0:T(8,128)S(1)} %get-tuple-element.19), channel_id=1, source_target_pairs={{8,16},{24,32},{40,48},{56,64},{72,80},{88,96},{104,112},{120,128}... | collective-permute-start | bytes 49160 | tf_op jit(solution)/shard_map/ppermute | solution.py:393
  12.3 5.5 %collective-permute-start.1 = (f32[32,128]{1,0:T(8,128)S(1)}, f32[32,128]{1,0:T(8,128)S(1)}, u32[]{:S(2)}, u32[]{:S(2)}) collective-permute-start(f32[32,128]{1,0:T(8,128)S(1)} %get-tuple-element.20), channel_id=1, source_target_pairs={{0,8},{8,0},{16,24},{24,16},{32,40},{40,32},{48,56},{56,48},{64,72... | collective-permute-start | bytes 49160 | tf_op jit(solution)/shard_map/ppermute | solution.py:394
  17.8 0.0 collective-permute-done.far
  17.8 0.8 %collective-permute-done.1.near = f32[32,128]{1,0:T(8,128)S(1)} collective-permute-done((f32[32,128]{1,0:T(8,128)S(1)}, f32[32,128]{1,0:T(8,128)S(1)}, u32[]{:S(2)}, u32[]{:S(2)}) %collective-permute-start.1) | collective-permute-done | bytes 16416 | tf_op jit(solution)/shard_map/ppermute | solution.py:394
  18.7 0.0 all-to-all-done.arrived
  18.7 0.0 copy-done
  18.7 0.0 copy-done.1
  18.7 1.3 %residual.1 = (f32[64,128]{1,0:T(8,128)S(1)}, f32[64,4,128]{2,1,0:T(4,128)}, f32[4,128]{1,0:T(4,128)S(1)}, f32[4,128]{1,0:T(4,128)S(1)}) custom-call(s32[8,256]{1,0:T(8,128)S(1)} %get-tuple-element.15.cells, f32[8,24,128]{2,1,0:T(8,128)S(1)} %all-to-all-done.arrived, f32[64,128]{1,0:T(8,128)S(1)} %get-tuple-element.17.smoothed, ...), custom_call_target="tpu_custom_call" | custom-call | flops 1000000 | bytes 200000 | tf_op jit(solution)/shard_map/residual/pallas_call | solution.py:346
  20.0 10.1 %all-to-all-start.1 = ((f32[64,4,128]{2,1,0:T(4,128)}), f32[64,4,128]{2,1,0:T(4,128)S(1)}, u32[]{:S(2)}, u32[]{:S(2)}) async-start(f32[64,4,128]{2,1,0:T(4,128)} %get-tuple-element.21), calls=%async_computation.1 | async-start | bytes 262144 | tf_op jit(solution)/shard_map/all_to_all | solution.py:404
  30.1 4.6 %collective-permute-start.2 = (f32[4,128]{1,0:T(4,128)S(1)}, f32[4,128]{1,0:T(4,128)S(1)}, u32[]{:S(2)}, u32[]{:S(2)}) collective-permute-start(f32[4,128]{1,0:T(4,128)S(1)} %get-tuple-element.22), channel_id=1, source_target_pairs={{0,1},{1,2},{2,3},{3,4},{4,5},{5,6},{6,7},{8,9},{9,10},{10,11},{11... | collective-permute-start | bytes 6152 | tf_op jit(solution)/shard_map/ppermute | solution.py:408
  34.7 1.9 %collective-permute-start.3 = (f32[4,128]{1,0:T(4,128)S(1)}, f32[4,128]{1,0:T(4,128)S(1)}, u32[]{:S(2)}, u32[]{:S(2)}) collective-permute-start(f32[4,128]{1,0:T(4,128)S(1)} %get-tuple-element.23), channel_id=1, source_target_pairs={{1,0},{2,1},{3,2},{4,3},{5,4},{6,5},{7,6},{9,8},{10,9},{11,10},{12... | collective-permute-start | bytes 6152 | tf_op jit(solution)/shard_map/ppermute | solution.py:409
  36.6 0.0 collective-permute-done.2.up
  36.7 4.7 %collective-permute-done.3.down = f32[4,128]{1,0:T(4,128)S(1)} collective-permute-done((f32[4,128]{1,0:T(4,128)S(1)}, f32[4,128]{1,0:T(4,128)S(1)}, u32[]{:S(2)}, u32[]{:S(2)}) %collective-permute-start.3) | collective-permute-done | bytes 2080 | tf_op jit(solution)/shard_map/ppermute | solution.py:409
  41.4 0.0 all-to-all-done.1
  41.4 1.9 %collective-permute-start.4 = (f32[32,4,128]{2,1,0:T(4,128)S(1)}, f32[32,4,128]{2,1,0:T(4,128)S(1)}, u32[]{:S(2)}, u32[]{:S(2)}) collective-permute-start(f32[32,4,128]{2,1,0:T(4,128)S(1)} %slice_select_fusion), channel_id=1, source_target_pairs={{0,64},{8,72},{16,80},{24,88},{64,128},{72,136},{80,144},{88,152},... | collective-permute-start | bytes 196616 | tf_op jit(solution)/shard_map/ppermute | solution.py:415
  43.3 0.6 %fix.1 = f32[64,128]{1,0:T(8,128)} custom-call(f32[64,128]{1,0:T(8,128)S(1)} %get-tuple-element.25.partial, f32[4,128]{1,0:T(4,128)S(1)} %collective-permute-done.2.up, f32[4,128]{1,0:T(4,128)S(1)} %collective-permute-done.3.down), custom_call_target="tpu_custom_call" | custom-call | flops 1000000 | bytes 200000 | tf_op jit(solution)/shard_map/fix/pallas_call | solution.py:346
  44.0 4.8 %collective-permute-done.4 = f32[32,4,128]{2,1,0:T(4,128)S(1)} collective-permute-done((f32[32,4,128]{2,1,0:T(4,128)S(1)}, f32[32,4,128]{2,1,0:T(4,128)S(1)}, u32[]{:S(2)}, u32[]{:S(2)}) %collective-permute-start.4) | collective-permute-done | bytes 65568 | tf_op jit(solution)/shard_map/ppermute | solution.py:415
  48.8 1.3 %coarse.1 = f32[64,128]{1,0:T(8,128)} custom-call(f32[256,128]{1,0:T(8,128)S(1)} %bitcast.10, f32[128,128]{1,0:T(8,128)S(1)} %bitcast.15, f32[64,128]{1,0:T(8,128)S(1)} %get-tuple-element.17.smoothed), custom_call_target="tpu_custom_call" | custom-call | flops 1000000 | bytes 200000 | tf_op jit(solution)/shard_map/coarse/pallas_call | solution.py:346
  (1 shorter events, 0.0 us)
Async XLA Ops:
  3.0 15.6 %copy-start = (f32[2,4,8,128]{3,2,1,0:T(8,128)S(1)}, f32[2,4,8,128]{3,2,1,0:T(8,128)}, u32[]{:S(2)}) copy-start(f32[2,4,8,128]{3,2,1,0:T(8,128)} %param.7) | copy-start | bytes 98308
  3.1 15.6 %copy-start.1 = (f32[2,4,8,128]{3,2,1,0:T(8,128)S(1)}, f32[2,4,8,128]{3,2,1,0:T(8,128)}, u32[]{:S(2)}) copy-start(f32[2,4,8,128]{3,2,1,0:T(8,128)} %param.6) | copy-start | bytes 98308
  3.1 15.6 %all-to-all-start = ((f32[8,24,128]{2,1,0:T(8,128)}), f32[8,24,128]{2,1,0:T(8,128)S(1)}, u32[]{:S(2)}, u32[]{:S(2)}) async-start(f32[8,24,128]{2,1,0:T(8,128)} %get-tuple-element.16), calls=%async_computation | async-start | bytes 196608 | tf_op jit(solution)/shard_map/all_to_all | solution.py:391
  10.4 7.4 %collective-permute-start = (f32[32,128]{1,0:T(8,128)S(1)}, f32[32,128]{1,0:T(8,128)S(1)}, u32[]{:S(2)}, u32[]{:S(2)}) collective-permute-start(f32[32,128]{1,0:T(8,128)S(1)} %get-tuple-element.19), channel_id=1, source_target_pairs={{8,16},{24,32},{40,48},{56,64},{72,80},{88,96},{104,112},{120,128}... | collective-permute-start | bytes 49160 | tf_op jit(solution)/shard_map/ppermute | solution.py:393
  12.3 6.3 %collective-permute-start.1 = (f32[32,128]{1,0:T(8,128)S(1)}, f32[32,128]{1,0:T(8,128)S(1)}, u32[]{:S(2)}, u32[]{:S(2)}) collective-permute-start(f32[32,128]{1,0:T(8,128)S(1)} %get-tuple-element.20), channel_id=1, source_target_pairs={{0,8},{8,0},{16,24},{24,16},{32,40},{40,32},{48,56},{56,48},{64,72... | collective-permute-start | bytes 49160 | tf_op jit(solution)/shard_map/ppermute | solution.py:394
  20.0 21.4 %all-to-all-start.1 = ((f32[64,4,128]{2,1,0:T(4,128)}), f32[64,4,128]{2,1,0:T(4,128)S(1)}, u32[]{:S(2)}, u32[]{:S(2)}) async-start(f32[64,4,128]{2,1,0:T(4,128)} %get-tuple-element.21), calls=%async_computation.1 | async-start | bytes 262144 | tf_op jit(solution)/shard_map/all_to_all | solution.py:404
  30.1 6.5 %collective-permute-start.2 = (f32[4,128]{1,0:T(4,128)S(1)}, f32[4,128]{1,0:T(4,128)S(1)}, u32[]{:S(2)}, u32[]{:S(2)}) collective-permute-start(f32[4,128]{1,0:T(4,128)S(1)} %get-tuple-element.22), channel_id=1, source_target_pairs={{0,1},{1,2},{2,3},{3,4},{4,5},{5,6},{6,7},{8,9},{9,10},{10,11},{11... | collective-permute-start | bytes 6152 | tf_op jit(solution)/shard_map/ppermute | solution.py:408
  34.7 6.7 %collective-permute-start.3 = (f32[4,128]{1,0:T(4,128)S(1)}, f32[4,128]{1,0:T(4,128)S(1)}, u32[]{:S(2)}, u32[]{:S(2)}) collective-permute-start(f32[4,128]{1,0:T(4,128)S(1)} %get-tuple-element.23), channel_id=1, source_target_pairs={{1,0},{2,1},{3,2},{4,3},{5,4},{6,5},{7,6},{9,8},{10,9},{11,10},{12... | collective-permute-start | bytes 6152 | tf_op jit(solution)/shard_map/ppermute | solution.py:409
  41.4 7.4 %collective-permute-start.4 = (f32[32,4,128]{2,1,0:T(4,128)S(1)}, f32[32,4,128]{2,1,0:T(4,128)S(1)}, u32[]{:S(2)}, u32[]{:S(2)}) collective-permute-start(f32[32,4,128]{2,1,0:T(4,128)S(1)} %slice_select_fusion), channel_id=1, source_target_pairs={{0,64},{8,72},{16,80},{24,88},{64,128},{72,136},{80,144},{88,152},... | collective-permute-start | bytes 196616 | tf_op jit(solution)/shard_map/ppermute | solution.py:415

commit v3 on v2

--- a/solution.py
+++ b/solution.py
@@ -9,6 +9,9 @@
 
 BLOCK = 128
 ROW = 8
+TURN = 3
+LATER = 4
+SIDE = 4
 F32 = jnp.float32
 BF16 = jnp.bfloat16
 damping = 0.8
@@ -89,7 +92,7 @@
     ]
     for d in range(8):
         for f in range(2):
-            sent[d, f * 8 : f * 8 + 8, :] = jnp.where(d > own, faces[1][f], faces[0][f])
+            sent[(d - TURN) % 8, f * 8 : f * 8 + 8, :] = jnp.where(d > own, faces[1][f], faces[0][f])
 
     copies[4].wait()
     copies[5].wait()
@@ -122,8 +125,8 @@
         )
         donors[row, :] = jnp.sum(mixed * weight_z, axis=0, keepdims=True)
     for d in range(8):
-        sent[d, 16:17, :] = donors[d : d + 1, 0:128]
-        sent[d, 17:18, :] = donors[d : d + 1, 128:256]
+        sent[(d - TURN) % 8, 16:17, :] = donors[d : d + 1, 0:128]
+        sent[(d - TURN) % 8, 17:18, :] = donors[d : d + 1, 128:256]
 
 
 def neighbour_sums(fields, shift_y, shift_z):
@@ -138,21 +141,21 @@
 
 
 def residual_kernel(
-    cells, arrived, smoothed, count, rhs, cond, far, near, partial, coarse, up, down
+    cells, arrived, smoothed, count, rhs, cond, far, near, partial, coarse
 ):
     own, first, _ = place()
     total = jnp.zeros((192, 128), F32)
     for b in range(8):
         high, low = one_hots(cells[b : b + 1, :])
-        values = jnp.concatenate([arrived[b, 16:17, :], arrived[b, 17:18, :]], axis=1)
+        values = jnp.concatenate([arrived[(b - TURN) % 8, 16:17, :], arrived[(b - TURN) % 8, 17:18, :]], axis=1)
         left = jnp.concatenate(
             [jnp.where(high, cut.astype(F32), 0.0).astype(BF16) for cut in parts(values, 3)], axis=0
         )
         total = total + contract_rows(left, low)
     total = total[0:64] + total[64:128] + total[128:192]
 
-    below = jnp.where(own > 0, arrived[jnp.maximum(own - 1, 0), 0:16, :], 0.0)
-    above = jnp.where(own < 7, arrived[jnp.minimum(own + 1, 7), 0:16, :], 0.0)
+    below = jnp.where(own > 0, arrived[(own + 7 - TURN) & 7, 0:16, :], 0.0)
+    above = jnp.where(own < 7, arrived[(own + 9 - TURN) & 7, 0:16, :], 0.0)
     lanes = iota((8, 128), 1)
     rows = iota((8, 128), 0)
     keep_up = lanes < 127
@@ -237,8 +240,6 @@
         + corner_sum(there[0] * there[1])
         - here[0] * corner_sum(there[1])
     )
-    down[...] = fix[0:4]
-    up[...] = fix[4:8]
     pooled.append(fix)
     pool = (iota((128, 128), 0) // 4 == iota((128, 128), 1) % 32).astype(F32)
     means = jnp.dot(
@@ -254,11 +255,37 @@
     ]
     fix_part = (rows % 2) * 2 + 1 - rows // 4 == lanes // 32
     lines.append(jnp.sum(jnp.where(fix_part, means[32:40], 0.0), axis=0, keepdims=True))
-    lines.append(jnp.zeros((1, 128), F32))
-    coarse[...] = jnp.broadcast_to(jnp.concatenate(lines, axis=0)[None], (64, 4, 128))
-
-
-def fix_kernel(partial, up, down, residual):
+    tiles = []
+    for j in range(8):
+        above = (j + LATER) % 8 > own
+        tiles += lines + [jnp.where(above, fix[4:8], fix[0:4])]
+    coarse[...] = jnp.concatenate(tiles, axis=0)
+
+
+def merge_kernel(lines, column):
+    lanes = iota((8, 128), 1)
+    rows = (iota((8, 128), 0) + LATER) & 7
+    rhs, cond, corner = [lines[pl.ds(f, 8, stride=7), :] for f in range(3)]
+    from_below = jnp.where(rows > 0, pltpu.roll(corner, 1, 0), 0.0)
+    from_above = jnp.where(rows < 7, pltpu.roll(corner, 7, 0), 0.0)
+    rhs = rhs + jnp.where(lanes % 64 < 32, from_below, from_above)
+    for i in range(ROW):
+        column[i * 16 : i * 16 + 8, :] = rhs
+        column[i * 16 + 8 : i * 16 + 16, :] = cond
+
+
+def pass_kernel(gathered, lines, passed, edges):
+    own, _, column = place()
+    upper = gathered[pl.ds(((4 - SIDE) & 7) * 16, 64), :]
+    lower = gathered[pl.ds(((0 - SIDE) & 7) * 16, 64), :]
+    passed[...] = jnp.where(column < ROW // 2, upper, lower)
+    below = lines[pl.ds(((own + 7 - LATER) & 7) * 7 + 3, 4), :]
+    above = lines[pl.ds(((own + 9 - LATER) & 7) * 7 + 3, 4), :]
+    edges[0:4, :] = jnp.where(own > 0, below, 0.0)
+    edges[4:8, :] = jnp.where(own < 7, above, 0.0)
+
+
+def fix_kernel(edges, partial, residual):
     rows = iota((8, 128), 0)
     for grid in range(2):
         for x in range(4):
@@ -268,8 +295,8 @@
                 row = (x // 3) * 2 + grid
                 value = value + jnp.where(
                     rows == 0,
-                    up[row : row + 1, :],
-                    jnp.where(rows == 7, down[row : row + 1, :], 0.0),
+                    edges[row : row + 1, :],
+                    jnp.where(rows == 7, edges[4 + row : 5 + row, :], 0.0),
                 )
             residual[at, :] = value
 
@@ -277,7 +304,7 @@
 def coarse_kernel(gathered, extra, smoothed, pressure):
     own, _, column = place()
     lanes = iota((8, 128), 1)
-    rows = iota((8, 128), 0)
+    rows = (iota((8, 128), 0) + LATER) & 7
     low_z = lanes % 32 > 0
     high_z = lanes % 32 < 31
     first_y = lanes % 64 < 32
@@ -299,20 +326,12 @@
     for slot in range(7):
         at = column + slot - 3
         inside = jnp.logical_and(at >= 0, at < ROW)
-        here = pl.multiple_of(jnp.clip(at, 0, ROW - 1) * 32, 32)
-        there = pl.multiple_of((at & 3) * 32, 32)
-        lines = [
-            jnp.where(
-                inside,
-                gathered[pl.ds(here + f, 8, stride=4), :],
-                extra[pl.ds(there + f, 8, stride=4), :],
+        here = pl.multiple_of(((jnp.clip(at, 0, ROW - 1) - SIDE) & 7) * 16, 16)
+        there = pl.multiple_of((at & 3) * 16, 16)
+        for f, out in ((0, rhs), (8, cond)):
+            out.append(
+                jnp.where(inside, gathered[pl.ds(here + f, 8), :], extra[pl.ds(there + f, 8), :])
             )
-            for f in range(3)
-        ]
-        from_below = jnp.where(rows > 0, pltpu.roll(lines[2], 1, 0), 0.0)
-        from_above = jnp.where(rows < 7, pltpu.roll(lines[2], 7, 0), 0.0)
-        rhs.append(lines[0] + jnp.where(first_y, from_below, from_above))
-        cond.append(lines[1])
     scale = [
         jnp.where(c > 0.0, damping / (stencil_weight_sum * coarse_scale * jnp.where(c > 0.0, c, 1.0)), 0.0)
         for c in cond
@@ -359,7 +378,6 @@
 
 def local(pressure_rhs, conductivity, block_counts, donor_base, donor_frac, receptor_cells):
     shape = pressure_rhs.shape
-    along = lax.axis_index("gx")
     size = lax.axis_size("gx")
     rhs = pressure_rhs.reshape(64, 128)
     cond = conductivity.reshape(64, 128)
@@ -388,37 +406,41 @@
             pltpu.SemaphoreType.DMA((6,)),
         ],
     )
-    arrived = lax.all_to_all(sent, "gy", split_axis=0, concat_axis=0, tiled=True)
+    turned = [[(i + TURN) % 8 for i in range(8)]]
+    arrived = lax.all_to_all(
+        sent, "gy", split_axis=0, concat_axis=0, tiled=True,
+        axis_index_groups=turned,
+    )
     beyond = [(i, i + 1) for i in range(1, size - 1, 2)]
     far_in = lax.ppermute(far, "gx", beyond + [(j, i) for i, j in beyond])
     near_in = lax.ppermute(near, "gx", [(i, i ^ 1) for i in range(size)])
-    partial, coarse, up, down = call(
-        residual_kernel, "residual", [whole, (64, 4, 128), (4, 128), (4, 128)],
+    partial, coarse = call(
+        residual_kernel, "residual", [whole, (56, 128)],
         (marked, arrived, smoothed, count, rhs, cond, far_in, near_in),
         [vector] * 8,
     )
-    groups = [
-        [(start + i) * 8 + j for i in range(ROW) for j in range(8)]
-        for start in range(0, size, ROW)
-    ]
+    lines = lax.all_to_all(
+        coarse.reshape(56, 1, 128), "gy", split_axis=0, concat_axis=0, tiled=True,
+        axis_index_groups=[[(i + LATER) % 8 for i in range(8)]],
+    ).reshape(56, 128)
+    (column,) = call(merge_kernel, "merge", [(128, 128)], (lines,), [vector])
     gathered = lax.all_to_all(
-        coarse, ("gx", "gy"), split_axis=0, concat_axis=0, tiled=True, axis_index_groups=groups
-    )
-    ahead = [(i, i + 1) for i in range(lax.axis_size("gy") - 1)]
-    from_below = lax.ppermute(up, "gy", ahead)
-    from_above = lax.ppermute(down, "gy", [(j, i) for i, j in ahead])
-    gathered, from_below, from_above = lax.optimization_barrier(
-        (gathered, from_below, from_above)
-    )
-    passed = jnp.where(along % ROW < ROW // 2, gathered[32:], gathered[:32])
+        column, "gx", split_axis=0, concat_axis=0, tiled=True,
+        axis_index_groups=[
+            [start + (i + SIDE) % ROW for i in range(ROW)] for start in range(0, size, ROW)
+        ],
+    )
+    passed, edges = call(
+        pass_kernel, "pass", [(64, 128), (8, 128)], (gathered, lines), [vector] * 2
+    )
     step = [(i, i + ROW) if i % ROW < ROW // 2 else (i, i - ROW) for i in range(size)]
     extra = lax.ppermute(passed, "gx", [(i, j) for i, j in step if 0 <= j < size])
     (residual,) = call(
-        fix_kernel, "fix", [whole], (partial, from_below, from_above), [vector] * 3
+        fix_kernel, "fix", [whole], (edges, partial), [vector] * 2
     )
     (pressure,) = call(
         coarse_kernel, "coarse", [whole],
-        (gathered.reshape(256, 128), extra.reshape(128, 128), smoothed), [vector] * 3,
+        (gathered, extra, smoothed), [vector] * 3,
     )
     return pressure.reshape(shape), residual.reshape(shape)
 

time: 50.6 us -> 47.7 us (0.943)
  the two profiles are of different devices: /device:TPU:222 before, /device:TPU:4 now
where the time goes in v3:
time: 47.7 us; the launch traced here: 47.3 us
  blocking collectives  22.4 us (47%)
  starting transfers between devices  14.4 us (30%)
  Pallas kernels  5.04 us (11%)
  waiting for transfers between devices  4.7 us (10%)
  between operations  0.7 us (1%)
    all_to_all x1, blocking collectives, local(): lax.all_to_all(column, 'gx', split_axis=0, concat_axis=0, tiled=True, axi...  12.8 us
    all_to_all x1, blocking collectives, local(): lax.all_to_all(coarse.reshape(56, 1, 128), 'gy', split_axis=0, concat_axi...  9.58 us
    all_to_all x1, starting transfers between devices, local(): lax.all_to_all(sent, 'gy', split_axis=0, concat_axis=0, tiled=True, axis_...  8.01 us
    pallas_call x6, Pallas kernels, call(): pl.pallas_call(kernel, out_shape=[jax.ShapeDtypeStruct(*(out if isinstanc...  5.04 us
    ppermute x1, waiting for transfers between devices, local(): lax.ppermute(passed, 'gx', [(i, j) for i, j in step if 0 <= j < size])  3.88 us
    ppermute x1, starting transfers between devices, local(): near_in = lax.ppermute(near, 'gx', [(i, i ^ 1) for i in range(size)])  3.21 us
    ppermute x1, starting transfers between devices, local(): far_in = lax.ppermute(far, 'gx', beyond + [(j, i) for i, j in beyond])  1.91 us
    ppermute x1, starting transfers between devices, local(): lax.ppermute(passed, 'gx', [(i, j) for i, j in step if 0 <= j < size])  1.29 us
  transfers between devices with their start and end apart: 4, of which 2 were waited for; matrix products, arithmetic and copies ran while one was open for 0% of the time, Pallas kernels for 1%

profile of v3, /device:TPU:4, one launch (start us, length us, event | category | flops | bytes accessed | tf_op | source)
XLA Modules:
  0.0 47.3 jit_solution(14272991571878896784)
XLA Ops:
  0.6 2.4 %front.1 = (f32[64,128]{1,0:T(8,128)S(1)}, f32[64,128]{1,0:T(8,128)S(1)}, f32[32,128]{1,0:T(8,128)S(1)}, f32[32,128]{1,0:T(8,128)S(1)}, f32[8,24,128]{2,1,0:T(8,128)}, /*index=5*/s32[8,256]{1,0:T(8,128)S(1)}) custom-call(s32[8,8]{1,0:T(8,128)} %bitcast.29, s32[8,256]{1,0:T(8,128)} %bitcast.27, f32[64,128]{1,0:T(8,128)} %bitcast.19, f32[64,128]{1,0:T(8,128)} %bitcast.21, ...), custom_call_target="tpu_custom_call" | custom-call | flops 1000000 | bytes 200000 | tf_op jit(solution)/shard_map/front/pallas_call | solution.py:365
  3.1 0.0 copy-start
  3.1 0.0 copy-start.1
  3.1 8.0 %all-to-all-start = ((f32[8,24,128]{2,1,0:T(8,128)}), f32[8,24,128]{2,1,0:T(8,128)S(1)}, u32[]{:S(2)}, u32[]{:S(2)}) async-start(f32[8,24,128]{2,1,0:T(8,128)} %get-tuple-element.13), calls=%async_computation | async-start | bytes 196608 | tf_op jit(solution)/shard_map/all_to_all | solution.py:410
  11.1 1.9 %collective-permute-start = (f32[32,128]{1,0:T(8,128)S(1)}, f32[32,128]{1,0:T(8,128)S(1)}, u32[]{:S(2)}, u32[]{:S(2)}) collective-permute-start(f32[32,128]{1,0:T(8,128)S(1)} %get-tuple-element.16), channel_id=1, source_target_pairs={{8,16},{24,32},{40,48},{56,64},{72,80},{88,96},{104,112},{120,128}... | collective-permute-start | bytes 49160 | tf_op jit(solution)/shard_map/ppermute | solution.py:415
  13.0 3.2 %collective-permute-start.1 = (f32[32,128]{1,0:T(8,128)S(1)}, f32[32,128]{1,0:T(8,128)S(1)}, u32[]{:S(2)}, u32[]{:S(2)}) collective-permute-start(f32[32,128]{1,0:T(8,128)S(1)} %get-tuple-element.17), channel_id=1, source_target_pairs={{0,8},{8,0},{16,24},{24,16},{32,40},{40,32},{48,56},{56,48},{64,72... | collective-permute-start | bytes 49160 | tf_op jit(solution)/shard_map/ppermute | solution.py:416
  16.2 0.0 collective-permute-done.far
  16.2 0.8 %collective-permute-done.1.near = f32[32,128]{1,0:T(8,128)S(1)} collective-permute-done((f32[32,128]{1,0:T(8,128)S(1)}, f32[32,128]{1,0:T(8,128)S(1)}, u32[]{:S(2)}, u32[]{:S(2)}) %collective-permute-start.1) | collective-permute-done | bytes 16416 | tf_op jit(solution)/shard_map/ppermute | solution.py:416
  17.0 0.0 all-to-all-done.arrived
  17.0 0.0 copy-done
  17.0 0.0 copy-done.1
  17.0 0.7 %residual.1 = (f32[64,128]{1,0:T(8,128)S(1)}, f32[56,128]{1,0:T(8,128)S(1)}) custom-call(s32[8,256]{1,0:T(8,128)S(1)} %get-tuple-element.12.cells, f32[8,24,128]{2,1,0:T(8,128)S(1)} %all-to-all-done.arrived, f32[64,128]{1,0:T(8,128)S(1)} %get-tuple-element.14.smoothed, f32[64,128]{1,0:T(8,128)S(1)} %get-tuple-element.15.count, f32[64,128]{1,0:T(8,128)S(1)} %bitcast.22, ...), custom_call_target="tpu_custom_call" | custom-call | flops 1000000 | bytes 200000 | tf_op jit(solution)/shard_map/residual/pallas_call | solution.py:365
  17.7 9.6 %all_to_all.21 = f32[56,1,128]{2,1,0:T(1,128)S(1)} all-to-all(f32[56,1,128]{2,1,0:T(1,128)S(1)} %bitcast.23), channel_id=1, replica_groups={{4,5,6,7,0,1,2,3},{12,13,14,15,8,9,10,11},{20,21,22,23,16,17,18,19},{28..., dimensions={0} | all-to-all | bytes 57344 | tf_op jit(solution)/shard_map/all_to_all | solution.py:422
  27.3 12.8 %all_to_all.22 = f32[8,16,128]{2,1,0:T(8,128)S(1)} all-to-all(f32[8,16,128]{2,1,0:T(8,128)S(1)} %bitcast.16), channel_id=1, replica_groups={{32,40,48,56,0,8,16,24},{96,104,112,120,64,72,80,88},{160,168,176,184,1..., dimensions={0} | all-to-all | bytes 131072 | tf_op jit(solution)/shard_map/all_to_all | solution.py:427
  40.2 1.3 %collective-permute-start.2 = (f32[64,128]{1,0:T(8,128)S(1)}, f32[64,128]{1,0:T(8,128)S(1)}, u32[]{:S(2)}, u32[]{:S(2)}) collective-permute-start(f32[64,128]{1,0:T(8,128)S(1)} %get-tuple-element.19), channel_id=1, source_target_pairs={{0,64},{8,72},{16,80},{24,88},{64,128},{72,136},{80,144},{88,152},... | collective-permute-start | bytes 98312 | tf_op jit(solution)/shard_map/ppermute | solution.py:437
  41.5 0.6 %fix.1 = f32[64,128]{1,0:T(8,128)} custom-call(f32[8,128]{1,0:T(8,128)S(1)} %get-tuple-element.20.edges, f32[64,128]{1,0:T(8,128)S(1)} %get-tuple-element.21.partial), custom_call_target="tpu_custom_call" | custom-call | flops 1000000 | bytes 200000 | tf_op jit(solution)/shard_map/fix/pallas_call | solution.py:365
  42.1 3.9 %collective-permute-done.2.extra = f32[64,128]{1,0:T(8,128)S(1)} collective-permute-done((f32[64,128]{1,0:T(8,128)S(1)}, f32[64,128]{1,0:T(8,128)S(1)}, u32[]{:S(2)}, u32[]{:S(2)}) %collective-permute-start.2) | collective-permute-done | bytes 32800 | tf_op jit(solution)/shard_map/ppermute | solution.py:437
  46.0 1.3 %coarse.1 = f32[64,128]{1,0:T(8,128)} custom-call(f32[128,128]{1,0:T(8,128)S(1)} %bitcast.15, f32[64,128]{1,0:T(8,128)S(1)} %collective-permute-done.2.extra, f32[64,128]{1,0:T(8,128)S(1)} %get-tuple-element.14.smoothed), custom_call_target="tpu_custom_call" | custom-call | flops 1000000 | bytes 200000 | tf_op jit(solution)/shard_map/coarse/pallas_call | solution.py:365
  (2 shorter events, 0.0 us)
Async XLA Ops:
  3.1 14.0 %copy-start = (f32[2,4,8,128]{3,2,1,0:T(8,128)S(1)}, f32[2,4,8,128]{3,2,1,0:T(8,128)}, u32[]{:S(2)}) copy-start(f32[2,4,8,128]{3,2,1,0:T(8,128)} %param.7) | copy-start | bytes 98308
  3.1 14.0 %copy-start.1 = (f32[2,4,8,128]{3,2,1,0:T(8,128)S(1)}, f32[2,4,8,128]{3,2,1,0:T(8,128)}, u32[]{:S(2)}) copy-start(f32[2,4,8,128]{3,2,1,0:T(8,128)} %param.6) | copy-start | bytes 98308
  3.1 14.0 %all-to-all-start = ((f32[8,24,128]{2,1,0:T(8,128)}), f32[8,24,128]{2,1,0:T(8,128)S(1)}, u32[]{:S(2)}, u32[]{:S(2)}) async-start(f32[8,24,128]{2,1,0:T(8,128)} %get-tuple-element.13), calls=%async_computation | async-start | bytes 196608 | tf_op jit(solution)/shard_map/all_to_all | solution.py:410
  11.1 5.1 %collective-permute-start = (f32[32,128]{1,0:T(8,128)S(1)}, f32[32,128]{1,0:T(8,128)S(1)}, u32[]{:S(2)}, u32[]{:S(2)}) collective-permute-start(f32[32,128]{1,0:T(8,128)S(1)} %get-tuple-element.16), channel_id=1, source_target_pairs={{8,16},{24,32},{40,48},{56,64},{72,80},{88,96},{104,112},{120,128}... | collective-permute-start | bytes 49160 | tf_op jit(solution)/shard_map/ppermute | solution.py:415
  13.0 4.0 %collective-permute-start.1 = (f32[32,128]{1,0:T(8,128)S(1)}, f32[32,128]{1,0:T(8,128)S(1)}, u32[]{:S(2)}, u32[]{:S(2)}) collective-permute-start(f32[32,128]{1,0:T(8,128)S(1)} %get-tuple-element.17), channel_id=1, source_target_pairs={{0,8},{8,0},{16,24},{24,16},{32,40},{40,32},{48,56},{56,48},{64,72... | collective-permute-start | bytes 49160 | tf_op jit(solution)/shard_map/ppermute | solution.py:416
  40.2 5.8 %collective-permute-start.2 = (f32[64,128]{1,0:T(8,128)S(1)}, f32[64,128]{1,0:T(8,128)S(1)}, u32[]{:S(2)}, u32[]{:S(2)}) collective-permute-start(f32[64,128]{1,0:T(8,128)S(1)} %get-tuple-element.19), channel_id=1, source_target_pairs={{0,64},{8,72},{16,80},{24,88},{64,128},{72,136},{80,144},{88,152},... | collective-permute-start | bytes 98312 | tf_op jit(solution)/shard_map/ppermute | solution.py:437

commit v4 on v3

--- a/solution.py
+++ b/solution.py
@@ -11,7 +11,12 @@
 ROW = 8
 TURN = 3
 LATER = 4
-SIDE = 4
+
+
+def side_of(along):
+    return 4 * (along >= ROW)
+
+
 F32 = jnp.float32
 BF16 = jnp.bfloat16
 damping = 0.8
@@ -28,7 +33,7 @@
 
 def place():
     along = lax.axis_index("gx")
-    return lax.axis_index("gy"), lax.rem(along, 2) == 0, lax.rem(along, ROW)
+    return along, lax.axis_index("gy"), lax.rem(along, 2) == 0
 
 
 def parts(value, count):
@@ -55,7 +60,7 @@
     counts_in, cells_in, cond_in, rhs_in, base_in, frac_in, smoothed, count, near, far, sent,
     marked, counts, cells, cond, rhs, base, frac, donors, sems,
 ):
-    own, first, _ = place()
+    _, own, first = place()
     pairs = (
         (counts_in, counts), (cells_in, cells), (cond_in, cond), (rhs_in, rhs), (base_in, base),
         (frac_in, frac),
@@ -143,7 +148,7 @@
 def residual_kernel(
     cells, arrived, smoothed, count, rhs, cond, far, near, partial, coarse
 ):
-    own, first, _ = place()
+    _, own, first = place()
     total = jnp.zeros((192, 128), F32)
     for b in range(8):
         high, low = one_hots(cells[b : b + 1, :])
@@ -275,10 +280,10 @@
 
 
 def pass_kernel(gathered, lines, passed, edges):
-    own, _, column = place()
-    upper = gathered[pl.ds(((4 - SIDE) & 7) * 16, 64), :]
-    lower = gathered[pl.ds(((0 - SIDE) & 7) * 16, 64), :]
-    passed[...] = jnp.where(column < ROW // 2, upper, lower)
+    along, own, _ = place()
+    low_half = lax.rem(along, ROW) < ROW // 2
+    start = (jnp.where(low_half, ROW // 2, 0) - side_of(along)) & 7
+    passed[...] = gathered[pl.ds(pl.multiple_of(start * 16, 64), 64), :]
     below = lines[pl.ds(((own + 7 - LATER) & 7) * 7 + 3, 4), :]
     above = lines[pl.ds(((own + 9 - LATER) & 7) * 7 + 3, 4), :]
     edges[0:4, :] = jnp.where(own > 0, below, 0.0)
@@ -302,7 +307,8 @@
 
 
 def coarse_kernel(gathered, extra, smoothed, pressure):
-    own, _, column = place()
+    along, own, _ = place()
+    column, side = lax.rem(along, ROW), side_of(along)
     lanes = iota((8, 128), 1)
     rows = (iota((8, 128), 0) + LATER) & 7
     low_z = lanes % 32 > 0
@@ -326,7 +332,7 @@
     for slot in range(7):
         at = column + slot - 3
         inside = jnp.logical_and(at >= 0, at < ROW)
-        here = pl.multiple_of(((jnp.clip(at, 0, ROW - 1) - SIDE) & 7) * 16, 16)
+        here = pl.multiple_of(((jnp.clip(at, 0, ROW - 1) - side) & 7) * 16, 16)
         there = pl.multiple_of((at & 3) * 16, 16)
         for f, out in ((0, rhs), (8, cond)):
             out.append(
@@ -408,8 +414,7 @@
     )
     turned = [[(i + TURN) % 8 for i in range(8)]]
     arrived = lax.all_to_all(
-        sent, "gy", split_axis=0, concat_axis=0, tiled=True,
-        axis_index_groups=turned,
+        sent, "gy", split_axis=0, concat_axis=0, tiled=True, axis_index_groups=turned
     )
     beyond = [(i, i + 1) for i in range(1, size - 1, 2)]
     far_in = lax.ppermute(far, "gx", beyond + [(j, i) for i, j in beyond])
@@ -427,7 +432,8 @@
     gathered = lax.all_to_all(
         column, "gx", split_axis=0, concat_axis=0, tiled=True,
         axis_index_groups=[
-            [start + (i + SIDE) % ROW for i in range(ROW)] for start in range(0, size, ROW)
+            [start + (i + int(side_of(start))) % ROW for i in range(ROW)]
+            for start in range(0, size, ROW)
         ],
     )
     passed, edges = call(

time: 47.7 us -> 46.9 us (0.983)
  the two profiles are of different devices: /device:TPU:4 before, /device:TPU:6 now
where the time goes in v4:
time: 46.9 us; the launch traced here: 46.5 us
  blocking collectives  20.5 us (44%)
  starting transfers between devices  15.5 us (33%)
  Pallas kernels  5.03 us (11%)
  waiting for transfers between devices  4.7 us (10%)
  between operations  0.7 us (1%)
    all_to_all x1, blocking collectives, local(): lax.all_to_all(column, 'gx', split_axis=0, concat_axis=0, tiled=True, axi...  10.9 us
    all_to_all x1, blocking collectives, local(): lax.all_to_all(coarse.reshape(56, 1, 128), 'gy', split_axis=0, concat_axi...  9.58 us
    all_to_all x1, starting transfers between devices, local(): lax.all_to_all(sent, 'gy', split_axis=0, concat_axis=0, tiled=True, axis_...  8.02 us
    pallas_call x6, Pallas kernels, call(): pl.pallas_call(kernel, out_shape=[jax.ShapeDtypeStruct(*(out if isinstanc...  5.03 us
    ppermute x1, starting transfers between devices, local(): near_in = lax.ppermute(near, 'gx', [(i, i ^ 1) for i in range(size)])  4.29 us
    ppermute x1, waiting for transfers between devices, local(): lax.ppermute(passed, 'gx', [(i, j) for i, j in step if 0 <= j < size])  3.88 us
    ppermute x1, starting transfers between devices, local(): far_in = lax.ppermute(far, 'gx', beyond + [(j, i) for i, j in beyond])  1.91 us
    ppermute x1, starting transfers between devices, local(): lax.ppermute(passed, 'gx', [(i, j) for i, j in step if 0 <= j < size])  1.28 us
  transfers between devices with their start and end apart: 4, of which 2 were waited for; matrix products, arithmetic and copies ran while one was open for 0% of the time, Pallas kernels for 1%

profile of v4, /device:TPU:6, one launch (start us, length us, event | category | flops | bytes accessed | tf_op | source)
XLA Modules:
  0.0 46.5 jit_solution(12007774697095130984)
XLA Ops:
  0.6 2.4 %front.1 = (f32[64,128]{1,0:T(8,128)S(1)}, f32[64,128]{1,0:T(8,128)S(1)}, f32[32,128]{1,0:T(8,128)S(1)}, f32[32,128]{1,0:T(8,128)S(1)}, f32[8,24,128]{2,1,0:T(8,128)}, /*index=5*/s32[8,256]{1,0:T(8,128)S(1)}) custom-call(s32[8,8]{1,0:T(8,128)} %bitcast.29, s32[8,256]{1,0:T(8,128)} %bitcast.27, f32[64,128]{1,0:T(8,128)} %bitcast.19, f32[64,128]{1,0:T(8,128)} %bitcast.21, ...), custom_call_target="tpu_custom_call" | custom-call | flops 1000000 | bytes 200000 | tf_op jit(solution)/shard_map/front/pallas_call | solution.py:371
  3.0 0.0 copy-start
  3.1 0.0 copy-start.1
  3.1 8.0 %all-to-all-start = ((f32[8,24,128]{2,1,0:T(8,128)}), f32[8,24,128]{2,1,0:T(8,128)S(1)}, u32[]{:S(2)}, u32[]{:S(2)}) async-start(f32[8,24,128]{2,1,0:T(8,128)} %get-tuple-element.13), calls=%async_computation | async-start | bytes 196608 | tf_op jit(solution)/shard_map/all_to_all | solution.py:416
  11.1 1.9 %collective-permute-start = (f32[32,128]{1,0:T(8,128)S(1)}, f32[32,128]{1,0:T(8,128)S(1)}, u32[]{:S(2)}, u32[]{:S(2)}) collective-permute-start(f32[32,128]{1,0:T(8,128)S(1)} %get-tuple-element.16), channel_id=1, source_target_pairs={{8,16},{24,32},{40,48},{56,64},{72,80},{88,96},{104,112},{120,128}... | collective-permute-start | bytes 49160 | tf_op jit(solution)/shard_map/ppermute | solution.py:420
  13.0 4.3 %collective-permute-start.1 = (f32[32,128]{1,0:T(8,128)S(1)}, f32[32,128]{1,0:T(8,128)S(1)}, u32[]{:S(2)}, u32[]{:S(2)}) collective-permute-start(f32[32,128]{1,0:T(8,128)S(1)} %get-tuple-element.17), channel_id=1, source_target_pairs={{0,8},{8,0},{16,24},{24,16},{32,40},{40,32},{48,56},{56,48},{64,72... | collective-permute-start | bytes 49160 | tf_op jit(solution)/shard_map/ppermute | solution.py:421
  17.3 0.0 collective-permute-done.far
  17.3 0.8 %collective-permute-done.1.near = f32[32,128]{1,0:T(8,128)S(1)} collective-permute-done((f32[32,128]{1,0:T(8,128)S(1)}, f32[32,128]{1,0:T(8,128)S(1)}, u32[]{:S(2)}, u32[]{:S(2)}) %collective-permute-start.1) | collective-permute-done | bytes 16416 | tf_op jit(solution)/shard_map/ppermute | solution.py:421
  18.1 0.0 all-to-all-done.arrived
  18.1 0.0 copy-done
  18.1 0.0 copy-done.1
  18.1 0.7 %residual.1 = (f32[64,128]{1,0:T(8,128)S(1)}, f32[56,128]{1,0:T(8,128)S(1)}) custom-call(s32[8,256]{1,0:T(8,128)S(1)} %get-tuple-element.12.cells, f32[8,24,128]{2,1,0:T(8,128)S(1)} %all-to-all-done.arrived, f32[64,128]{1,0:T(8,128)S(1)} %get-tuple-element.14.smoothed, f32[64,128]{1,0:T(8,128)S(1)} %get-tuple-element.15.count, f32[64,128]{1,0:T(8,128)S(1)} %bitcast.22, ...), custom_call_target="tpu_custom_call" | custom-call | flops 1000000 | bytes 200000 | tf_op jit(solution)/shard_map/residual/pallas_call | solution.py:371
  18.8 9.6 %all_to_all.21 = f32[56,1,128]{2,1,0:T(1,128)S(1)} all-to-all(f32[56,1,128]{2,1,0:T(1,128)S(1)} %bitcast.23), channel_id=1, replica_groups={{4,5,6,7,0,1,2,3},{12,13,14,15,8,9,10,11},{20,21,22,23,16,17,18,19},{28..., dimensions={0} | all-to-all | bytes 57344 | tf_op jit(solution)/shard_map/all_to_all | solution.py:427
  28.4 10.9 %all_to_all.22 = f32[8,16,128]{2,1,0:T(8,128)S(1)} all-to-all(f32[8,16,128]{2,1,0:T(8,128)S(1)} %bitcast.16), channel_id=1, replica_groups={{0,8,16,24,32,40,48,56},{96,104,112,120,64,72,80,88},{160,168,176,184,1..., dimensions={0} | all-to-all | bytes 131072 | tf_op jit(solution)/shard_map/all_to_all | solution.py:432
  39.3 1.3 %collective-permute-start.2 = (f32[64,128]{1,0:T(8,128)S(1)}, f32[64,128]{1,0:T(8,128)S(1)}, u32[]{:S(2)}, u32[]{:S(2)}) collective-permute-start(f32[64,128]{1,0:T(8,128)S(1)} %get-tuple-element.19), channel_id=1, source_target_pairs={{0,64},{8,72},{16,80},{24,88},{64,128},{72,136},{80,144},{88,152},... | collective-permute-start | bytes 98312 | tf_op jit(solution)/shard_map/ppermute | solution.py:443
  40.6 0.6 %fix.1 = f32[64,128]{1,0:T(8,128)} custom-call(f32[8,128]{1,0:T(8,128)S(1)} %get-tuple-element.20.edges, f32[64,128]{1,0:T(8,128)S(1)} %get-tuple-element.21.partial), custom_call_target="tpu_custom_call" | custom-call | flops 1000000 | bytes 200000 | tf_op jit(solution)/shard_map/fix/pallas_call | solution.py:371
  41.3 3.9 %collective-permute-done.2.extra = f32[64,128]{1,0:T(8,128)S(1)} collective-permute-done((f32[64,128]{1,0:T(8,128)S(1)}, f32[64,128]{1,0:T(8,128)S(1)}, u32[]{:S(2)}, u32[]{:S(2)}) %collective-permute-start.2) | collective-permute-done | bytes 32800 | tf_op jit(solution)/shard_map/ppermute | solution.py:443
  45.1 1.3 %coarse.1 = f32[64,128]{1,0:T(8,128)} custom-call(f32[128,128]{1,0:T(8,128)S(1)} %bitcast.15, f32[64,128]{1,0:T(8,128)S(1)} %collective-permute-done.2.extra, f32[64,128]{1,0:T(8,128)S(1)} %get-tuple-element.14.smoothed), custom_call_target="tpu_custom_call" | custom-call | flops 1000000 | bytes 200000 | tf_op jit(solution)/shard_map/coarse/pallas_call | solution.py:371
  (2 shorter events, 0.0 us)
Async XLA Ops:
  3.0 15.1 %copy-start = (f32[2,4,8,128]{3,2,1,0:T(8,128)S(1)}, f32[2,4,8,128]{3,2,1,0:T(8,128)}, u32[]{:S(2)}) copy-start(f32[2,4,8,128]{3,2,1,0:T(8,128)} %param.7) | copy-start | bytes 98308
  3.1 15.1 %copy-start.1 = (f32[2,4,8,128]{3,2,1,0:T(8,128)S(1)}, f32[2,4,8,128]{3,2,1,0:T(8,128)}, u32[]{:S(2)}) copy-start(f32[2,4,8,128]{3,2,1,0:T(8,128)} %param.6) | copy-start | bytes 98308
  3.1 15.1 %all-to-all-start = ((f32[8,24,128]{2,1,0:T(8,128)}), f32[8,24,128]{2,1,0:T(8,128)S(1)}, u32[]{:S(2)}, u32[]{:S(2)}) async-start(f32[8,24,128]{2,1,0:T(8,128)} %get-tuple-element.13), calls=%async_computation | async-start | bytes 196608 | tf_op jit(solution)/shard_map/all_to_all | solution.py:416
  11.1 6.2 %collective-permute-start = (f32[32,128]{1,0:T(8,128)S(1)}, f32[32,128]{1,0:T(8,128)S(1)}, u32[]{:S(2)}, u32[]{:S(2)}) collective-permute-start(f32[32,128]{1,0:T(8,128)S(1)} %get-tuple-element.16), channel_id=1, source_target_pairs={{8,16},{24,32},{40,48},{56,64},{72,80},{88,96},{104,112},{120,128}... | collective-permute-start | bytes 49160 | tf_op jit(solution)/shard_map/ppermute | solution.py:420
  13.0 5.1 %collective-permute-start.1 = (f32[32,128]{1,0:T(8,128)S(1)}, f32[32,128]{1,0:T(8,128)S(1)}, u32[]{:S(2)}, u32[]{:S(2)}) collective-permute-start(f32[32,128]{1,0:T(8,128)S(1)} %get-tuple-element.17), channel_id=1, source_target_pairs={{0,8},{8,0},{16,24},{24,16},{32,40},{40,32},{48,56},{56,48},{64,72... | collective-permute-start | bytes 49160 | tf_op jit(solution)/shard_map/ppermute | solution.py:421
  39.3 5.8 %collective-permute-start.2 = (f32[64,128]{1,0:T(8,128)S(1)}, f32[64,128]{1,0:T(8,128)S(1)}, u32[]{:S(2)}, u32[]{:S(2)}) collective-permute-start(f32[64,128]{1,0:T(8,128)S(1)} %get-tuple-element.19), channel_id=1, source_target_pairs={{0,64},{8,72},{16,80},{24,88},{64,128},{72,136},{80,144},{88,152},... | collective-permute-start | bytes 98312 | tf_op jit(solution)/shard_map/ppermute | solution.py:443

commit v5 on v4

--- a/solution.py
+++ b/solution.py
@@ -9,7 +9,8 @@
 
 BLOCK = 128
 ROW = 8
-TURN = 3
+TURN = 5
+CHUNK = 26
 LATER = 4
 
 
@@ -52,19 +53,25 @@
     return iota((64, rows), 0) == (cells >> 7), low.astype(F32).astype(BF16)
 
 
+def exact_product(value, table):
+    rows = value.shape[0]
+    cuts = jnp.dot(
+        jnp.concatenate(parts(value, 3), axis=0), table.astype(F32).astype(BF16),
+        preferred_element_type=F32,
+    )
+    return cuts[0:rows] + cuts[rows : 2 * rows] + cuts[2 * rows : 3 * rows]
+
+
 def contract_rows(left, right):
     return lax.dot_general(left, right, (((1,), (1,)), ((), ())), preferred_element_type=F32)
 
 
 def front_kernel(
-    counts_in, cells_in, cond_in, rhs_in, base_in, frac_in, smoothed, count, near, far, sent,
-    marked, counts, cells, cond, rhs, base, frac, donors, sems,
+    counts_in, cells_in, cond_in, rhs_in, smoothed, count, near, far, marked,
+    counts, cells, cond, rhs, sems,
 ):
     _, own, first = place()
-    pairs = (
-        (counts_in, counts), (cells_in, cells), (cond_in, cond), (rhs_in, rhs), (base_in, base),
-        (frac_in, frac),
-    )
+    pairs = ((counts_in, counts), (cells_in, cells), (cond_in, cond), (rhs_in, rhs))
     copies = [
         pltpu.make_async_copy(source, target, sems.at[i]) for i, (source, target) in enumerate(pairs)
     ]
@@ -92,15 +99,9 @@
             near[at, :] = jnp.where(first, high_x, low_x)
             far[at, :] = jnp.where(first, low_x, high_x)
 
-    faces = [
-        [ref[pl.ds(y, 8, stride=8), :] for ref in (smoothed, cond)] for y in (0, 7)
-    ]
-    for d in range(8):
-        for f in range(2):
-            sent[(d - TURN) % 8, f * 8 : f * 8 + 8, :] = jnp.where(d > own, faces[1][f], faces[0][f])
-
-    copies[4].wait()
-    copies[5].wait()
+
+def donor_kernel(base, frac, smoothed, donors):
+    field = smoothed[...]
     high = field.astype(BF16).astype(F32)
     stacked = jnp.concatenate([high, field - high, high], axis=0)
     columns = stacked.T.astype(BF16)
@@ -129,9 +130,30 @@
             columns, jnp.concatenate([upper, upper, lower], axis=0), preferred_element_type=F32
         )
         donors[row, :] = jnp.sum(mixed * weight_z, axis=0, keepdims=True)
+
+
+def pack_kernel(donors, smoothed, cond, far, near, sent):
+    _, own, first = place()
+    faces = []
+    for y in (0, 7):
+        near_rows = near[pl.ds(y, 4, stride=8), :]
+        far_rows = far[pl.ds(y, 4, stride=8), :]
+        faces.append(
+            (
+                smoothed[pl.ds(y, 8, stride=8), :],
+                cond[pl.ds(y, 8, stride=8), :],
+                jnp.where(first, far_rows, near_rows),
+                jnp.where(first, near_rows, far_rows),
+            )
+        )
     for d in range(8):
-        sent[(d - TURN) % 8, 16:17, :] = donors[d : d + 1, 0:128]
-        sent[(d - TURN) % 8, 17:18, :] = donors[d : d + 1, 128:256]
+        start = (d - TURN) % 8 * CHUNK
+        for f, (row, count) in enumerate(((0, 8), (8, 8), (16, 4), (20, 4))):
+            sent[start + row : start + row + count, :] = jnp.where(
+                d > own, faces[1][f], faces[0][f]
+            )
+        sent[start + 24 : start + 25, :] = donors[d : d + 1, 0:128]
+        sent[start + 25 : start + 26, :] = donors[d : d + 1, 128:256]
 
 
 def neighbour_sums(fields, shift_y, shift_z):
@@ -149,18 +171,21 @@
     cells, arrived, smoothed, count, rhs, cond, far, near, partial, coarse
 ):
     _, own, first = place()
-    total = jnp.zeros((192, 128), F32)
+    total = jnp.zeros((128, 128), F32)
     for b in range(8):
         high, low = one_hots(cells[b : b + 1, :])
-        values = jnp.concatenate([arrived[(b - TURN) % 8, 16:17, :], arrived[(b - TURN) % 8, 17:18, :]], axis=1)
+        values = jnp.concatenate([
+                arrived[(b - TURN) % 8 * CHUNK + row : (b - TURN) % 8 * CHUNK + row + 1, :]
+                for row in (24, 25)
+            ], axis=1)
         left = jnp.concatenate(
-            [jnp.where(high, cut.astype(F32), 0.0).astype(BF16) for cut in parts(values, 3)], axis=0
+            [jnp.where(high, cut.astype(F32), 0.0).astype(BF16) for cut in parts(values, 2)], axis=0
         )
         total = total + contract_rows(left, low)
-    total = total[0:64] + total[64:128] + total[128:192]
-
-    below = jnp.where(own > 0, arrived[(own + 7 - TURN) & 7, 0:16, :], 0.0)
-    above = jnp.where(own < 7, arrived[(own + 9 - TURN) & 7, 0:16, :], 0.0)
+    total = total[0:64] + total[64:128]
+
+    below = jnp.where(own > 0, arrived[pl.ds(((own + 7 - TURN) & 7) * CHUNK, 24), :], 0.0)
+    above = jnp.where(own < 7, arrived[pl.ds(((own + 9 - TURN) & 7) * CHUNK, 24), :], 0.0)
     lanes = iota((8, 128), 1)
     rows = iota((8, 128), 0)
     keep_up = lanes < 127
@@ -186,9 +211,9 @@
             right = jnp.where(first, near_plane, far_plane)
             start = grid * 32
             planes = [left] + [ref[start + x * 8 : start + x * 8 + 8, :] for x in range(4)] + [right]
-            at = 8 * f + grid * 4
-            lower = [0.0] + [below[at + x : at + x + 1, :] for x in range(4)] + [0.0]
-            upper = [0.0] + [above[at + x : at + x + 1, :] for x in range(4)] + [0.0]
+            at = [16 + 2 * f + grid] + [8 * f + grid * 4 + x for x in range(4)] + [20 + 2 * f + grid]
+            lower = [below[row : row + 1, :] for row in at]
+            upper = [above[row : row + 1, :] for row in at]
             fields.append((planes, lower, upper))
         fields.append(tuple([v * c for v, c in zip(*pair)] for pair in zip(*fields)))
         sums = []
@@ -215,95 +240,26 @@
         start = grid * 32
         pooled.append(sum(cond[start + x * 8 : start + x * 8 + 8, :] for x in range(4)))
 
-    here = []
-    there = []
-    for f in range(2):
-        here.append(
-            jnp.concatenate(
-                [
-                    face[8 * f + 4 * grid + x : 8 * f + 4 * grid + x + 1, :]
-                    for face in (below, above)
-                    for x in (0, 3)
-                    for grid in range(2)
-                ],
-                axis=0,
-            )
-        )
-        corner = []
-        for y in (0, 7):
-            near_rows = near[pl.ds(16 * f + y, 2, stride=8), :]
-            far_rows = far[pl.ds(16 * f + y, 2, stride=8), :]
-            corner.append(jnp.where(first, far_rows, near_rows))
-            corner.append(jnp.where(first, near_rows, far_rows))
-        there.append(jnp.concatenate(corner, axis=0))
-
-    def corner_sum(value):
-        return 0.25 * value + (1.0 / 6.0) * shift_z(value)
-
-    fix = (
-        here[1] * corner_sum(there[0])
-        + corner_sum(there[0] * there[1])
-        - here[0] * corner_sum(there[1])
-    )
-    pooled.append(fix)
-    pool = (iota((128, 128), 0) // 4 == iota((128, 128), 1) % 32).astype(F32)
-    means = jnp.dot(
-        jnp.concatenate(pooled, axis=0),
-        pool,
-        preferred_element_type=F32,
-        precision=lax.Precision.HIGHEST,
-    ) * (1.0 / 64.0)
+    pool = iota((128, 128), 0) // 4 == iota((128, 128), 1) % 32
+    means = exact_product(jnp.concatenate(pooled, axis=0), pool) * (1.0 / 64.0)
     own_part = iota((16, 128), 0) // 4 == iota((16, 128), 1) // 32
     lines = [
         jnp.sum(jnp.where(own_part, means[f * 16 : f * 16 + 16], 0.0), axis=0, keepdims=True)
         for f in range(2)
     ]
-    fix_part = (rows % 2) * 2 + 1 - rows // 4 == lanes // 32
-    lines.append(jnp.sum(jnp.where(fix_part, means[32:40], 0.0), axis=0, keepdims=True))
-    tiles = []
-    for j in range(8):
-        above = (j + LATER) % 8 > own
-        tiles += lines + [jnp.where(above, fix[4:8], fix[0:4])]
-    coarse[...] = jnp.concatenate(tiles, axis=0)
-
-
-def merge_kernel(lines, column):
-    lanes = iota((8, 128), 1)
-    rows = (iota((8, 128), 0) + LATER) & 7
-    rhs, cond, corner = [lines[pl.ds(f, 8, stride=7), :] for f in range(3)]
-    from_below = jnp.where(rows > 0, pltpu.roll(corner, 1, 0), 0.0)
-    from_above = jnp.where(rows < 7, pltpu.roll(corner, 7, 0), 0.0)
-    rhs = rhs + jnp.where(lanes % 64 < 32, from_below, from_above)
-    for i in range(ROW):
-        column[i * 16 : i * 16 + 8, :] = rhs
-        column[i * 16 + 8 : i * 16 + 16, :] = cond
-
-
-def pass_kernel(gathered, lines, passed, edges):
-    along, own, _ = place()
+    coarse[...] = jnp.broadcast_to(jnp.concatenate(lines, axis=0)[None], (64, 2, 128))
+
+
+def pass_kernel(gathered, passed, token):
+    along, _, _ = place()
     low_half = lax.rem(along, ROW) < ROW // 2
     start = (jnp.where(low_half, ROW // 2, 0) - side_of(along)) & 7
     passed[...] = gathered[pl.ds(pl.multiple_of(start * 16, 64), 64), :]
-    below = lines[pl.ds(((own + 7 - LATER) & 7) * 7 + 3, 4), :]
-    above = lines[pl.ds(((own + 9 - LATER) & 7) * 7 + 3, 4), :]
-    edges[0:4, :] = jnp.where(own > 0, below, 0.0)
-    edges[4:8, :] = jnp.where(own < 7, above, 0.0)
-
-
-def fix_kernel(edges, partial, residual):
-    rows = iota((8, 128), 0)
-    for grid in range(2):
-        for x in range(4):
-            at = slice(grid * 32 + x * 8, grid * 32 + x * 8 + 8)
-            value = partial[at, :]
-            if x in (0, 3):
-                row = (x // 3) * 2 + grid
-                value = value + jnp.where(
-                    rows == 0,
-                    edges[row : row + 1, :],
-                    jnp.where(rows == 7, edges[4 + row : 5 + row, :], 0.0),
-                )
-            residual[at, :] = value
+    token[...] = gathered[0:8, :]
+
+
+def store_kernel(token, partial, residual):
+    residual[...] = partial[...]
 
 
 def coarse_kernel(gathered, extra, smoothed, pressure):
@@ -334,9 +290,10 @@
         inside = jnp.logical_and(at >= 0, at < ROW)
         here = pl.multiple_of(((jnp.clip(at, 0, ROW - 1) - side) & 7) * 16, 16)
         there = pl.multiple_of((at & 3) * 16, 16)
-        for f, out in ((0, rhs), (8, cond)):
+        for f, out in ((0, rhs), (1, cond)):
             out.append(
-                jnp.where(inside, gathered[pl.ds(here + f, 8), :], extra[pl.ds(there + f, 8), :])
+                jnp.where(inside, gathered[pl.ds(here + f, 8, stride=2), :],
+                    extra[pl.ds(there + f, 8, stride=2), :],)
             )
     scale = [
         jnp.where(c > 0.0, damping / (stencil_weight_sum * coarse_scale * jnp.where(c > 0.0, c, 1.0)), 0.0)
@@ -359,8 +316,8 @@
         own_sum = own_sum[1:-1]
     mine = jnp.sum(jnp.where(rows == own, value[0], 0.0), axis=0, keepdims=True)
     spread = jnp.where(iota((16, 128), 0) // 4 == iota((16, 128), 1) // 32, mine, 0.0)
-    expand = (iota((128, 128), 0) % 32 == iota((128, 128), 1) // 4).astype(F32)
-    fine = jnp.dot(spread, expand, preferred_element_type=F32, precision=lax.Precision.HIGHEST)
+    expand = iota((128, 128), 0) % 32 == iota((128, 128), 1) // 4
+    fine = exact_product(spread, expand)
     for grid in range(2):
         for x in range(4):
             at = slice(grid * 32 + x * 8, grid * 32 + x * 8 + 8)
@@ -393,57 +350,55 @@
     frac = donor_frac[:, 0, 0]
     vector, far_memory = pltpu.VMEM, pltpu.HBM
     whole = (64, 128)
-    smoothed, count, near, far, sent, marked = call(
+    smoothed, count, near, far, marked = call(
         front_kernel, "front",
-        [whole, whole, (32, 128), (32, 128), (8, 24, 128), ((8, 256), jnp.int32)],
+        [whole, whole, (32, 128), (32, 128), ((8, 256), jnp.int32)],
         tuple(
             pltpu.with_memory_space_constraint(value, far_memory)
-            for value in (counts, cells, cond, rhs, base, frac)
+            for value in (counts, cells, cond, rhs)
         ),
-        [far_memory] * 6,
+        [far_memory] * 4,
         [
             pltpu.SMEM((8, 8), jnp.int32),
             pltpu.VMEM((8, 256), jnp.int32),
             pltpu.VMEM(whole, F32),
             pltpu.VMEM(whole, F32),
-            pltpu.VMEM((8, 256), jnp.int32),
-            pltpu.VMEM((3, 8, 256), F32),
-            pltpu.VMEM((8, 256), F32),
-            pltpu.SemaphoreType.DMA((6,)),
+            pltpu.SemaphoreType.DMA((4,)),
         ],
-    )
-    turned = [[(i + TURN) % 8 for i in range(8)]]
-    arrived = lax.all_to_all(
-        sent, "gy", split_axis=0, concat_axis=0, tiled=True, axis_index_groups=turned
     )
     beyond = [(i, i + 1) for i in range(1, size - 1, 2)]
     far_in = lax.ppermute(far, "gx", beyond + [(j, i) for i, j in beyond])
     near_in = lax.ppermute(near, "gx", [(i, i ^ 1) for i in range(size)])
+    (donors,) = call(donor_kernel, "donor", [(8, 256)], (base, frac, smoothed), [vector] * 3)
+    (sent,) = call(
+        pack_kernel, "pack", [(8 * CHUNK, 128)], (donors, smoothed, cond, far_in, near_in),
+        [vector] * 5,
+    )
+    arrived = lax.all_to_all(
+        sent.reshape(8 * CHUNK, 1, 128), "gy", split_axis=0, concat_axis=0, tiled=True,
+        axis_index_groups=[[(i + TURN) % 8 for i in range(8)]],
+    ).reshape(8 * CHUNK, 128)
     partial, coarse = call(
-        residual_kernel, "residual", [whole, (56, 128)],
-        (marked, arrived, smoothed, count, rhs, cond, far_in, near_in),
-        [vector] * 8,
-    )
-    lines = lax.all_to_all(
-        coarse.reshape(56, 1, 128), "gy", split_axis=0, concat_axis=0, tiled=True,
-        axis_index_groups=[[(i + LATER) % 8 for i in range(8)]],
-    ).reshape(56, 128)
-    (column,) = call(merge_kernel, "merge", [(128, 128)], (lines,), [vector])
+        residual_kernel, "residual", [whole, (64, 2, 128)],
+        (marked, arrived, smoothed, count, rhs, cond, far_in, near_in), [vector] * 8,
+    )
+    groups = [
+        [
+            (start + (i + int(side_of(start))) % ROW) * 8 + (j + LATER) % 8
+            for i in range(ROW)
+            for j in range(8)
+        ]
+        for start in range(0, size, ROW)
+    ]
     gathered = lax.all_to_all(
-        column, "gx", split_axis=0, concat_axis=0, tiled=True,
-        axis_index_groups=[
-            [start + (i + int(side_of(start))) % ROW for i in range(ROW)]
-            for start in range(0, size, ROW)
-        ],
-    )
-    passed, edges = call(
-        pass_kernel, "pass", [(64, 128), (8, 128)], (gathered, lines), [vector] * 2
+        coarse, ("gx", "gy"), split_axis=0, concat_axis=0, tiled=True, axis_index_groups=groups
+    ).reshape(128, 128)
+    passed, token = call(
+        pass_kernel, "pass", [(64, 128), (8, 128)], (gathered,), [vector]
     )
     step = [(i, i + ROW) if i % ROW < ROW // 2 else (i, i - ROW) for i in range(size)]
     extra = lax.ppermute(passed, "gx", [(i, j) for i, j in step if 0 <= j < size])
-    (residual,) = call(
-        fix_kernel, "fix", [whole], (edges, partial), [vector] * 2
-    )
+    (residual,) = call(store_kernel, "store", [whole], (token, partial), [vector] * 2)
     (pressure,) = call(
         coarse_kernel, "coarse", [whole],
         (gathered, extra, smoothed), [vector] * 3,

time: 46.9 us -> 45.3 us (0.966)
  the two profiles are of different devices: /device:TPU:6 before, /device:TPU:196 now
where the time goes in v5:
time: 45.3 us; the launch traced here: 44.9 us
  blocking collectives  28.1 us (62%)
  starting transfers between devices  7.04 us (16%)
  waiting for transfers between devices  4.78 us (11%)
  Pallas kernels  4.22 us (9%)
  between operations  0.74 us (2%)
    all_to_all x1, blocking collectives, local(): lax.all_to_all(coarse, ('gx', 'gy'), split_axis=0, concat_axis=0, tiled=T...  16 us
    all_to_all x1, blocking collectives, local(): lax.all_to_all(sent.reshape(8 * CHUNK, 1, 128), 'gy', split_axis=0, conca...  12.1 us
    ppermute x1, waiting for transfers between devices, local(): lax.ppermute(passed, 'gx', [(i, j) for i, j in step if 0 <= j < size])  4.47 us
    pallas_call x7, Pallas kernels, call(): pl.pallas_call(kernel, out_shape=[jax.ShapeDtypeStruct(*(out if isinstanc...  4.22 us
    ppermute x1, starting transfers between devices, local(): near_in = lax.ppermute(near, 'gx', [(i, i ^ 1) for i in range(size)])  3.21 us
    ppermute x1, starting transfers between devices, local(): far_in = lax.ppermute(far, 'gx', beyond + [(j, i) for i, j in beyond])  1.92 us
    ppermute x1, starting transfers between devices, local(): lax.ppermute(passed, 'gx', [(i, j) for i, j in step if 0 <= j < size])  1.91 us
  transfers between devices with their start and end apart: 3, of which 2 were waited for; matrix products, arithmetic and copies ran while one was open for 0% of the time, Pallas kernels for 2%

profile of v5, /device:TPU:196, one launch (start us, length us, event | category | flops | bytes accessed | tf_op | source)
XLA Modules:
  0.0 44.9 jit_solution(15170798549563432786)
XLA Ops:
  0.6 0.0 copy-start.2
  0.6 1.2 %front.1 = (f32[64,128]{1,0:T(8,128)S(1)}, f32[64,128]{1,0:T(8,128)S(1)}, f32[32,128]{1,0:T(8,128)S(1)}, f32[32,128]{1,0:T(8,128)S(1)}, s32[8,256]{1,0:T(8,128)S(1)}) custom-call(s32[8,8]{1,0:T(8,128)} %bitcast.27, s32[8,256]{1,0:T(8,128)} %bitcast.26, f32[64,128]{1,0:T(8,128)} %bitcast.17, f32[64,128]{1,0:T(8,128)} %bitcast.20), custom_call_target="tpu_custom_call" | custom-call | flops 1000000 | bytes 200000 | tf_op jit(solution)/shard_map/front/pallas_call | solution.py:328
  1.9 0.0 copy-start.3
  1.9 1.9 %collective-permute-start = (f32[32,128]{1,0:T(8,128)S(1)}, f32[32,128]{1,0:T(8,128)S(1)}, u32[]{:S(2)}, u32[]{:S(2)}) collective-permute-start(f32[32,128]{1,0:T(8,128)S(1)} %get-tuple-element.13), channel_id=1, source_target_pairs={{8,16},{24,32},{40,48},{56,64},{72,80},{88,96},{104,112},{120,128}... | collective-permute-start | bytes 49160 | tf_op jit(solution)/shard_map/ppermute | solution.py:370
  3.8 3.2 %collective-permute-start.1 = (f32[32,128]{1,0:T(8,128)S(1)}, f32[32,128]{1,0:T(8,128)S(1)}, u32[]{:S(2)}, u32[]{:S(2)}) collective-permute-start(f32[32,128]{1,0:T(8,128)S(1)} %get-tuple-element.14), channel_id=1, source_target_pairs={{0,8},{8,0},{16,24},{24,16},{32,40},{40,32},{48,56},{56,48},{64,72... | collective-permute-start | bytes 49160 | tf_op jit(solution)/shard_map/ppermute | solution.py:371
  7.0 0.0 copy-done.2
  7.0 0.0 copy-done.3
  7.0 0.0 copy-start
  7.1 0.5 %donor.1.donors = f32[8,256]{1,0:T(8,128)S(1)} custom-call(s32[8,256]{1,0:T(8,128)S(1)} %bitcast.23, f32[3,8,256]{2,1,0:T(8,128)S(1)} %bitcast.22, f32[64,128]{1,0:T(8,128)S(1)} %get-tuple-element.12.smoothed), custom_call_target="tpu_custom_call" | custom-call | flops 1000000 | bytes 200000 | tf_op jit(solution)/shard_map/donor/pallas_call | solution.py:328
  7.5 0.0 collective-permute-done.far
  7.5 0.3 collective-permute-done.1.near
  7.8 0.0 copy-done
  7.9 0.0 copy-start.1
  7.9 12.1 %all_to_all.10 = f32[208,1,128]{2,1,0:T(1,128)S(1)} all-to-all(f32[208,1,128]{2,1,0:T(1,128)S(1)} %bitcast.16), channel_id=1, replica_groups={{5,6,7,0,1,2,3,4},{13,14,15,8,9,10,11,12},{21,22,23,16,17,18,19,20},{29..., dimensions={0} | all-to-all | bytes 212992 | tf_op jit(solution)/shard_map/all_to_all | solution.py:377
  20.0 0.0 copy-done.1
  20.0 0.6 %residual.1 = (f32[64,128]{1,0:T(8,128)S(1)}, f32[64,2,128]{2,1,0:T(2,128)S(1)}) custom-call(s32[8,256]{1,0:T(8,128)S(1)} %get-tuple-element.11.cells, f32[208,128]{1,0:T(8,128)S(1)} %bitcast.15, f32[64,128]{1,0:T(8,128)S(1)} %get-tuple-element.12.smoothed, f32[64,128]{1,0:T(8,128)S(1)} %get-tuple-element.15.count, f32[64,128]{1,0:T(8,128)S(1)} %bitcast.21, ...), custom_call_target="tpu_custom_call" | custom-call | flops 1000000 | bytes 200000 | tf_op jit(solution)/shard_map/residual/pallas_call | solution.py:328
  20.6 16.0 %all_to_all.11 = f32[64,2,128]{2,1,0:T(2,128)S(1)} all-to-all(f32[64,2,128]{2,1,0:T(2,128)S(1)} %get-tuple-element.16), channel_id=1, replica_groups={{4,5,6,7,0,1,2,3,12,13,14,15,8,9,10,11,20,21,22,23,16,17,18,19,28,29,30..., dimensions={0} | all-to-all | bytes 131072 | tf_op jit(solution)/shard_map/all_to_all | solution.py:393
  36.6 1.9 %collective-permute-start.2 = (f32[64,128]{1,0:T(8,128)S(1)}, f32[64,128]{1,0:T(8,128)S(1)}, u32[]{:S(2)}, u32[]{:S(2)}) collective-permute-start(f32[64,128]{1,0:T(8,128)S(1)} %get-tuple-element.17), channel_id=1, source_target_pairs={{0,64},{8,72},{16,80},{24,88},{64,128},{72,136},{80,144},{88,152},... | collective-permute-start | bytes 98312 | tf_op jit(solution)/shard_map/ppermute | solution.py:400
  38.5 0.6 %store.1 = f32[64,128]{1,0:T(8,128)} custom-call(f32[8,128]{1,0:T(8,128)S(1)} %get-tuple-element.18.token, f32[64,128]{1,0:T(8,128)S(1)} %get-tuple-element.19.partial), custom_call_target="tpu_custom_call" | custom-call | flops 1000000 | bytes 200000 | tf_op jit(solution)/shard_map/store/pallas_call | solution.py:328
  39.2 4.5 %collective-permute-done.2.extra = f32[64,128]{1,0:T(8,128)S(1)} collective-permute-done((f32[64,128]{1,0:T(8,128)S(1)}, f32[64,128]{1,0:T(8,128)S(1)}, u32[]{:S(2)}, u32[]{:S(2)}) %collective-permute-start.2) | collective-permute-done | bytes 32800 | tf_op jit(solution)/shard_map/ppermute | solution.py:400
  43.6 1.3 %coarse.1 = f32[64,128]{1,0:T(8,128)} custom-call(f32[128,128]{1,0:T(8,128)S(1)} %bitcast.14, f32[64,128]{1,0:T(8,128)S(1)} %collective-permute-done.2.extra, f32[64,128]{1,0:T(8,128)S(1)} %get-tuple-element.12.smoothed), custom_call_target="tpu_custom_call" | custom-call | flops 1000000 | bytes 200000 | tf_op jit(solution)/shard_map/coarse/pallas_call | solution.py:328
  (2 shorter events, 0.0 us)
Async XLA Ops:
  0.6 6.4 %copy-start.2 = (f32[3,1,1,8,256]{4,3,2,1,0:T(8,128)S(1)}, f32[3,1,1,8,256]{4,3,2,1,0:T(8,128)}, u32[]{:S(2)}) copy-start(f32[3,1,1,8,256]{4,3,2,1,0:T(8,128)} %param.10) | copy-start | bytes 73732
  1.9 5.2 %copy-start.3 = (s32[1,1,8,256]{3,2,1,0:T(8,128)S(1)}, s32[1,1,8,256]{3,2,1,0:T(8,128)}, u32[]{:S(2)}) copy-start(s32[1,1,8,256]{3,2,1,0:T(8,128)} %param.9) | copy-start | bytes 24580
  1.9 5.7 %collective-permute-start = (f32[32,128]{1,0:T(8,128)S(1)}, f32[32,128]{1,0:T(8,128)S(1)}, u32[]{:S(2)}, u32[]{:S(2)}) collective-permute-start(f32[32,128]{1,0:T(8,128)S(1)} %get-tuple-element.13), channel_id=1, source_target_pairs={{8,16},{24,32},{40,48},{56,64},{72,80},{88,96},{104,112},{120,128}... | collective-permute-start | bytes 49160 | tf_op jit(solution)/shard_map/ppermute | solution.py:370
  3.8 4.0 %collective-permute-start.1 = (f32[32,128]{1,0:T(8,128)S(1)}, f32[32,128]{1,0:T(8,128)S(1)}, u32[]{:S(2)}, u32[]{:S(2)}) collective-permute-start(f32[32,128]{1,0:T(8,128)S(1)} %get-tuple-element.14), channel_id=1, source_target_pairs={{0,8},{8,0},{16,24},{24,16},{32,40},{40,32},{48,56},{56,48},{64,72... | collective-permute-start | bytes 49160 | tf_op jit(solution)/shard_map/ppermute | solution.py:371
  7.0 0.8 %copy-start = (f32[2,4,8,128]{3,2,1,0:T(8,128)S(1)}, f32[2,4,8,128]{3,2,1,0:T(8,128)}, u32[]{:S(2)}) copy-start(f32[2,4,8,128]{3,2,1,0:T(8,128)} %param.7) | copy-start | bytes 98308
  7.9 12.2 %copy-start.1 = (f32[2,4,8,128]{3,2,1,0:T(8,128)S(1)}, f32[2,4,8,128]{3,2,1,0:T(8,128)}, u32[]{:S(2)}) copy-start(f32[2,4,8,128]{3,2,1,0:T(8,128)} %param.6) | copy-start | bytes 98308
  36.6 7.0 %collective-permute-start.2 = (f32[64,128]{1,0:T(8,128)S(1)}, f32[64,128]{1,0:T(8,128)S(1)}, u32[]{:S(2)}, u32[]{:S(2)}) collective-permute-start(f32[64,128]{1,0:T(8,128)S(1)} %get-tuple-element.17), channel_id=1, source_target_pairs={{0,64},{8,72},{16,80},{24,88},{64,128},{72,136},{80,144},{88,152},... | collective-permute-start | bytes 98312 | tf_op jit(solution)/shard_map/ppermute | solution.py:400

commit v6 on v5

--- a/solution.py
+++ b/solution.py
@@ -154,17 +154,6 @@
             )
         sent[start + 24 : start + 25, :] = donors[d : d + 1, 0:128]
         sent[start + 25 : start + 26, :] = donors[d : d + 1, 128:256]
-
-
-def neighbour_sums(fields, shift_y, shift_z):
-    inner, outer = [], []
-    for field in fields:
-        beside_z = shift_z(field)
-        beside_y = shift_y(field)
-        both = shift_z(beside_y)
-        inner.append(0.5 * (beside_z + beside_y) + 0.25 * both)
-        outer.append(0.5 * field + 0.25 * (beside_z + beside_y) + (1.0 / 6.0) * both)
-    return [inner[i] + outer[i - 1] + outer[i + 1] for i in range(1, len(fields) - 1)]
 
 
 def residual_kernel(
@@ -253,8 +242,9 @@
 def pass_kernel(gathered, passed, token):
     along, _, _ = place()
     low_half = lax.rem(along, ROW) < ROW // 2
-    start = (jnp.where(low_half, ROW // 2, 0) - side_of(along)) & 7
-    passed[...] = gathered[pl.ds(pl.multiple_of(start * 16, 64), 64), :]
+    start = (jnp.where(low_half, ROW // 2, 0) ^ side_of(along)) & 4
+    start = start * 16 + jnp.where(low_half, 16, 0)
+    passed[...] = gathered[pl.ds(pl.multiple_of(start, 16), 48), :]
     token[...] = gathered[0:8, :]
 
 
@@ -265,6 +255,7 @@
 def coarse_kernel(gathered, extra, smoothed, pressure):
     along, own, _ = place()
     column, side = lax.rem(along, ROW), side_of(along)
+    skip = jnp.where(column < ROW // 2, 1, 0)
     lanes = iota((8, 128), 1)
     rows = (iota((8, 128), 0) + LATER) & 7
     low_z = lanes % 32 > 0
@@ -284,12 +275,21 @@
         from_above = jnp.where(rows < 7, pltpu.roll(behind, 7, 0), 0.0)
         return within + jnp.where(first_y, from_below, from_above)
 
+    def neighbour_sums(fields):
+        sums = []
+        for i in range(1, len(fields) - 1):
+            field, beside = fields[i], fields[i - 1] + fields[i + 1]
+            edge = 0.5 * field + 0.25 * beside
+            corner = 0.25 * field + (1.0 / 6.0) * beside
+            sums.append(0.5 * beside + shift_y(edge) + shift_z(edge + shift_y(corner)))
+        return sums
+
     rhs, cond = [], []
     for slot in range(7):
         at = column + slot - 3
         inside = jnp.logical_and(at >= 0, at < ROW)
-        here = pl.multiple_of(((jnp.clip(at, 0, ROW - 1) - side) & 7) * 16, 16)
-        there = pl.multiple_of((at & 3) * 16, 16)
+        here = pl.multiple_of((jnp.clip(at, 0, ROW - 1) ^ side) * 16, 16)
+        there = pl.multiple_of(jnp.clip((at & 3) - skip, 0, 2) * 16, 16)
         for f, out in ((0, rhs), (1, cond)):
             out.append(
                 jnp.where(inside, gathered[pl.ds(here + f, 8, stride=2), :],
@@ -301,13 +301,11 @@
     ]
     value = [r * s for r, s in zip(rhs, scale)]
     own_sum = [
-        half_weight_sum * c + s for c, s in zip(cond[1:-1], neighbour_sums(cond, shift_y, shift_z))
+        half_weight_sum * c + s for c, s in zip(cond[1:-1], neighbour_sums(cond))
     ]
     for sweep in range(3):
-        around = neighbour_sums(value, shift_y, shift_z)
-        around_both = neighbour_sums(
-            [v * c for v, c in zip(value, cond)], shift_y, shift_z
-        )
+        around = neighbour_sums(value)
+        around_both = neighbour_sums([v * c for v, c in zip(value, cond)])
         value, cond, rhs, scale = value[1:-1], cond[1:-1], rhs[1:-1], scale[1:-1]
         value = [
             v + s * (r - coarse_scale * (v * o - c * a - b))
@@ -384,7 +382,7 @@
     )
     groups = [
         [
-            (start + (i + int(side_of(start))) % ROW) * 8 + (j + LATER) % 8
+            (start + (i ^ int(side_of(start)))) * 8 + (j + LATER) % 8
             for i in range(ROW)
             for j in range(8)
         ]
@@ -394,7 +392,7 @@
         coarse, ("gx", "gy"), split_axis=0, concat_axis=0, tiled=True, axis_index_groups=groups
     ).reshape(128, 128)
     passed, token = call(
-        pass_kernel, "pass", [(64, 128), (8, 128)], (gathered,), [vector]
+        pass_kernel, "pass", [(48, 128), (8, 128)], (gathered,), [vector]
     )
     step = [(i, i + ROW) if i % ROW < ROW // 2 else (i, i - ROW) for i in range(size)]
     extra = lax.ppermute(passed, "gx", [(i, j) for i, j in step if 0 <= j < size])

time: 45.3 us -> 45.2 us (level)
  no operation moved by 1% of the time
where the time goes in v6:
time: 45.2 us; the launch traced here: 44.8 us
  blocking collectives  28.1 us (62%)
  starting transfers between devices  7.04 us (16%)
  waiting for transfers between devices  4.69 us (10%)
  Pallas kernels  4.21 us (9%)
  between operations  0.74 us (2%)
    all_to_all x1, blocking collectives, local(): lax.all_to_all(coarse, ('gx', 'gy'), split_axis=0, concat_axis=0, tiled=T...  16 us
    all_to_all x1, blocking collectives, local(): lax.all_to_all(sent.reshape(8 * CHUNK, 1, 128), 'gy', split_axis=0, conca...  12.1 us
    ppermute x1, waiting for transfers between devices, local(): lax.ppermute(passed, 'gx', [(i, j) for i, j in step if 0 <= j < size])  4.38 us
    pallas_call x7, Pallas kernels, call(): pl.pallas_call(kernel, out_shape=[jax.ShapeDtypeStruct(*(out if isinstanc...  4.21 us
    ppermute x1, starting transfers between devices, local(): near_in = lax.ppermute(near, 'gx', [(i, i ^ 1) for i in range(size)])  3.21 us
    ppermute x1, starting transfers between devices, local(): far_in = lax.ppermute(far, 'gx', beyond + [(j, i) for i, j in beyond])  1.92 us
    ppermute x1, starting transfers between devices, local(): lax.ppermute(passed, 'gx', [(i, j) for i, j in step if 0 <= j < size])  1.91 us
  transfers between devices with their start and end apart: 3, of which 2 were waited for; matrix products, arithmetic and copies ran while one was open for 0% of the time, Pallas kernels for 2%

profile of v6, /device:TPU:196, one launch (start us, length us, event | category | flops | bytes accessed | tf_op | source)
XLA Modules:
  0.0 44.8 jit_solution(3779887329682827529)
XLA Ops:
  0.6 0.0 copy-start.2
  0.6 1.2 %front.1 = (f32[64,128]{1,0:T(8,128)S(1)}, f32[64,128]{1,0:T(8,128)S(1)}, f32[32,128]{1,0:T(8,128)S(1)}, f32[32,128]{1,0:T(8,128)S(1)}, s32[8,256]{1,0:T(8,128)S(1)}) custom-call(s32[8,8]{1,0:T(8,128)} %bitcast.27, s32[8,256]{1,0:T(8,128)} %bitcast.26, f32[64,128]{1,0:T(8,128)} %bitcast.17, f32[64,128]{1,0:T(8,128)} %bitcast.20), custom_call_target="tpu_custom_call" | custom-call | flops 1000000 | bytes 200000 | tf_op jit(solution)/shard_map/front/pallas_call | solution.py:326
  1.9 0.0 copy-start.3
  1.9 1.9 %collective-permute-start = (f32[32,128]{1,0:T(8,128)S(1)}, f32[32,128]{1,0:T(8,128)S(1)}, u32[]{:S(2)}, u32[]{:S(2)}) collective-permute-start(f32[32,128]{1,0:T(8,128)S(1)} %get-tuple-element.13), channel_id=1, source_target_pairs={{8,16},{24,32},{40,48},{56,64},{72,80},{88,96},{104,112},{120,128}... | collective-permute-start | bytes 49160 | tf_op jit(solution)/shard_map/ppermute | solution.py:368
  3.8 3.2 %collective-permute-start.1 = (f32[32,128]{1,0:T(8,128)S(1)}, f32[32,128]{1,0:T(8,128)S(1)}, u32[]{:S(2)}, u32[]{:S(2)}) collective-permute-start(f32[32,128]{1,0:T(8,128)S(1)} %get-tuple-element.14), channel_id=1, source_target_pairs={{0,8},{8,0},{16,24},{24,16},{32,40},{40,32},{48,56},{56,48},{64,72... | collective-permute-start | bytes 49160 | tf_op jit(solution)/shard_map/ppermute | solution.py:369
  7.0 0.0 copy-done.2
  7.0 0.0 copy-done.3
  7.0 0.0 copy-start
  7.1 0.5 %donor.1.donors = f32[8,256]{1,0:T(8,128)S(1)} custom-call(s32[8,256]{1,0:T(8,128)S(1)} %bitcast.23, f32[3,8,256]{2,1,0:T(8,128)S(1)} %bitcast.22, f32[64,128]{1,0:T(8,128)S(1)} %get-tuple-element.12.smoothed), custom_call_target="tpu_custom_call" | custom-call | flops 1000000 | bytes 200000 | tf_op jit(solution)/shard_map/donor/pallas_call | solution.py:326
  7.5 0.0 collective-permute-done.far
  7.5 0.3 collective-permute-done.1.near
  7.8 0.0 copy-done
  7.9 0.0 copy-start.1
  7.9 12.1 %all_to_all.10 = f32[208,1,128]{2,1,0:T(1,128)S(1)} all-to-all(f32[208,1,128]{2,1,0:T(1,128)S(1)} %bitcast.16), channel_id=1, replica_groups={{5,6,7,0,1,2,3,4},{13,14,15,8,9,10,11,12},{21,22,23,16,17,18,19,20},{29..., dimensions={0} | all-to-all | bytes 212992 | tf_op jit(solution)/shard_map/all_to_all | solution.py:375
  20.0 0.0 copy-done.1
  20.0 0.6 %residual.1 = (f32[64,128]{1,0:T(8,128)S(1)}, f32[64,2,128]{2,1,0:T(2,128)S(1)}) custom-call(s32[8,256]{1,0:T(8,128)S(1)} %get-tuple-element.11.cells, f32[208,128]{1,0:T(8,128)S(1)} %bitcast.15, f32[64,128]{1,0:T(8,128)S(1)} %get-tuple-element.12.smoothed, f32[64,128]{1,0:T(8,128)S(1)} %get-tuple-element.15.count, f32[64,128]{1,0:T(8,128)S(1)} %bitcast.21, ...), custom_call_target="tpu_custom_call" | custom-call | flops 1000000 | bytes 200000 | tf_op jit(solution)/shard_map/residual/pallas_call | solution.py:326
  20.6 16.0 %all_to_all.11 = f32[64,2,128]{2,1,0:T(2,128)S(1)} all-to-all(f32[64,2,128]{2,1,0:T(2,128)S(1)} %get-tuple-element.16), channel_id=1, replica_groups={{4,5,6,7,0,1,2,3,12,13,14,15,8,9,10,11,20,21,22,23,16,17,18,19,28,29,30..., dimensions={0} | all-to-all | bytes 131072 | tf_op jit(solution)/shard_map/all_to_all | solution.py:391
  36.6 1.9 %collective-permute-start.2 = (f32[48,128]{1,0:T(8,128)S(1)}, f32[48,128]{1,0:T(8,128)S(1)}, u32[]{:S(2)}, u32[]{:S(2)}) collective-permute-start(f32[48,128]{1,0:T(8,128)S(1)} %get-tuple-element.17), channel_id=1, source_target_pairs={{0,64},{8,72},{16,80},{24,88},{64,128},{72,136},{80,144},{88,152},... | collective-permute-start | bytes 73736 | tf_op jit(solution)/shard_map/ppermute | solution.py:398
  38.5 0.6 %store.1 = f32[64,128]{1,0:T(8,128)} custom-call(f32[8,128]{1,0:T(8,128)S(1)} %get-tuple-element.18.token, f32[64,128]{1,0:T(8,128)S(1)} %get-tuple-element.19.partial), custom_call_target="tpu_custom_call" | custom-call | flops 1000000 | bytes 200000 | tf_op jit(solution)/shard_map/store/pallas_call | solution.py:326
  39.2 4.4 %collective-permute-done.2.extra = f32[48,128]{1,0:T(8,128)S(1)} collective-permute-done((f32[48,128]{1,0:T(8,128)S(1)}, f32[48,128]{1,0:T(8,128)S(1)}, u32[]{:S(2)}, u32[]{:S(2)}) %collective-permute-start.2) | collective-permute-done | bytes 24608 | tf_op jit(solution)/shard_map/ppermute | solution.py:398
  43.5 1.3 %coarse.1 = f32[64,128]{1,0:T(8,128)} custom-call(f32[128,128]{1,0:T(8,128)S(1)} %bitcast.14, f32[48,128]{1,0:T(8,128)S(1)} %collective-permute-done.2.extra, f32[64,128]{1,0:T(8,128)S(1)} %get-tuple-element.12.smoothed), custom_call_target="tpu_custom_call" | custom-call | flops 1000000 | bytes 200000 | tf_op jit(solution)/shard_map/coarse/pallas_call | solution.py:326
  (2 shorter events, 0.0 us)
Async XLA Ops:
  0.6 6.4 %copy-start.2 = (f32[3,1,1,8,256]{4,3,2,1,0:T(8,128)S(1)}, f32[3,1,1,8,256]{4,3,2,1,0:T(8,128)}, u32[]{:S(2)}) copy-start(f32[3,1,1,8,256]{4,3,2,1,0:T(8,128)} %param.10) | copy-start | bytes 73732
  1.9 5.2 %copy-start.3 = (s32[1,1,8,256]{3,2,1,0:T(8,128)S(1)}, s32[1,1,8,256]{3,2,1,0:T(8,128)}, u32[]{:S(2)}) copy-start(s32[1,1,8,256]{3,2,1,0:T(8,128)} %param.9) | copy-start | bytes 24580
  1.9 5.7 %collective-permute-start = (f32[32,128]{1,0:T(8,128)S(1)}, f32[32,128]{1,0:T(8,128)S(1)}, u32[]{:S(2)}, u32[]{:S(2)}) collective-permute-start(f32[32,128]{1,0:T(8,128)S(1)} %get-tuple-element.13), channel_id=1, source_target_pairs={{8,16},{24,32},{40,48},{56,64},{72,80},{88,96},{104,112},{120,128}... | collective-permute-start | bytes 49160 | tf_op jit(solution)/shard_map/ppermute | solution.py:368
  3.8 4.0 %collective-permute-start.1 = (f32[32,128]{1,0:T(8,128)S(1)}, f32[32,128]{1,0:T(8,128)S(1)}, u32[]{:S(2)}, u32[]{:S(2)}) collective-permute-start(f32[32,128]{1,0:T(8,128)S(1)} %get-tuple-element.14), channel_id=1, source_target_pairs={{0,8},{8,0},{16,24},{24,16},{32,40},{40,32},{48,56},{56,48},{64,72... | collective-permute-start | bytes 49160 | tf_op jit(solution)/shard_map/ppermute | solution.py:369
  7.0 0.8 %copy-start = (f32[2,4,8,128]{3,2,1,0:T(8,128)S(1)}, f32[2,4,8,128]{3,2,1,0:T(8,128)}, u32[]{:S(2)}) copy-start(f32[2,4,8,128]{3,2,1,0:T(8,128)} %param.7) | copy-start | bytes 98308
  7.9 12.2 %copy-start.1 = (f32[2,4,8,128]{3,2,1,0:T(8,128)S(1)}, f32[2,4,8,128]{3,2,1,0:T(8,128)}, u32[]{:S(2)}) copy-start(f32[2,4,8,128]{3,2,1,0:T(8,128)} %param.6) | copy-start | bytes 98308
  36.6 6.9 %collective-permute-start.2 = (f32[48,128]{1,0:T(8,128)S(1)}, f32[48,128]{1,0:T(8,128)S(1)}, u32[]{:S(2)}, u32[]{:S(2)}) collective-permute-start(f32[48,128]{1,0:T(8,128)S(1)} %get-tuple-element.17), channel_id=1, source_target_pairs={{0,64},{8,72},{16,80},{24,88},{64,128},{72,136},{80,144},{88,152},... | collective-permute-start | bytes 73736 | tf_op jit(solution)/shard_map/ppermute | solution.py:398

commit v7 on v6

--- a/solution.py
+++ b/solution.py
@@ -79,11 +79,13 @@
         copy.start()
     copies[0].wait()
     copies[1].wait()
-    lane = iota((1, 256), 1)
+    mine = jnp.where(iota((8, 8), 1) == own, counts[...], 0)
+    limit = jnp.sum(mine, axis=1, keepdims=True) * BLOCK
+    valid = jnp.where(iota((8, 256), 1) < limit, cells[...], -BLOCK)
+    marked[...] = valid
     total = jnp.zeros((64, 128), F32)
     for b in range(8):
-        row = jnp.where(lane < counts[b, own] * BLOCK, cells[b : b + 1, :], -BLOCK)
-        marked[b : b + 1, :] = row
+        row = valid[b : b + 1, :]
         high, low = one_hots(row)
         total = total + contract_rows(high.astype(F32).astype(BF16), low)
     count[...] = total
@@ -357,7 +359,7 @@
         ),
         [far_memory] * 4,
         [
-            pltpu.SMEM((8, 8), jnp.int32),
+            pltpu.VMEM((8, 8), jnp.int32),
             pltpu.VMEM((8, 256), jnp.int32),
             pltpu.VMEM(whole, F32),
             pltpu.VMEM(whole, F32),

time: 45.2 us -> 45.2 us (level)
  no operation moved by 1% of the time
where the time goes in v7:
time: 45.2 us; the launch traced here: 44.8 us
  blocking collectives  28.1 us (62%)
  starting transfers between devices  7.04 us (16%)
  waiting for transfers between devices  4.69 us (10%)
  Pallas kernels  4.16 us (9%)
  between operations  0.74 us (2%)
    all_to_all x1, blocking collectives, local(): lax.all_to_all(coarse, ('gx', 'gy'), split_axis=0, concat_axis=0, tiled=T...  16 us
    all_to_all x1, blocking collectives, local(): lax.all_to_all(sent.reshape(8 * CHUNK, 1, 128), 'gy', split_axis=0, conca...  12.1 us
    ppermute x1, waiting for transfers between devices, local(): lax.ppermute(passed, 'gx', [(i, j) for i, j in step if 0 <= j < size])  4.38 us
    pallas_call x7, Pallas kernels, call(): pl.pallas_call(kernel, out_shape=[jax.ShapeDtypeStruct(*(out if isinstanc...  4.16 us
    ppermute x1, starting transfers between devices, local(): near_in = lax.ppermute(near, 'gx', [(i, i ^ 1) for i in range(size)])  3.21 us
    ppermute x1, starting transfers between devices, local(): far_in = lax.ppermute(far, 'gx', beyond + [(j, i) for i, j in beyond])  1.92 us
    ppermute x1, starting transfers between devices, local(): lax.ppermute(passed, 'gx', [(i, j) for i, j in step if 0 <= j < size])  1.91 us
  transfers between devices with their start and end apart: 3, of which 2 were waited for; matrix products, arithmetic and copies ran while one was open for 0% of the time, Pallas kernels for 2%

profile of v7, /device:TPU:196, one launch (start us, length us, event | category | flops | bytes accessed | tf_op | source)
XLA Modules:
  0.0 44.8 jit_solution(3029396154391106821)
XLA Ops:
  0.6 0.0 copy-start.2
  0.6 1.2 %front.1 = (f32[64,128]{1,0:T(8,128)S(1)}, f32[64,128]{1,0:T(8,128)S(1)}, f32[32,128]{1,0:T(8,128)S(1)}, f32[32,128]{1,0:T(8,128)S(1)}, s32[8,256]{1,0:T(8,128)S(1)}) custom-call(s32[8,8]{1,0:T(8,128)} %bitcast.27, s32[8,256]{1,0:T(8,128)} %bitcast.26, f32[64,128]{1,0:T(8,128)} %bitcast.17, f32[64,128]{1,0:T(8,128)} %bitcast.20), custom_call_target="tpu_custom_call" | custom-call | flops 1000000 | bytes 200000 | tf_op jit(solution)/shard_map/front/pallas_call | solution.py:328
  1.8 0.0 copy-start.3
  1.8 1.9 %collective-permute-start = (f32[32,128]{1,0:T(8,128)S(1)}, f32[32,128]{1,0:T(8,128)S(1)}, u32[]{:S(2)}, u32[]{:S(2)}) collective-permute-start(f32[32,128]{1,0:T(8,128)S(1)} %get-tuple-element.13), channel_id=1, source_target_pairs={{8,16},{24,32},{40,48},{56,64},{72,80},{88,96},{104,112},{120,128}... | collective-permute-start | bytes 49160 | tf_op jit(solution)/shard_map/ppermute | solution.py:370
  3.8 3.2 %collective-permute-start.1 = (f32[32,128]{1,0:T(8,128)S(1)}, f32[32,128]{1,0:T(8,128)S(1)}, u32[]{:S(2)}, u32[]{:S(2)}) collective-permute-start(f32[32,128]{1,0:T(8,128)S(1)} %get-tuple-element.14), channel_id=1, source_target_pairs={{0,8},{8,0},{16,24},{24,16},{32,40},{40,32},{48,56},{56,48},{64,72... | collective-permute-start | bytes 49160 | tf_op jit(solution)/shard_map/ppermute | solution.py:371
  7.0 0.0 copy-done.2
  7.0 0.0 copy-done.3
  7.0 0.0 copy-start
  7.0 0.5 %donor.1.donors = f32[8,256]{1,0:T(8,128)S(1)} custom-call(s32[8,256]{1,0:T(8,128)S(1)} %bitcast.23, f32[3,8,256]{2,1,0:T(8,128)S(1)} %bitcast.22, f32[64,128]{1,0:T(8,128)S(1)} %get-tuple-element.12.smoothed), custom_call_target="tpu_custom_call" | custom-call | flops 1000000 | bytes 200000 | tf_op jit(solution)/shard_map/donor/pallas_call | solution.py:328
  7.5 0.0 collective-permute-done.far
  7.5 0.3 collective-permute-done.1.near
  7.8 0.0 copy-done
  7.8 0.0 copy-start.1
  7.8 12.1 %all_to_all.10 = f32[208,1,128]{2,1,0:T(1,128)S(1)} all-to-all(f32[208,1,128]{2,1,0:T(1,128)S(1)} %bitcast.16), channel_id=1, replica_groups={{5,6,7,0,1,2,3,4},{13,14,15,8,9,10,11,12},{21,22,23,16,17,18,19,20},{29..., dimensions={0} | all-to-all | bytes 212992 | tf_op jit(solution)/shard_map/all_to_all | solution.py:377
  20.0 0.0 copy-done.1
  20.0 0.6 %residual.1 = (f32[64,128]{1,0:T(8,128)S(1)}, f32[64,2,128]{2,1,0:T(2,128)S(1)}) custom-call(s32[8,256]{1,0:T(8,128)S(1)} %get-tuple-element.11.cells, f32[208,128]{1,0:T(8,128)S(1)} %bitcast.15, f32[64,128]{1,0:T(8,128)S(1)} %get-tuple-element.12.smoothed, f32[64,128]{1,0:T(8,128)S(1)} %get-tuple-element.15.count, f32[64,128]{1,0:T(8,128)S(1)} %bitcast.21, ...), custom_call_target="tpu_custom_call" | custom-call | flops 1000000 | bytes 200000 | tf_op jit(solution)/shard_map/residual/pallas_call | solution.py:328
  20.6 16.0 %all_to_all.11 = f32[64,2,128]{2,1,0:T(2,128)S(1)} all-to-all(f32[64,2,128]{2,1,0:T(2,128)S(1)} %get-tuple-element.16), channel_id=1, replica_groups={{4,5,6,7,0,1,2,3,12,13,14,15,8,9,10,11,20,21,22,23,16,17,18,19,28,29,30..., dimensions={0} | all-to-all | bytes 131072 | tf_op jit(solution)/shard_map/all_to_all | solution.py:393
  36.6 1.9 %collective-permute-start.2 = (f32[48,128]{1,0:T(8,128)S(1)}, f32[48,128]{1,0:T(8,128)S(1)}, u32[]{:S(2)}, u32[]{:S(2)}) collective-permute-start(f32[48,128]{1,0:T(8,128)S(1)} %get-tuple-element.17), channel_id=1, source_target_pairs={{0,64},{8,72},{16,80},{24,88},{64,128},{72,136},{80,144},{88,152},... | collective-permute-start | bytes 73736 | tf_op jit(solution)/shard_map/ppermute | solution.py:400
  38.5 0.6 %store.1 = f32[64,128]{1,0:T(8,128)} custom-call(f32[8,128]{1,0:T(8,128)S(1)} %get-tuple-element.18.token, f32[64,128]{1,0:T(8,128)S(1)} %get-tuple-element.19.partial), custom_call_target="tpu_custom_call" | custom-call | flops 1000000 | bytes 200000 | tf_op jit(solution)/shard_map/store/pallas_call | solution.py:328
  39.1 4.4 %collective-permute-done.2.extra = f32[48,128]{1,0:T(8,128)S(1)} collective-permute-done((f32[48,128]{1,0:T(8,128)S(1)}, f32[48,128]{1,0:T(8,128)S(1)}, u32[]{:S(2)}, u32[]{:S(2)}) %collective-permute-start.2) | collective-permute-done | bytes 24608 | tf_op jit(solution)/shard_map/ppermute | solution.py:400
  43.5 1.3 %coarse.1 = f32[64,128]{1,0:T(8,128)} custom-call(f32[128,128]{1,0:T(8,128)S(1)} %bitcast.14, f32[48,128]{1,0:T(8,128)S(1)} %collective-permute-done.2.extra, f32[64,128]{1,0:T(8,128)S(1)} %get-tuple-element.12.smoothed), custom_call_target="tpu_custom_call" | custom-call | flops 1000000 | bytes 200000 | tf_op jit(solution)/shard_map/coarse/pallas_call | solution.py:328
  (2 shorter events, 0.0 us)
Async XLA Ops:
  0.6 6.3 %copy-start.2 = (f32[3,1,1,8,256]{4,3,2,1,0:T(8,128)S(1)}, f32[3,1,1,8,256]{4,3,2,1,0:T(8,128)}, u32[]{:S(2)}) copy-start(f32[3,1,1,8,256]{4,3,2,1,0:T(8,128)} %param.10) | copy-start | bytes 73732
  1.8 5.2 %copy-start.3 = (s32[1,1,8,256]{3,2,1,0:T(8,128)S(1)}, s32[1,1,8,256]{3,2,1,0:T(8,128)}, u32[]{:S(2)}) copy-start(s32[1,1,8,256]{3,2,1,0:T(8,128)} %param.9) | copy-start | bytes 24580
  1.8 5.7 %collective-permute-start = (f32[32,128]{1,0:T(8,128)S(1)}, f32[32,128]{1,0:T(8,128)S(1)}, u32[]{:S(2)}, u32[]{:S(2)}) collective-permute-start(f32[32,128]{1,0:T(8,128)S(1)} %get-tuple-element.13), channel_id=1, source_target_pairs={{8,16},{24,32},{40,48},{56,64},{72,80},{88,96},{104,112},{120,128}... | collective-permute-start | bytes 49160 | tf_op jit(solution)/shard_map/ppermute | solution.py:370
  3.8 4.0 %collective-permute-start.1 = (f32[32,128]{1,0:T(8,128)S(1)}, f32[32,128]{1,0:T(8,128)S(1)}, u32[]{:S(2)}, u32[]{:S(2)}) collective-permute-start(f32[32,128]{1,0:T(8,128)S(1)} %get-tuple-element.14), channel_id=1, source_target_pairs={{0,8},{8,0},{16,24},{24,16},{32,40},{40,32},{48,56},{56,48},{64,72... | collective-permute-start | bytes 49160 | tf_op jit(solution)/shard_map/ppermute | solution.py:371
  7.0 0.8 %copy-start = (f32[2,4,8,128]{3,2,1,0:T(8,128)S(1)}, f32[2,4,8,128]{3,2,1,0:T(8,128)}, u32[]{:S(2)}) copy-start(f32[2,4,8,128]{3,2,1,0:T(8,128)} %param.7) | copy-start | bytes 98308
  7.8 12.2 %copy-start.1 = (f32[2,4,8,128]{3,2,1,0:T(8,128)S(1)}, f32[2,4,8,128]{3,2,1,0:T(8,128)}, u32[]{:S(2)}) copy-start(f32[2,4,8,128]{3,2,1,0:T(8,128)} %param.6) | copy-start | bytes 98308
  36.6 6.9 %collective-permute-start.2 = (f32[48,128]{1,0:T(8,128)S(1)}, f32[48,128]{1,0:T(8,128)S(1)}, u32[]{:S(2)}, u32[]{:S(2)}) collective-permute-start(f32[48,128]{1,0:T(8,128)S(1)} %get-tuple-element.17), channel_id=1, source_target_pairs={{0,64},{8,72},{16,80},{24,88},{64,128},{72,136},{80,144},{88,152},... | collective-permute-start | bytes 73736 | tf_op jit(solution)/shard_map/ppermute | solution.py:400

commit v8 on v7

--- a/solution.py
+++ b/solution.py
@@ -242,11 +242,12 @@
 
 
 def pass_kernel(gathered, passed, token):
-    along, _, _ = place()
+    along, own, _ = place()
     low_half = lax.rem(along, ROW) < ROW // 2
-    start = (jnp.where(low_half, ROW // 2, 0) ^ side_of(along)) & 4
-    start = start * 16 + jnp.where(low_half, 16, 0)
-    passed[...] = gathered[pl.ds(pl.multiple_of(start, 16), 48), :]
+    start = ((jnp.where(low_half, ROW // 2, 0) ^ side_of(along)) & 4) + jnp.where(low_half, 1, 0)
+    for r in range(5):
+        line = (own + r + 6 - LATER) & 7
+        passed[r * 6 : r * 6 + 6, :] = gathered[pl.ds(line * 16 + start * 2, 6), :]
     token[...] = gathered[0:8, :]
 
 
@@ -254,8 +255,11 @@
     residual[...] = partial[...]
 
 
-def coarse_kernel(gathered, extra, smoothed, pressure):
+def coarse_kernel(gathered, extra_in, smoothed, pressure, extra):
     along, own, _ = place()
+    extra[...] = jnp.zeros((48, 128), F32)
+    for r in range(5):
+        extra[pl.ds(((own + r + 6 - LATER) & 7) * 6, 6), :] = extra_in[r * 6 : r * 6 + 6, :]
     column, side = lax.rem(along, ROW), side_of(along)
     skip = jnp.where(column < ROW // 2, 1, 0)
     lanes = iota((8, 128), 1)
@@ -290,12 +294,12 @@
     for slot in range(7):
         at = column + slot - 3
         inside = jnp.logical_and(at >= 0, at < ROW)
-        here = pl.multiple_of((jnp.clip(at, 0, ROW - 1) ^ side) * 16, 16)
-        there = pl.multiple_of(jnp.clip((at & 3) - skip, 0, 2) * 16, 16)
+        here = (jnp.clip(at, 0, ROW - 1) ^ side) * 2
+        there = jnp.clip((at & 3) - skip, 0, 2) * 2
         for f, out in ((0, rhs), (1, cond)):
             out.append(
-                jnp.where(inside, gathered[pl.ds(here + f, 8, stride=2), :],
-                    extra[pl.ds(there + f, 8, stride=2), :],)
+                jnp.where(inside, gathered[pl.ds(here + f, 8, stride=16), :],
+                    extra[pl.ds(there + f, 8, stride=6), :],)
             )
     scale = [
         jnp.where(c > 0.0, damping / (stencil_weight_sum * coarse_scale * jnp.where(c > 0.0, c, 1.0)), 0.0)
@@ -385,8 +389,8 @@
     groups = [
         [
             (start + (i ^ int(side_of(start)))) * 8 + (j + LATER) % 8
+            for j in range(8)
             for i in range(ROW)
-            for j in range(8)
         ]
         for start in range(0, size, ROW)
     ]
@@ -394,14 +398,14 @@
         coarse, ("gx", "gy"), split_axis=0, concat_axis=0, tiled=True, axis_index_groups=groups
     ).reshape(128, 128)
     passed, token = call(
-        pass_kernel, "pass", [(48, 128), (8, 128)], (gathered,), [vector]
+        pass_kernel, "pass", [(30, 128), (8, 128)], (gathered,), [vector]
     )
     step = [(i, i + ROW) if i % ROW < ROW // 2 else (i, i - ROW) for i in range(size)]
     extra = lax.ppermute(passed, "gx", [(i, j) for i, j in step if 0 <= j < size])
     (residual,) = call(store_kernel, "store", [whole], (token, partial), [vector] * 2)
     (pressure,) = call(
         coarse_kernel, "coarse", [whole],
-        (gathered, extra, smoothed), [vector] * 3,
+        (gathered, extra, smoothed), [vector] * 3, [pltpu.VMEM((48, 128), F32)],
     )
     return pressure.reshape(shape), residual.reshape(shape)
 

time: 45.2 us -> 45 us (level)
  no operation moved by 1% of the time
where the time goes in v8:
time: 45 us; the launch traced here: 44.7 us
  blocking collectives  28.1 us (62%)
  starting transfers between devices  7.04 us (16%)
  waiting for transfers between devices  4.6 us (10%)
  Pallas kernels  4.17 us (9%)
  between operations  0.74 us (2%)
    all_to_all x1, blocking collectives, local(): lax.all_to_all(coarse, ('gx', 'gy'), split_axis=0, concat_axis=0, tiled=T...  15.9 us
    all_to_all x1, blocking collectives, local(): lax.all_to_all(sent.reshape(8 * CHUNK, 1, 128), 'gy', split_axis=0, conca...  12.1 us
    ppermute x1, waiting for transfers between devices, local(): lax.ppermute(passed, 'gx', [(i, j) for i, j in step if 0 <= j < size])  4.3 us
    pallas_call x7, Pallas kernels, call(): pl.pallas_call(kernel, out_shape=[jax.ShapeDtypeStruct(*(out if isinstanc...  4.17 us
    ppermute x1, starting transfers between devices, local(): near_in = lax.ppermute(near, 'gx', [(i, i ^ 1) for i in range(size)])  3.21 us
    ppermute x1, starting transfers between devices, local(): far_in = lax.ppermute(far, 'gx', beyond + [(j, i) for i, j in beyond])  1.92 us
    ppermute x1, starting transfers between devices, local(): lax.ppermute(passed, 'gx', [(i, j) for i, j in step if 0 <= j < size])  1.91 us
  transfers between devices with their start and end apart: 3, of which 2 were waited for; matrix products, arithmetic and copies ran while one was open for 0% of the time, Pallas kernels for 2%

profile of v8, /device:TPU:196, one launch (start us, length us, event | category | flops | bytes accessed | tf_op | source)
XLA Modules:
  0.0 44.7 jit_solution(177471840974433737)
XLA Ops:
  0.6 0.0 copy-start.2
  0.6 1.2 %front.1 = (f32[64,128]{1,0:T(8,128)S(1)}, f32[64,128]{1,0:T(8,128)S(1)}, f32[32,128]{1,0:T(8,128)S(1)}, f32[32,128]{1,0:T(8,128)S(1)}, s32[8,256]{1,0:T(8,128)S(1)}) custom-call(s32[8,8]{1,0:T(8,128)} %bitcast.27, s32[8,256]{1,0:T(8,128)} %bitcast.26, f32[64,128]{1,0:T(8,128)} %bitcast.17, f32[64,128]{1,0:T(8,128)} %bitcast.20), custom_call_target="tpu_custom_call" | custom-call | flops 1000000 | bytes 200000 | tf_op jit(solution)/shard_map/front/pallas_call | solution.py:332
  1.8 0.0 copy-start.3
  1.8 1.9 %collective-permute-start = (f32[32,128]{1,0:T(8,128)S(1)}, f32[32,128]{1,0:T(8,128)S(1)}, u32[]{:S(2)}, u32[]{:S(2)}) collective-permute-start(f32[32,128]{1,0:T(8,128)S(1)} %get-tuple-element.13), channel_id=1, source_target_pairs={{8,16},{24,32},{40,48},{56,64},{72,80},{88,96},{104,112},{120,128}... | collective-permute-start | bytes 49160 | tf_op jit(solution)/shard_map/ppermute | solution.py:374
  3.8 3.2 %collective-permute-start.1 = (f32[32,128]{1,0:T(8,128)S(1)}, f32[32,128]{1,0:T(8,128)S(1)}, u32[]{:S(2)}, u32[]{:S(2)}) collective-permute-start(f32[32,128]{1,0:T(8,128)S(1)} %get-tuple-element.14), channel_id=1, source_target_pairs={{0,8},{8,0},{16,24},{24,16},{32,40},{40,32},{48,56},{56,48},{64,72... | collective-permute-start | bytes 49160 | tf_op jit(solution)/shard_map/ppermute | solution.py:375
  7.0 0.0 copy-done.2
  7.0 0.0 copy-done.3
  7.0 0.0 copy-start
  7.0 0.5 %donor.1.donors = f32[8,256]{1,0:T(8,128)S(1)} custom-call(s32[8,256]{1,0:T(8,128)S(1)} %bitcast.23, f32[3,8,256]{2,1,0:T(8,128)S(1)} %bitcast.22, f32[64,128]{1,0:T(8,128)S(1)} %get-tuple-element.12.smoothed), custom_call_target="tpu_custom_call" | custom-call | flops 1000000 | bytes 200000 | tf_op jit(solution)/shard_map/donor/pallas_call | solution.py:332
  7.5 0.0 collective-permute-done.far
  7.5 0.3 collective-permute-done.1.near
  7.8 0.0 copy-done
  7.8 0.0 copy-start.1
  7.8 12.1 %all_to_all.10 = f32[208,1,128]{2,1,0:T(1,128)S(1)} all-to-all(f32[208,1,128]{2,1,0:T(1,128)S(1)} %bitcast.16), channel_id=1, replica_groups={{5,6,7,0,1,2,3,4},{13,14,15,8,9,10,11,12},{21,22,23,16,17,18,19,20},{29..., dimensions={0} | all-to-all | bytes 212992 | tf_op jit(solution)/shard_map/all_to_all | solution.py:381
  20.0 0.0 copy-done.1
  20.0 0.6 %residual.1 = (f32[64,128]{1,0:T(8,128)S(1)}, f32[64,2,128]{2,1,0:T(2,128)S(1)}) custom-call(s32[8,256]{1,0:T(8,128)S(1)} %get-tuple-element.11.cells, f32[208,128]{1,0:T(8,128)S(1)} %bitcast.15, f32[64,128]{1,0:T(8,128)S(1)} %get-tuple-element.12.smoothed, f32[64,128]{1,0:T(8,128)S(1)} %get-tuple-element.15.count, f32[64,128]{1,0:T(8,128)S(1)} %bitcast.21, ...), custom_call_target="tpu_custom_call" | custom-call | flops 1000000 | bytes 200000 | tf_op jit(solution)/shard_map/residual/pallas_call | solution.py:332
  20.6 15.9 %all_to_all.11 = f32[64,2,128]{2,1,0:T(2,128)S(1)} all-to-all(f32[64,2,128]{2,1,0:T(2,128)S(1)} %get-tuple-element.16), channel_id=1, replica_groups={{4,12,20,28,36,44,52,60,5,13,21,29,37,45,53,61,6,14,22,30,38,46,54,62,7..., dimensions={0} | all-to-all | bytes 131072 | tf_op jit(solution)/shard_map/all_to_all | solution.py:397
  36.5 1.9 %collective-permute-start.2 = (f32[30,128]{1,0:T(8,128)S(1)}, f32[30,128]{1,0:T(8,128)S(1)}, u32[]{:S(2)}, u32[]{:S(2)}) collective-permute-start(f32[30,128]{1,0:T(8,128)S(1)} %get-tuple-element.17), channel_id=1, source_target_pairs={{0,64},{8,72},{16,80},{24,88},{64,128},{72,136},{80,144},{88,152},... | collective-permute-start | bytes 46088 | tf_op jit(solution)/shard_map/ppermute | solution.py:404
  38.4 0.6 %store.1 = f32[64,128]{1,0:T(8,128)} custom-call(f32[8,128]{1,0:T(8,128)S(1)} %get-tuple-element.18.token, f32[64,128]{1,0:T(8,128)S(1)} %get-tuple-element.19.partial), custom_call_target="tpu_custom_call" | custom-call | flops 1000000 | bytes 200000 | tf_op jit(solution)/shard_map/store/pallas_call | solution.py:332
  39.1 4.3 %collective-permute-done.2.extra_in = f32[30,128]{1,0:T(8,128)S(1)} collective-permute-done((f32[30,128]{1,0:T(8,128)S(1)}, f32[30,128]{1,0:T(8,128)S(1)}, u32[]{:S(2)}, u32[]{:S(2)}) %collective-permute-start.2) | collective-permute-done | bytes 15392 | tf_op jit(solution)/shard_map/ppermute | solution.py:404
  43.4 1.3 %coarse.1 = f32[64,128]{1,0:T(8,128)} custom-call(f32[128,128]{1,0:T(8,128)S(1)} %bitcast.14, f32[30,128]{1,0:T(8,128)S(1)} %collective-permute-done.2.extra_in, f32[64,128]{1,0:T(8,128)S(1)} %get-tuple-element.12.smoothed), custom_call_target="tpu_custom_call" | custom-call | flops 1000000 | bytes 200000 | tf_op jit(solution)/shard_map/coarse/pallas_call | solution.py:332
  (2 shorter events, 0.0 us)
Async XLA Ops:
  0.6 6.3 %copy-start.2 = (f32[3,1,1,8,256]{4,3,2,1,0:T(8,128)S(1)}, f32[3,1,1,8,256]{4,3,2,1,0:T(8,128)}, u32[]{:S(2)}) copy-start(f32[3,1,1,8,256]{4,3,2,1,0:T(8,128)} %param.10) | copy-start | bytes 73732
  1.8 5.2 %copy-start.3 = (s32[1,1,8,256]{3,2,1,0:T(8,128)S(1)}, s32[1,1,8,256]{3,2,1,0:T(8,128)}, u32[]{:S(2)}) copy-start(s32[1,1,8,256]{3,2,1,0:T(8,128)} %param.9) | copy-start | bytes 24580
  1.8 5.7 %collective-permute-start = (f32[32,128]{1,0:T(8,128)S(1)}, f32[32,128]{1,0:T(8,128)S(1)}, u32[]{:S(2)}, u32[]{:S(2)}) collective-permute-start(f32[32,128]{1,0:T(8,128)S(1)} %get-tuple-element.13), channel_id=1, source_target_pairs={{8,16},{24,32},{40,48},{56,64},{72,80},{88,96},{104,112},{120,128}... | collective-permute-start | bytes 49160 | tf_op jit(solution)/shard_map/ppermute | solution.py:374
  3.8 4.0 %collective-permute-start.1 = (f32[32,128]{1,0:T(8,128)S(1)}, f32[32,128]{1,0:T(8,128)S(1)}, u32[]{:S(2)}, u32[]{:S(2)}) collective-permute-start(f32[32,128]{1,0:T(8,128)S(1)} %get-tuple-element.14), channel_id=1, source_target_pairs={{0,8},{8,0},{16,24},{24,16},{32,40},{40,32},{48,56},{56,48},{64,72... | collective-permute-start | bytes 49160 | tf_op jit(solution)/shard_map/ppermute | solution.py:375
  7.0 0.8 %copy-start = (f32[2,4,8,128]{3,2,1,0:T(8,128)S(1)}, f32[2,4,8,128]{3,2,1,0:T(8,128)}, u32[]{:S(2)}) copy-start(f32[2,4,8,128]{3,2,1,0:T(8,128)} %param.7) | copy-start | bytes 98308
  7.8 12.2 %copy-start.1 = (f32[2,4,8,128]{3,2,1,0:T(8,128)S(1)}, f32[2,4,8,128]{3,2,1,0:T(8,128)}, u32[]{:S(2)}) copy-start(f32[2,4,8,128]{3,2,1,0:T(8,128)} %param.6) | copy-start | bytes 98308
  36.5 6.8 %collective-permute-start.2 = (f32[30,128]{1,0:T(8,128)S(1)}, f32[30,128]{1,0:T(8,128)S(1)}, u32[]{:S(2)}, u32[]{:S(2)}) collective-permute-start(f32[30,128]{1,0:T(8,128)S(1)} %get-tuple-element.17), channel_id=1, source_target_pairs={{0,64},{8,72},{16,80},{24,88},{64,128},{72,136},{80,144},{88,152},... | collective-permute-start | bytes 46088 | tf_op jit(solution)/shard_map/ppermute | solution.py:404

commit v9 on v8

--- a/solution.py
+++ b/solution.py
@@ -83,11 +83,13 @@
     limit = jnp.sum(mine, axis=1, keepdims=True) * BLOCK
     valid = jnp.where(iota((8, 256), 1) < limit, cells[...], -BLOCK)
     marked[...] = valid
-    total = jnp.zeros((64, 128), F32)
+    lefts, lows = [], []
     for b in range(8):
         row = valid[b : b + 1, :]
         high, low = one_hots(row)
-        total = total + contract_rows(high.astype(F32).astype(BF16), low)
+        lefts.append(high.astype(F32).astype(BF16))
+        lows.append(low)
+    total = contract_rows(jnp.concatenate(lefts, axis=1), jnp.concatenate(lows, axis=1))
     count[...] = total
     copies[2].wait()
     copies[3].wait()
@@ -162,7 +164,7 @@
     cells, arrived, smoothed, count, rhs, cond, far, near, partial, coarse
 ):
     _, own, first = place()
-    total = jnp.zeros((128, 128), F32)
+    lefts, lows = [], []
     for b in range(8):
         high, low = one_hots(cells[b : b + 1, :])
         values = jnp.concatenate([
@@ -172,7 +174,9 @@
         left = jnp.concatenate(
             [jnp.where(high, cut.astype(F32), 0.0).astype(BF16) for cut in parts(values, 2)], axis=0
         )
-        total = total + contract_rows(left, low)
+        lefts.append(left)
+        lows.append(low)
+    total = contract_rows(jnp.concatenate(lefts, axis=1), jnp.concatenate(lows, axis=1))
     total = total[0:64] + total[64:128]
 
     below = jnp.where(own > 0, arrived[pl.ds(((own + 7 - TURN) & 7) * CHUNK, 24), :], 0.0)

time: 45 us -> 45 us (level)
  no operation moved by 1% of the time
where the time goes in v9:
time: 45 us; the launch traced here: 44.7 us
  blocking collectives  28.1 us (62%)
  starting transfers between devices  7.04 us (16%)
  waiting for transfers between devices  4.6 us (10%)
  Pallas kernels  4.16 us (9%)
  between operations  0.74 us (2%)
    all_to_all x1, blocking collectives, local(): lax.all_to_all(coarse, ('gx', 'gy'), split_axis=0, concat_axis=0, tiled=T...  15.9 us
    all_to_all x1, blocking collectives, local(): lax.all_to_all(sent.reshape(8 * CHUNK, 1, 128), 'gy', split_axis=0, conca...  12.1 us
    ppermute x1, waiting for transfers between devices, local(): lax.ppermute(passed, 'gx', [(i, j) for i, j in step if 0 <= j < size])  4.3 us
    pallas_call x7, Pallas kernels, call(): pl.pallas_call(kernel, out_shape=[jax.ShapeDtypeStruct(*(out if isinstanc...  4.16 us
    ppermute x1, starting transfers between devices, local(): near_in = lax.ppermute(near, 'gx', [(i, i ^ 1) for i in range(size)])  3.21 us
    ppermute x1, starting transfers between devices, local(): far_in = lax.ppermute(far, 'gx', beyond + [(j, i) for i, j in beyond])  1.92 us
    ppermute x1, starting transfers between devices, local(): lax.ppermute(passed, 'gx', [(i, j) for i, j in step if 0 <= j < size])  1.91 us
  transfers between devices with their start and end apart: 3, of which 2 were waited for; matrix products, arithmetic and copies ran while one was open for 0% of the time, Pallas kernels for 2%

profile of v9, /device:TPU:196, one launch (start us, length us, event | category | flops | bytes accessed | tf_op | source)
XLA Modules:
  0.0 44.7 jit_solution(13513312034840612756)
XLA Ops:
  0.6 0.0 copy-start.2
  0.6 1.2 %front.1 = (f32[64,128]{1,0:T(8,128)S(1)}, f32[64,128]{1,0:T(8,128)S(1)}, f32[32,128]{1,0:T(8,128)S(1)}, f32[32,128]{1,0:T(8,128)S(1)}, s32[8,256]{1,0:T(8,128)S(1)}) custom-call(s32[8,8]{1,0:T(8,128)} %bitcast.27, s32[8,256]{1,0:T(8,128)} %bitcast.26, f32[64,128]{1,0:T(8,128)} %bitcast.17, f32[64,128]{1,0:T(8,128)} %bitcast.20), custom_call_target="tpu_custom_call" | custom-call | flops 1000000 | bytes 200000 | tf_op jit(solution)/shard_map/front/pallas_call | solution.py:336
  1.8 0.0 copy-start.3
  1.8 1.9 %collective-permute-start = (f32[32,128]{1,0:T(8,128)S(1)}, f32[32,128]{1,0:T(8,128)S(1)}, u32[]{:S(2)}, u32[]{:S(2)}) collective-permute-start(f32[32,128]{1,0:T(8,128)S(1)} %get-tuple-element.13), channel_id=1, source_target_pairs={{8,16},{24,32},{40,48},{56,64},{72,80},{88,96},{104,112},{120,128}... | collective-permute-start | bytes 49160 | tf_op jit(solution)/shard_map/ppermute | solution.py:378
  3.7 3.2 %collective-permute-start.1 = (f32[32,128]{1,0:T(8,128)S(1)}, f32[32,128]{1,0:T(8,128)S(1)}, u32[]{:S(2)}, u32[]{:S(2)}) collective-permute-start(f32[32,128]{1,0:T(8,128)S(1)} %get-tuple-element.14), channel_id=1, source_target_pairs={{0,8},{8,0},{16,24},{24,16},{32,40},{40,32},{48,56},{56,48},{64,72... | collective-permute-start | bytes 49160 | tf_op jit(solution)/shard_map/ppermute | solution.py:379
  7.0 0.0 copy-done.2
  7.0 0.0 copy-done.3
  7.0 0.0 copy-start
  7.0 0.5 %donor.1.donors = f32[8,256]{1,0:T(8,128)S(1)} custom-call(s32[8,256]{1,0:T(8,128)S(1)} %bitcast.23, f32[3,8,256]{2,1,0:T(8,128)S(1)} %bitcast.22, f32[64,128]{1,0:T(8,128)S(1)} %get-tuple-element.12.smoothed), custom_call_target="tpu_custom_call" | custom-call | flops 1000000 | bytes 200000 | tf_op jit(solution)/shard_map/donor/pallas_call | solution.py:336
  7.5 0.0 collective-permute-done.far
  7.5 0.3 collective-permute-done.1.near
  7.8 0.0 copy-done
  7.8 0.0 copy-start.1
  7.8 12.1 %all_to_all.10 = f32[208,1,128]{2,1,0:T(1,128)S(1)} all-to-all(f32[208,1,128]{2,1,0:T(1,128)S(1)} %bitcast.16), channel_id=1, replica_groups={{5,6,7,0,1,2,3,4},{13,14,15,8,9,10,11,12},{21,22,23,16,17,18,19,20},{29..., dimensions={0} | all-to-all | bytes 212992 | tf_op jit(solution)/shard_map/all_to_all | solution.py:385
  20.0 0.0 copy-done.1
  20.0 0.6 %residual.1 = (f32[64,128]{1,0:T(8,128)S(1)}, f32[64,2,128]{2,1,0:T(2,128)S(1)}) custom-call(s32[8,256]{1,0:T(8,128)S(1)} %get-tuple-element.11.cells, f32[208,128]{1,0:T(8,128)S(1)} %bitcast.15, f32[64,128]{1,0:T(8,128)S(1)} %get-tuple-element.12.smoothed, f32[64,128]{1,0:T(8,128)S(1)} %get-tuple-element.15.count, f32[64,128]{1,0:T(8,128)S(1)} %bitcast.21, ...), custom_call_target="tpu_custom_call" | custom-call | flops 1000000 | bytes 200000 | tf_op jit(solution)/shard_map/residual/pallas_call | solution.py:336
  20.6 15.9 %all_to_all.11 = f32[64,2,128]{2,1,0:T(2,128)S(1)} all-to-all(f32[64,2,128]{2,1,0:T(2,128)S(1)} %get-tuple-element.16), channel_id=1, replica_groups={{4,12,20,28,36,44,52,60,5,13,21,29,37,45,53,61,6,14,22,30,38,46,54,62,7..., dimensions={0} | all-to-all | bytes 131072 | tf_op jit(solution)/shard_map/all_to_all | solution.py:401
  36.5 1.9 %collective-permute-start.2 = (f32[30,128]{1,0:T(8,128)S(1)}, f32[30,128]{1,0:T(8,128)S(1)}, u32[]{:S(2)}, u32[]{:S(2)}) collective-permute-start(f32[30,128]{1,0:T(8,128)S(1)} %get-tuple-element.17), channel_id=1, source_target_pairs={{0,64},{8,72},{16,80},{24,88},{64,128},{72,136},{80,144},{88,152},... | collective-permute-start | bytes 46088 | tf_op jit(solution)/shard_map/ppermute | solution.py:408
  38.4 0.6 %store.1 = f32[64,128]{1,0:T(8,128)} custom-call(f32[8,128]{1,0:T(8,128)S(1)} %get-tuple-element.18.token, f32[64,128]{1,0:T(8,128)S(1)} %get-tuple-element.19.partial), custom_call_target="tpu_custom_call" | custom-call | flops 1000000 | bytes 200000 | tf_op jit(solution)/shard_map/store/pallas_call | solution.py:336
  39.1 4.3 %collective-permute-done.2.extra_in = f32[30,128]{1,0:T(8,128)S(1)} collective-permute-done((f32[30,128]{1,0:T(8,128)S(1)}, f32[30,128]{1,0:T(8,128)S(1)}, u32[]{:S(2)}, u32[]{:S(2)}) %collective-permute-start.2) | collective-permute-done | bytes 15392 | tf_op jit(solution)/shard_map/ppermute | solution.py:408
  43.4 1.3 %coarse.1 = f32[64,128]{1,0:T(8,128)} custom-call(f32[128,128]{1,0:T(8,128)S(1)} %bitcast.14, f32[30,128]{1,0:T(8,128)S(1)} %collective-permute-done.2.extra_in, f32[64,128]{1,0:T(8,128)S(1)} %get-tuple-element.12.smoothed), custom_call_target="tpu_custom_call" | custom-call | flops 1000000 | bytes 200000 | tf_op jit(solution)/shard_map/coarse/pallas_call | solution.py:336
  (2 shorter events, 0.0 us)
Async XLA Ops:
  0.6 6.3 %copy-start.2 = (f32[3,1,1,8,256]{4,3,2,1,0:T(8,128)S(1)}, f32[3,1,1,8,256]{4,3,2,1,0:T(8,128)}, u32[]{:S(2)}) copy-start(f32[3,1,1,8,256]{4,3,2,1,0:T(8,128)} %param.10) | copy-start | bytes 73732
  1.8 5.2 %copy-start.3 = (s32[1,1,8,256]{3,2,1,0:T(8,128)S(1)}, s32[1,1,8,256]{3,2,1,0:T(8,128)}, u32[]{:S(2)}) copy-start(s32[1,1,8,256]{3,2,1,0:T(8,128)} %param.9) | copy-start | bytes 24580
  1.8 5.7 %collective-permute-start = (f32[32,128]{1,0:T(8,128)S(1)}, f32[32,128]{1,0:T(8,128)S(1)}, u32[]{:S(2)}, u32[]{:S(2)}) collective-permute-start(f32[32,128]{1,0:T(8,128)S(1)} %get-tuple-element.13), channel_id=1, source_target_pairs={{8,16},{24,32},{40,48},{56,64},{72,80},{88,96},{104,112},{120,128}... | collective-permute-start | bytes 49160 | tf_op jit(solution)/shard_map/ppermute | solution.py:378
  3.7 4.0 %collective-permute-start.1 = (f32[32,128]{1,0:T(8,128)S(1)}, f32[32,128]{1,0:T(8,128)S(1)}, u32[]{:S(2)}, u32[]{:S(2)}) collective-permute-start(f32[32,128]{1,0:T(8,128)S(1)} %get-tuple-element.14), channel_id=1, source_target_pairs={{0,8},{8,0},{16,24},{24,16},{32,40},{40,32},{48,56},{56,48},{64,72... | collective-permute-start | bytes 49160 | tf_op jit(solution)/shard_map/ppermute | solution.py:379
  7.0 0.8 %copy-start = (f32[2,4,8,128]{3,2,1,0:T(8,128)S(1)}, f32[2,4,8,128]{3,2,1,0:T(8,128)}, u32[]{:S(2)}) copy-start(f32[2,4,8,128]{3,2,1,0:T(8,128)} %param.7) | copy-start | bytes 98308
  7.8 12.2 %copy-start.1 = (f32[2,4,8,128]{3,2,1,0:T(8,128)S(1)}, f32[2,4,8,128]{3,2,1,0:T(8,128)}, u32[]{:S(2)}) copy-start(f32[2,4,8,128]{3,2,1,0:T(8,128)} %param.6) | copy-start | bytes 98308
  36.5 6.8 %collective-permute-start.2 = (f32[30,128]{1,0:T(8,128)S(1)}, f32[30,128]{1,0:T(8,128)S(1)}, u32[]{:S(2)}, u32[]{:S(2)}) collective-permute-start(f32[30,128]{1,0:T(8,128)S(1)} %get-tuple-element.17), channel_id=1, source_target_pairs={{0,64},{8,72},{16,80},{24,88},{64,128},{72,136},{80,144},{88,152},... | collective-permute-start | bytes 46088 | tf_op jit(solution)/shard_map/ppermute | solution.py:408
